TPU v7x, 32 devices: a whole 2x2x4 slice. The times are simulated.
32 devices in a mesh: grp: 2 (over y), own: 8 (over z, x), tile: 2 (over core).
Axes of the slice: x: 2, y: 2, z: 4, core: 2. Of those that a mesh axis runs over, the one named last changes fastest.
Arguments:
- known: bfloat16 [32, 512, 1536], P(('grp', 'own'), None, 'tile'), parts along dimension 0, may hold values from -6 to 6
- outer_blocks: bfloat16 [256, 512, 512], P(('grp', 'own')), parts along dimension 0, may hold values from -0.0625 to 0.0625
- outer_row: int32 [256], P(('grp', 'own')), parts along dimension 0, may hold values from 0 to 15, as said below
- outer_col: int32 [256], P(('grp', 'own')), parts along dimension 0, may hold values from 0 to 7, as said below
- right_side: bfloat16 [16, 512, 1536], P('grp', 'own', 'tile'), parts along dimension 0, may hold values from -6 to 6
- window_blocks: bfloat16 [16, 8, 512, 512], P('grp', None, 'own'), parts along dimension 0, may hold values from -0.125 to 0.125
- window_pattern: int32 [16, 8], P('grp'), parts along dimension 0, may hold values from 0 to 1, as said below
- diag_inverse: bfloat16 [16, 512, 512], P('grp', None, 'own'), parts along dimension 0, may hold values from -1 to 2, as said below
Outputs:
- solution: bfloat16 [16, 512, 1536], P('grp', 'own', 'tile'), parts along dimension 0
There are 2 independent parts, one for each index of `grp`. A program takes and returns all parts, laid end to end along the dimension named above; each array names one. Nothing has to cross between parts.
Inputs may be any that keep to these rules, and one draw needn't show every extreme that they name: `outer_row`: block b lies in one of the rows 2 * (b // 16) to 2 * (b // 16) + 1, and each of these rows holds some such block. `outer_col`: each window column is named by some block among b // 16 = o, for every o. `window_pattern`: entry [j, k] is 0 unless j > k, and 1 where j = k + 1. `diag_inverse`: each block is lower triangular, with diagonal entries between 0.5 and 2.
All inputs are finite; a program needn't handle non-finite values.
Results may differ from a plain program's by a relative error of at most 0.0068.
Values may be sent and summed in bfloat16 or wider, within the bound.
No kernel may reach another device: no remote copies, remote signals or barrier semaphores. Data moves between devices by JAX's collectives and lax.ppermute only.
A program may use at most 128 MiB of HBM per device.

v0:
```python
import jax
import jax.numpy as jnp
from jax import lax
from jax.sharding import PartitionSpec as P


def body(
    known,
    outer_blocks,
    outer_row,
    outer_col,
    right_side,
    window_blocks,
    window_pattern,
    diag_inverse,
):
    owner_index = lax.axis_index("own")
    columns = right_side.shape[0]
    rows_dev = right_side.shape[1]
    super_size = window_blocks.shape[3]
    sample_count = known.shape[2]
    local_row = outer_row - owner_index * known.shape[0]

    def add_block(block_index, totals):
        factor_block = lax.dynamic_index_in_dim(outer_blocks, block_index, 0, keepdims=False)
        source_row = lax.dynamic_index_in_dim(local_row, block_index, 0, keepdims=False)
        target_col = lax.dynamic_index_in_dim(outer_col, block_index, 0, keepdims=False)
        source = lax.dynamic_index_in_dim(known, source_row, 0, keepdims=False)
        product = lax.dot_general(
            factor_block, source, (((0,), (0,)), ((), ())), preferred_element_type=jnp.float32
        )
        current = lax.dynamic_index_in_dim(totals, target_col, 0, keepdims=False)
        return lax.dynamic_update_index_in_dim(totals, current + product, target_col, 0)

    outer_sum = lax.fori_loop(
        0,
        outer_blocks.shape[0],
        add_block,
        jnp.zeros((columns, super_size, sample_count), jnp.float32),
    )
    solved = jnp.zeros((columns, rows_dev, sample_count), jnp.bfloat16)
    for column in reversed(range(columns)):
        draw_rows = right_side[column, :, 0 : 0 + sample_count].astype(jnp.float32)
        local_term = lax.dynamic_update_slice(
            jnp.zeros((super_size, sample_count), jnp.float32),
            draw_rows,
            (owner_index * rows_dev, jnp.zeros((), jnp.int32)),
        )
        pattern_mask = window_pattern[:, column].astype(jnp.bfloat16)
        weighted = solved * pattern_mask[:, None, None]
        window_term = jnp.einsum(
            "jrc,jrs->cs", window_blocks[:, column], weighted, preferred_element_type=jnp.float32
        )
        local_term = local_term - outer_sum[column, :, 0 : 0 + sample_count] - window_term
        residual = lax.psum(local_term, "own")
        rounded = residual.astype(jnp.bfloat16)
        values = lax.dot_general(
            diag_inverse[column],
            rounded,
            (((0,), (0,)), ((), ())),
            preferred_element_type=jnp.float32,
        )
        solved_rows = values.astype(jnp.bfloat16)
        solved = solved.at[column].set(solved_rows)
    return solved


def solution(mesh):
    return jax.shard_map(
        body,
        mesh=mesh,
        in_specs=(
            P(("grp", "own"), None, "tile"),
            P(("grp", "own"), None, None),
            P(("grp", "own")),
            P(("grp", "own")),
            P("grp", "own", "tile"),
            P("grp", None, "own", None),
            P("grp", None),
            P("grp", None, "own"),
        ),
        out_specs=P("grp", "own", "tile"),
        check_vma=False,
    )
```

profile of v0, /device:TPU:0, one launch (start us, length us, event | category | flops | bytes accessed | tf_op | source)
XLA Modules:
  0.0 836.2 jit_solution(13410035316192254381)
XLA Ops:
  2.9 5.6 broadcast_in_dim.22
  8.6 149.9 %while.21 = (s32[]{:T(128)}, f32[8,512,768]{2,1,0:T(8,128)}, s32[16]{0:T(128)S(1)}, bf16[16,512,512]{2,1,0:T(8,128)(2,1)}, s32[16]{0:T(128)S(1)}, /*index=5*/bf1...) while((s32[]{:T(128)}, f32[8,512,768]{2,1,0:T(8,128)}, s32[16]{0:T(128)S(1)}, ...), condition=%wide.region_1.2_spmd, body=%wide.region_0.1_spmd.sunk | while | flops 403046400 | bytes 7602893 | solution.py:35
  15.1 2.8 bitcast_dynamic-update-slice_fusion.2
  24.5 2.8 bitcast_dynamic-update-slice_fusion.2
  33.8 2.8 bitcast_dynamic-update-slice_fusion.2
  43.2 2.8 bitcast_dynamic-update-slice_fusion.2
  52.6 2.8 bitcast_dynamic-update-slice_fusion.2
  61.9 2.8 bitcast_dynamic-update-slice_fusion.2
  71.3 2.8 bitcast_dynamic-update-slice_fusion.2
  80.6 2.8 bitcast_dynamic-update-slice_fusion.2
  90.0 2.8 bitcast_dynamic-update-slice_fusion.2
  99.3 2.8 bitcast_dynamic-update-slice_fusion.2
  108.7 2.8 bitcast_dynamic-update-slice_fusion.2
  118.0 2.8 bitcast_dynamic-update-slice_fusion.2
  127.4 2.8 bitcast_dynamic-update-slice_fusion.2
  136.7 2.9 bitcast_dynamic-update-slice_fusion.2
  146.2 2.8 bitcast_dynamic-update-slice_fusion.2
  155.5 2.9 bitcast_dynamic-update-slice_fusion.2
  158.7 2.7 bitcast_subtract_fusion.7
  161.4 82.4 %all-reduce.9 = bf16[512,768]{1,0:T(8,128)(2,1)S(1)} all-reduce(f32[512,768]{1,0:T(8,128)S(1)} %bitcast_subtract_fusion.7), channel_id=1, replica_groups=mesh['grp'=2,'own'=8,'tile'=2] {'own'}, use_global_device_ids=true, to_apply=%region_2.3 | all-reduce | flops 393216 | bytes 2359296 | tf_op jit(solution)/shard_map/psum | solution.py:55
  248.2 80.0 %all-reduce.10 = bf16[512,768]{1,0:T(8,128)(2,1)S(1)} all-reduce(f32[512,768]{1,0:T(8,128)S(1)} %bitcast_subtract_fusion.6), channel_id=1, replica_groups=mesh['grp'=2,'own'=8,'tile'=2] {'own'}, use_global_device_ids=true, to_apply=%region_3.4 | all-reduce | flops 393216 | bytes 2359296 | tf_op jit(solution)/shard_map/psum | solution.py:55
  332.3 2.7 bitcast_subtract_fusion.5
  335.0 80.1 %all-reduce.11 = bf16[512,768]{1,0:T(8,128)(2,1)S(1)} all-reduce(f32[512,768]{1,0:T(8,128)S(1)} %bitcast_subtract_fusion.5), channel_id=1, replica_groups=mesh['grp'=2,'own'=8,'tile'=2] {'own'}, use_global_device_ids=true, to_apply=%region_4.5 | all-reduce | flops 393216 | bytes 2359296 | tf_op jit(solution)/shard_map/psum | solution.py:55
  421.8 79.1 %all-reduce.12 = bf16[512,768]{1,0:T(8,128)(2,1)S(1)} all-reduce(f32[512,768]{1,0:T(8,128)S(1)} %bitcast_subtract_fusion.4), channel_id=1, replica_groups=mesh['grp'=2,'own'=8,'tile'=2] {'own'}, use_global_device_ids=true, to_apply=%region_5.6 | all-reduce | flops 393216 | bytes 2359296 | tf_op jit(solution)/shard_map/psum | solution.py:55
  504.9 2.7 bitcast_subtract_fusion.3
  507.7 77.5 %all-reduce.13 = bf16[512,768]{1,0:T(8,128)(2,1)S(1)} all-reduce(f32[512,768]{1,0:T(8,128)S(1)} %bitcast_subtract_fusion.3), channel_id=1, replica_groups=mesh['grp'=2,'own'=8,'tile'=2] {'own'}, use_global_device_ids=true, to_apply=%region_6.7 | all-reduce | flops 393216 | bytes 2359296 | tf_op jit(solution)/shard_map/psum | solution.py:55
  589.1 2.7 bitcast_subtract_fusion.2
  591.8 79.9 %all-reduce.14 = bf16[512,768]{1,0:T(8,128)(2,1)S(1)} all-reduce(f32[512,768]{1,0:T(8,128)S(1)} %bitcast_subtract_fusion.2), channel_id=1, replica_groups=mesh['grp'=2,'own'=8,'tile'=2] {'own'}, use_global_device_ids=true, to_apply=%region_7.8 | all-reduce | flops 393216 | bytes 2359296 | tf_op jit(solution)/shard_map/psum | solution.py:55
  675.8 2.7 bitcast_subtract_fusion.1
  678.5 80.9 %all-reduce.15 = bf16[512,768]{1,0:T(8,128)(2,1)S(1)} all-reduce(f32[512,768]{1,0:T(8,128)S(1)} %bitcast_subtract_fusion.1), channel_id=1, replica_groups=mesh['grp'=2,'own'=8,'tile'=2] {'own'}, use_global_device_ids=true, to_apply=%region_8.9 | all-reduce | flops 393216 | bytes 2359296 | tf_op jit(solution)/shard_map/psum | solution.py:55
  763.5 2.7 bitcast_subtract_fusion
  766.2 68.3 %all-reduce.16 = bf16[512,768]{1,0:T(8,128)(2,1)S(1)} all-reduce(f32[512,768]{1,0:T(8,128)S(1)} %bitcast_subtract_fusion), channel_id=1, replica_groups=mesh['grp'=2,'own'=8,'tile'=2] {'own'}, use_global_device_ids=true, to_apply=%region_9.10 | all-reduce | flops 393216 | bytes 2359296 | tf_op jit(solution)/shard_map/psum | solution.py:55
  (88 shorter events, 80.0 us)
Async XLA Ops:
  0.0 2.9 copy-start.3
  2.9 5.7 copy-start.1
  2.9 5.7 copy-start.4
  8.6 149.9 %copy-start.2 = (s32[8,8]{1,0:T(8,128)S(1)}, s32[8,8]{1,0:T(8,128)}, u32[]{:S(2)}) copy-start(s32[8,8]{1,0:T(8,128)} %param.32) | copy-start | bytes 772
  760.5 5.7 copy-start
where the time goes:
time: 841 us; the launch traced here: 836 us
  blocking collectives  628 us (75%)
  matrix products  75.7 us (9%)
  loops' own time  61.1 us (7%)
  local copies, waits for them, and re-layouts  58.9 us (7%)
  other arithmetic  12.3 us (1%)
    psum x8, blocking collectives, body(): residual = lax.psum(local_term, 'own')  628 us
    another operation x1, loops' own time, body(): lax.fori_loop(0, outer_blocks.shape[0], add_block, jnp.zeros((columns, su...  61.1 us
    dot_general x16, matrix products, add_block(): lax.dot_general(factor_block, source, (((0,), (0,)), ((), ())), preferred...  45 us
    dynamic_slice x16, local copies, waits for them, and re-layouts, add_block(): current = lax.dynamic_index_in_dim(totals, target_col, 0, keepdims=False)  24.2 us
    dot_general x8, matrix products, body(): jnp.einsum('jrc,jrs->cs', window_blocks[:, column], weighted, preferred_e...  21.2 us

commit v1 on v0

v1 whole, which is shorter than its diff:
```python
import functools

import jax
import jax.numpy as jnp
from jax import lax
from jax.experimental import pallas as pl
from jax.experimental.pallas import tpu as pltpu
from jax.sharding import PartitionSpec as P

F32, BF16 = jnp.float32, jnp.bfloat16
VMEM_LIMIT = 50 * 1024 * 1024
STAGES = ((7, 6, 5, 4), (3, 2, 1, 0))
CHUNK = 2

SMEM_SPEC = pl.BlockSpec(memory_space=pltpu.SMEM)
VMEM_SPEC = pl.BlockSpec(memory_space=pltpu.VMEM)
ANY_SPEC = pl.BlockSpec(memory_space=pl.ANY)


def params(**extra):
    return pltpu.CompilerParams(vmem_limit_bytes=VMEM_LIMIT, **extra)


def stage_blocks(columns):
    blocks = []
    for place, k in enumerate(columns):
        blocks += [(j, k) for j in columns[:place]] + [(k, k)]
    return blocks


def weights_kernel(stages, meta, window_ref, diag_ref, *refs):
    outs, (turned, sems) = refs[: len(stages)], refs[len(stages) :]
    half = outs[0].shape[1]
    start = pl.multiple_of(meta[2] * half, half)
    copies = []
    for out, columns in zip(outs, stages):
        for place, (j, k) in enumerate(stage_blocks(columns)):
            if j != k:
                copy = pltpu.make_async_copy(
                    window_ref.at[j, k, pl.ds(start, half)], out.at[place], sems.at[len(copies)]
                )
                copy.start()
                copies.append(copy)
    for out, columns in zip(outs, stages):
        for place, (j, k) in enumerate(stage_blocks(columns)):
            if j == k:
                turned[k] = diag_ref[k].T
                copy = pltpu.make_async_copy(
                    turned.at[k, pl.ds(start, half)], out.at[place], sems.at[len(copies)]
                )
                copy.start()
                copies.append(copy)
    for copy in copies:
        copy.wait()


def gather_weights(meta, window_blocks, diag_inverse, stages):
    columns, super_size, rows = diag_inverse.shape
    shapes = [
        jax.ShapeDtypeStruct((len(stage_blocks(c)), rows // 2, super_size), BF16) for c in stages
    ]
    total = sum(s.shape[0] for s in shapes)
    parts = pl.pallas_call(
        functools.partial(weights_kernel, stages),
        out_shape=shapes,
        in_specs=[SMEM_SPEC, ANY_SPEC, VMEM_SPEC],
        out_specs=[ANY_SPEC] * len(shapes),
        scratch_shapes=[
            pltpu.VMEM((columns, rows, super_size), BF16),
            pltpu.SemaphoreType.DMA((total,)),
        ],
        compiler_params=params(),
        name="own_weights",
    )(meta, window_blocks, diag_inverse)
    return [lax.all_gather(p, ("own", "tile"), axis=0, tiled=False) for p in parts]


def store_split(total, kk, side, send, keep):
    rows = send.shape[1]
    send[kk] = total[pl.ds(pl.multiple_of((1 - side) * rows, rows), rows)].astype(BF16)
    keep[kk] = total[pl.ds(pl.multiple_of(side * rows, rows), rows)]


def outer_kernel(columns, split, meta, row_ref, col_ref, known, draws, blocks, *refs):
    outs, (turned, slab, total, sems) = refs[:-4], refs[-4:]
    high, low = columns[0], columns[-1]
    count, rows_dev = blocks.shape[0], known.shape[0]

    def block_copy(b):
        return pltpu.make_async_copy(blocks.at[b], slab.at[b], sems.at[b])

    def start(b, _):
        @pl.when((col_ref[b] >= low) & (col_ref[b] <= high))
        def _():
            block_copy(b).start()

        return 0

    lax.fori_loop(0, count, start, 0)
    for r in range(rows_dev):
        turned[r] = known[r].T
    rows = draws.shape[1]
    place = lax.broadcasted_iota(jnp.int32, (rows, total.shape[1]), 0) + meta[0] * rows
    lane = lax.broadcasted_iota(jnp.int32, (rows, total.shape[1]), 1)
    spread = jnp.where(place == lane, 1.0, 0.0).astype(BF16)

    def column(kk, _):
        k = high - kk
        total[...] = jnp.dot(draws[k].T, spread, preferred_element_type=F32)

        def block(b, _):
            @pl.when(col_ref[b] == k)
            def _():
                block_copy(b).wait()
                source = row_ref[b] - meta[0] * rows_dev
                total[...] -= jnp.dot(turned[source], slab[b], preferred_element_type=F32)

            return 0

        lax.fori_loop(0, count, block, 0)
        if split:
            store_split(total, kk, meta[1], *outs)
        else:
            outs[0][kk] = total[...]
        return 0

    lax.fori_loop(0, len(columns), column, 0)


def outer_terms(meta, outer_row, outer_col, known, right_side, outer_blocks, columns, split):
    rows_dev, super_size, samples = known.shape
    count, n = outer_blocks.shape[0], len(columns)
    if split:
        shapes = [
            jax.ShapeDtypeStruct((n, samples // 2, super_size), BF16),
            jax.ShapeDtypeStruct((n, samples // 2, super_size), F32),
        ]
    else:
        shapes = [jax.ShapeDtypeStruct((n, samples, super_size), F32)]
    return pl.pallas_call(
        functools.partial(outer_kernel, columns, split),
        out_shape=shapes,
        in_specs=[SMEM_SPEC] * 3 + [VMEM_SPEC, VMEM_SPEC, ANY_SPEC],
        out_specs=[VMEM_SPEC] * len(shapes),
        scratch_shapes=[
            pltpu.VMEM((rows_dev, samples, super_size), BF16),
            pltpu.VMEM((count, super_size, super_size), BF16),
            pltpu.VMEM((samples, super_size), F32),
            pltpu.SemaphoreType.DMA((count,)),
        ],
        compiler_params=params(),
        cost_estimate=pl.CostEstimate(
            flops=4 * n * samples * super_size * super_size,
            bytes_accessed=4 * n * samples * super_size,
            transcendentals=0,
        ),
        name="outer_terms",
    )(meta, outer_row, outer_col, known, right_side, outer_blocks)


def cross_kernel(chunk, before, meta, pattern, base, window, *refs):
    solved, (send, keep, joined, total) = refs[: len(before)], refs[len(before) :]
    piece = solved[0].shape[1]
    lanes = 0
    for ref, columns in zip(solved, before):
        width = ref.shape[2]
        for o in range(ref.shape[0]):
            z, x = o // 2, o % 2
            start = (x * (ref.shape[0] // 2) + z) * piece
            joined[start : start + piece, lanes : lanes + width] = ref[o]
        lanes += width
    earlier = [j for columns in before for j in columns]
    for kk, k in enumerate(chunk):
        block = jnp.concatenate(
            [window[j, k] * pattern[j, k].astype(F32).astype(BF16) for j in earlier], axis=0
        )
        total[...] = base[kk] - jnp.dot(joined[...], block, preferred_element_type=F32)
        store_split(total, kk, meta[1], send, keep)


def cross_terms(meta, pattern, base, window_blocks, solved, chunk, before):
    n, samples, super_size = base.shape
    rows = window_blocks.shape[2]
    return pl.pallas_call(
        functools.partial(cross_kernel, chunk, before),
        out_shape=[
            jax.ShapeDtypeStruct((n, samples // 2, super_size), BF16),
            jax.ShapeDtypeStruct((n, samples // 2, super_size), F32),
        ],
        in_specs=[SMEM_SPEC, SMEM_SPEC] + [VMEM_SPEC] * (2 + len(solved)),
        out_specs=[VMEM_SPEC] * 2,
        scratch_shapes=[
            pltpu.VMEM((samples, rows * sum(len(c) for c in before)), BF16),
            pltpu.VMEM((samples, super_size), F32),
        ],
        compiler_params=params(),
        name="cross_terms",
    )(meta, pattern, base, window_blocks, *solved)


def add_kernel(meta, keep, got, *outs):
    piece = outs[0].shape[1]
    for kk in range(keep.shape[0]):
        for d, out in enumerate(outs):
            rows = pl.ds(pl.multiple_of(meta[4 + d] * piece, piece), piece)
            out[kk] = (keep[kk, rows] + got[kk, rows].astype(F32)).astype(out.dtype)


def scatter_sum(meta, send, keep, owners):
    pair_swap = [(o, o ^ 1) for o in range(owners)]
    got = lax.ppermute(send, "own", pair_swap)
    n, half, super_size = keep.shape
    depth = owners // 2
    shapes = [
        jax.ShapeDtypeStruct((n, half // depth, super_size), F32 if d == 0 else BF16)
        for d in range(depth)
    ]
    parts = pl.pallas_call(
        add_kernel,
        out_shape=shapes,
        in_specs=[SMEM_SPEC, VMEM_SPEC, VMEM_SPEC],
        out_specs=[VMEM_SPEC] * depth,
        compiler_params=params(),
        name="pair_sum",
    )(meta, keep, got)
    moved = [
        lax.ppermute(parts[d], "own", [(o, o ^ (2 * d)) for o in range(owners)])
        for d in range(1, depth)
    ]
    return [parts[0]] + moved


def solve_kernel(columns, pattern, weights, *refs):
    chunks = (len(refs) - 3) // 4
    parts, (out, slab, sems) = refs[: 4 * chunks], refs[4 * chunks :]
    blocks = stage_blocks(columns)
    copies = []
    for place in range(len(blocks)):
        copy = pltpu.make_async_copy(weights.at[:, place], slab.at[place], sems.at[place])
        copy.start()
        copies.append(copy)
    size = slab.shape[3]
    done, place = {}, 0
    per = len(columns) // chunks
    width = size // out.shape[0]
    for index, k in enumerate(columns):
        mine = parts[4 * (index // per) : 4 * (index // per) + 4]
        value = mine[0][index % per]
        for part in mine[1:]:
            value = value + part[index % per].astype(F32)
        for j in columns[:index]:
            copies[place].wait()
            block = slab[place].reshape(size, size)
            value = value - pattern[j, k].astype(F32) * jnp.dot(
                done[j], block, preferred_element_type=F32
            )
            place += 1
        copies[place].wait()
        block = slab[place].reshape(size, size)
        done[k] = lax.dot_general(
            value.astype(BF16), block, (((1,), (1,)), ((), ())), preferred_element_type=F32
        ).astype(BF16)
        place += 1
        for o in range(out.shape[0]):
            out[o, :, index * width : (index + 1) * width] = done[k][:, o * width : (o + 1) * width]


def solve_stage(pattern, weights, chunks, columns, owners):
    pieces, count, rows, super_size = weights.shape
    piece = chunks[0][0].shape[1]
    width = super_size // owners
    flat = [part for parts in chunks for part in parts]
    return pl.pallas_call(
        functools.partial(solve_kernel, columns),
        out_shape=jax.ShapeDtypeStruct((owners, piece, width * len(columns)), BF16),
        in_specs=[SMEM_SPEC, ANY_SPEC] + [VMEM_SPEC] * len(flat),
        out_specs=VMEM_SPEC,
        scratch_shapes=[
            pltpu.VMEM((count, pieces, rows, super_size), BF16),
            pltpu.SemaphoreType.DMA((count,)),
        ],
        compiler_params=params(),
        name="solve_stage",
    )(pattern, weights, *flat)


def place_kernel(stages, *refs):
    solved, (out, joined) = refs[: len(stages)], refs[len(stages) :]
    owners, piece = solved[0].shape[0], solved[0].shape[1]
    rows = out.shape[1]
    for ref, columns in zip(solved, stages):
        for first in range(0, len(columns), 2):
            for o in range(owners):
                joined[o * piece : (o + 1) * piece] = ref[o, :, first * rows : (first + 2) * rows]
            flipped = joined[...].T
            out[columns[first]] = flipped[:rows]
            out[columns[first + 1]] = flipped[rows:]


def place_rows(solved, stages, columns, rows):
    owners, piece, _ = solved[0].shape
    return pl.pallas_call(
        functools.partial(place_kernel, stages),
        out_shape=jax.ShapeDtypeStruct((columns, rows, owners * piece), BF16),
        in_specs=[VMEM_SPEC] * len(solved),
        out_specs=VMEM_SPEC,
        scratch_shapes=[pltpu.VMEM((owners * piece, 2 * rows), BF16)],
        compiler_params=params(),
        name="place_rows",
    )(*solved)


def staged_body(
    owners,
    known,
    outer_blocks,
    outer_row,
    outer_col,
    right_side,
    window_blocks,
    window_pattern,
    diag_inverse,
):
    own = lax.axis_index("own")
    z, x = own // 2, own % 2
    meta = jnp.stack([own, x, lax.axis_index("tile"), z, z, z ^ 1, z ^ 2, z ^ 3]).astype(jnp.int32)
    weights = gather_weights(meta, window_blocks, diag_inverse, STAGES)
    solved = []
    for stage, columns in enumerate(STAGES):
        chunks = []
        for first in range(0, len(columns), CHUNK):
            chunk = columns[first : first + CHUNK]
            outer = outer_terms(
                meta, outer_row, outer_col, known, right_side, outer_blocks, chunk, stage == 0
            )
            if stage == 0:
                send, keep = outer
            else:
                send, keep = cross_terms(
                    meta, window_pattern, outer[0], window_blocks, solved, chunk, STAGES[:stage]
                )
            chunks.append(scatter_sum(meta, send, keep, owners))
        mine = solve_stage(window_pattern, weights[stage], chunks, columns, owners)
        solved.append(lax.all_to_all(mine, "own", 0, 0, tiled=True))
    solved = [
        s.reshape(owners // 2, 2, *s.shape[1:]).swapaxes(0, 1).reshape(s.shape) for s in solved
    ]
    return place_rows(solved, STAGES, right_side.shape[0], right_side.shape[1])


def plain_body(
    known,
    outer_blocks,
    outer_row,
    outer_col,
    right_side,
    window_blocks,
    window_pattern,
    diag_inverse,
):
    owner_index = lax.axis_index("own")
    columns = right_side.shape[0]
    rows_dev = right_side.shape[1]
    super_size = window_blocks.shape[3]
    sample_count = known.shape[2]
    local_row = outer_row - owner_index * known.shape[0]

    def add_block(block_index, totals):
        factor_block = lax.dynamic_index_in_dim(outer_blocks, block_index, 0, keepdims=False)
        source_row = lax.dynamic_index_in_dim(local_row, block_index, 0, keepdims=False)
        target_col = lax.dynamic_index_in_dim(outer_col, block_index, 0, keepdims=False)
        source = lax.dynamic_index_in_dim(known, source_row, 0, keepdims=False)
        product = lax.dot_general(
            factor_block, source, (((0,), (0,)), ((), ())), preferred_element_type=F32
        )
        current = lax.dynamic_index_in_dim(totals, target_col, 0, keepdims=False)
        return lax.dynamic_update_index_in_dim(totals, current + product, target_col, 0)

    outer_sum = lax.fori_loop(
        0,
        outer_blocks.shape[0],
        add_block,
        jnp.zeros((columns, super_size, sample_count), F32),
    )
    solved = jnp.zeros((columns, rows_dev, sample_count), BF16)
    for column in reversed(range(columns)):
        local_term = lax.dynamic_update_slice(
            jnp.zeros((super_size, sample_count), F32),
            right_side[column].astype(F32),
            (owner_index * rows_dev, jnp.zeros((), jnp.int32)),
        )
        pattern_mask = window_pattern[:, column].astype(BF16)
        weighted = solved * pattern_mask[:, None, None]
        window_term = jnp.einsum(
            "jrc,jrs->cs", window_blocks[:, column], weighted, preferred_element_type=F32
        )
        residual = lax.psum(local_term - outer_sum[column] - window_term, "own")
        values = lax.dot_general(
            diag_inverse[column],
            residual.astype(BF16),
            (((0,), (0,)), ((), ())),
            preferred_element_type=F32,
        )
        solved = solved.at[column].set(values.astype(BF16))
    return solved


def solution(mesh):
    owners = mesh.shape["own"]
    body = functools.partial(staged_body, owners) if owners == 8 else plain_body
    return jax.shard_map(
        body,
        mesh=mesh,
        in_specs=(
            P(("grp", "own"), None, "tile"),
            P(("grp", "own"), None, None),
            P(("grp", "own")),
            P(("grp", "own")),
            P("grp", "own", "tile"),
            P("grp", None, "own", None),
            P("grp", None),
            P("grp", None, "own"),
        ),
        out_specs=P("grp", "own", "tile"),
        check_vma=False,
    )
```

time: 841 us -> 242 us (0.29)
  blocking collectives: 628 us -> 0 us
  waiting for transfers between devices: 0 us -> 119 us
  matrix products: 75.7 us -> 0 us
  Pallas kernels: 0 us -> 62.9 us
  loops' own time: 61.1 us -> 0 us
  local copies, waits for them, and re-layouts: 58.9 us -> 8.07 us
  starting transfers between devices: 0 us -> 38 us
  between operations: 0.18 us -> 13.6 us
  other arithmetic: 12.3 us -> 0 us
    psum x8 -> x0, blocking collectives: 628 us -> none  [body(): residual = lax.psum(local_term, 'own')]
    ppermute x0 -> x16, waiting for transfers between devices: none -> 99.4 us  [the longest x4 65 us: scatter_sum(): got = lax.ppermute(send, 'own', pair_swap)]
    dot_general x32 -> x0, matrix products: 75.7 us -> none  [the longest x16 45 us: add_block(): lax.dot_general(factor_block, source, (((0,), (0,)), ((), ())), preferred...]
    pallas_call x0 -> x14, Pallas kernels: none -> 62.9 us  [the longest x4 25.9 us: outer_terms(): pl.pallas_call(functools.partial(outer_kernel, columns, split), out_shape...]
    another operation x1 -> x0, loops' own time: 61.1 us -> none  [body(): lax.fori_loop(0, outer_blocks.shape[0], add_block, jnp.zeros((columns, su...]
    dynamic_slice x48 -> x0, local copies, waits for them, and re-layouts: 43.8 us -> none  [the longest x16 24.2 us: add_block(): current = lax.dynamic_index_in_dim(totals, target_col, 0, keepdims=False)]
    ppermute x0 -> x16, starting transfers between devices: none -> 27.8 us  [the longest x12 22 us: scatter_sum(): lax.ppermute(parts[d], 'own', [(o, o ^ 2 * d) for o in range(owners)])]
    all_to_all x0 -> x2, waiting for transfers between devices: none -> 18.6 us  [staged_body(): solved.append(lax.all_to_all(mine, 'own', 0, 0, tiled=True))]
  transfers between devices with their start and end apart: 0 -> 20, of which waited for: 0 -> 9; matrix products, arithmetic and copies ran while one was open for 0% -> 0% of each run, Pallas kernels for 0% -> 18%
where the time goes in v1:
time: 242 us; the launch traced here: 241 us
  waiting for transfers between devices  119 us (49%)
  Pallas kernels  62.9 us (26%)
  starting transfers between devices  38 us (16%)
  between operations  13.6 us (6%)
  local copies, waits for them, and re-layouts  8.07 us (3%)
    ppermute x4, waiting for transfers between devices, scatter_sum(): got = lax.ppermute(send, 'own', pair_swap)  65 us
    ppermute x12, waiting for transfers between devices, scatter_sum(): lax.ppermute(parts[d], 'own', [(o, o ^ 2 * d) for o in range(owners)])  34.3 us
    pallas_call x4, Pallas kernels, outer_terms(): pl.pallas_call(functools.partial(outer_kernel, columns, split), out_shape...  25.9 us
    ppermute x12, starting transfers between devices, scatter_sum(): lax.ppermute(parts[d], 'own', [(o, o ^ 2 * d) for o in range(owners)])  22 us
    all_to_all x2, waiting for transfers between devices, staged_body(): solved.append(lax.all_to_all(mine, 'own', 0, 0, tiled=True))  18.6 us
    pallas_call x1, Pallas kernels, gather_weights(): pl.pallas_call(functools.partial(weights_kernel, stages), out_shape=shape...  13.8 us
    pallas_call x2, Pallas kernels, solve_stage(): pl.pallas_call(functools.partial(solve_kernel, columns), out_shape=jax.Sh...  11 us
    all_to_all x2, starting transfers between devices, staged_body(): solved.append(lax.all_to_all(mine, 'own', 0, 0, tiled=True))  10.1 us
  transfers between devices with their start and end apart: 20, of which 9 were waited for; matrix products, arithmetic and copies ran while one was open for 0% of the time, Pallas kernels for 18%

profile of v1, /device:TPU:0, one launch (start us, length us, event | category | flops | bytes accessed | tf_op | source)
XLA Modules:
  0.0 241.3 jit_solution(6744069947084634324)
XLA Ops:
  6.5 1.5 copy.12.diag_ref
  8.2 13.8 %own_weights.1 = (bf16[10,32,512]{2,1,0:T(8,128)(2,1)}, bf16[10,32,512]{2,1,0:T(8,128)(2,1)}) custom-call(s32[8]{0:T(128)S(1)} %stack.32.meta, bf16[8,8,64,512]{3,2,1,0:T(8,128)(2,1)} %window.3, bf16[8,512,64]{2,1,0:T(8,128)(2,1)S(1)} %copy.12.diag_ref), custom_call_target="tpu_custom_call" | custom-call | tf_op jit(solution)/shard_map/own_weights/pallas_call | solution.py:63
  22.8 4.8 %outer_terms.5 = (bf16[2,384,512]{2,1,0:T(8,128)(2,1)S(1)}, f32[2,384,512]{2,1,0:T(8,128)S(1)}) custom-call(s32[8]{0:T(128)S(1)} %stack.32.meta, s32[16]{0:T(128)S(1)} %copy-done.11, s32[16]{0:T(128)S(1)} %copy-done.12, bf16[2,512,768]{2,1,0:T(8,128)(2,1)} %known.7, bf16[8,64,768]{2,1,0:T(8,128)(2,1)S(1)} %copy-done.1, bf16[16,512,512]{2,1,0:T(8,128)(2,1)} %blocks.7), custom_call_target="tpu_custom_call" | custom-call | flops 1610612736 | bytes 3145728 | tf_op jit(solution)/shard_map/outer_terms/pallas_call | solution.py:140
  27.6 3.6 %collective-permute-start.4 = (bf16[2,384,512]{2,1,0:T(8,128)(2,1)S(1)}, bf16[2,384,512]{2,1,0:T(8,128)(2,1)S(1)}, u32[]{:S(2)}, u32[]{:S(2)}) collective-permute-start(bf16[2,384,512]{2,1,0:T(8,128)(2,1)S(1)} %get-tuple-element.39), channel_id=1, source_target_pairs={{0,2},{2,0},{4,6},{6,4},{8,10},{10,8},{12,14},{14,12},{1,3},{3,1},... | collective-permute-start | bytes 2359304 | tf_op jit(solution)/shard_map/ppermute | solution.py:211
  31.2 7.4 %outer_terms.4 = (bf16[2,384,512]{2,1,0:T(8,128)(2,1)S(1)}, f32[2,384,512]{2,1,0:T(8,128)S(1)}) custom-call(s32[8]{0:T(128)S(1)} %stack.32.meta, s32[16]{0:T(128)S(1)} %copy-done.11, s32[16]{0:T(128)S(1)} %copy-done.12, bf16[2,512,768]{2,1,0:T(8,128)(2,1)} %known.7, bf16[8,64,768]{2,1,0:T(8,128)(2,1)S(1)} %copy-done.1, bf16[16,512,512]{2,1,0:T(8,128)(2,1)} %blocks.7), custom_call_target="tpu_custom_call" | custom-call | flops 1610612736 | bytes 3145728 | tf_op jit(solution)/shard_map/outer_terms/pallas_call | solution.py:140
  38.7 14.4 %collective-permute-done.4.got = bf16[2,384,512]{2,1,0:T(8,128)(2,1)S(1)} collective-permute-done((bf16[2,384,512]{2,1,0:T(8,128)(2,1)S(1)}, bf16[2,384,512]{2,1,0:T(8,128)(2,1)S(1)}, u32[]{:S(2)}, u32[]{:S(2)}) %collective-permute-start.4) | collective-permute-done | bytes 786464 | tf_op jit(solution)/shard_map/ppermute | solution.py:211
  53.7 4.1 %collective-permute-start.5 = (bf16[2,96,512]{2,1,0:T(8,128)(2,1)S(1)}, bf16[2,96,512]{2,1,0:T(8,128)(2,1)S(1)}, u32[]{:S(2)}, u32[]{:S(2)}) collective-permute-start(bf16[2,96,512]{2,1,0:T(8,128)(2,1)S(1)} %get-tuple-element.41), channel_id=1, source_target_pairs={{0,4},{2,6},{4,0},{6,2},{8,12},{10,14},{12,8},{14,10},{1,5},{3,7},... | collective-permute-start | bytes 589832 | tf_op jit(solution)/shard_map/ppermute | solution.py:227
  57.8 1.2 collective-permute-start.6
  59.0 1.2 collective-permute-start.7
  60.2 21.9 %collective-permute-done.got = bf16[2,384,512]{2,1,0:T(8,128)(2,1)S(1)} collective-permute-done((bf16[2,384,512]{2,1,0:T(8,128)(2,1)S(1)}, bf16[2,384,512]{2,1,0:T(8,128)(2,1)S(1)}, u32[]{:S(2)}, u32[]{:S(2)}) %collective-permute-start) | collective-permute-done | bytes 786464 | tf_op jit(solution)/shard_map/ppermute | solution.py:211
  82.8 4.7 %collective-permute-start.1 = (bf16[2,96,512]{2,1,0:T(8,128)(2,1)S(1)}, bf16[2,96,512]{2,1,0:T(8,128)(2,1)S(1)}, u32[]{:S(2)}, u32[]{:S(2)}) collective-permute-start(bf16[2,96,512]{2,1,0:T(8,128)(2,1)S(1)} %get-tuple-element.35), channel_id=1, source_target_pairs={{0,4},{2,6},{4,0},{6,2},{8,12},{10,14},{12,8},{14,10},{1,5},{3,7},... | collective-permute-start | bytes 589832 | tf_op jit(solution)/shard_map/ppermute | solution.py:227
  88.1 1.9 collective-permute-start.3
  90.7 6.8 %collective-permute-done.1.refs_1_ = bf16[2,96,512]{2,1,0:T(8,128)(2,1)S(1)} collective-permute-done((bf16[2,96,512]{2,1,0:T(8,128)(2,1)S(1)}, bf16[2,96,512]{2,1,0:T(8,128)(2,1)S(1)}, u32[]{:S(2)}, u32[]{:S(2)}) %collective-permute-start.1) | collective-permute-done | bytes 196640 | tf_op jit(solution)/shard_map/ppermute | solution.py:227
  98.2 11.9 %collective-permute-done.2.refs_2_ = bf16[2,96,512]{2,1,0:T(8,128)(2,1)S(1)} collective-permute-done((bf16[2,96,512]{2,1,0:T(8,128)(2,1)S(1)}, bf16[2,96,512]{2,1,0:T(8,128)(2,1)S(1)}, u32[]{:S(2)}, u32[]{:S(2)}) %collective-permute-start.2) | collective-permute-done | bytes 196640 | tf_op jit(solution)/shard_map/ppermute | solution.py:227
  115.1 5.5 %solve_stage.2 = bf16[8,96,256]{2,1,0:T(8,128)(2,1)} custom-call(s32[8,8]{1,0:T(8,128)S(1)} %copy-done.10, bf16[16,10,32,512]{3,2,1,0:T(8,128)(2,1)} %bitcast.21, f32[2,96,512]{2,1,0:T(8,128)S(1)} %get-tuple-element.34.refs_0_, bf16[2,96,512]{2,1,0:T(8,128)(2,1)S(1)} %copy-done.5, bf16[2,96,512]{2,1,0:T(8,128)(2,1)S(1)} %copy-done.7, ...), custom_call_target="tpu_custom_call" | custom-call | tf_op jit(solution)/shard_map/solve_stage/pallas_call | solution.py:273
  120.6 5.4 %all-to-all-start = ((bf16[8,96,256]{2,1,0:T(8,128)(2,1)}), bf16[8,96,256]{2,1,0:T(8,128)(2,1)S(1)}, u32[]{:S(2)}, u32[]{:S(2)}) async-start(bf16[8,96,256]{2,1,0:T(8,128)(2,1)} %solve_stage.2), calls=%async_computation | async-start | bytes 786432 | tf_op jit(solution)/shard_map/all_to_all | solution.py:344
  126.0 7.6 %outer_terms.7.base = f32[2,768,512]{2,1,0:T(8,128)} custom-call(s32[8]{0:T(128)S(1)} %stack.32.meta, s32[16]{0:T(128)S(1)} %copy-done.11, s32[16]{0:T(128)S(1)} %copy-done.12, bf16[2,512,768]{2,1,0:T(8,128)(2,1)S(1)} %copy-done, bf16[8,64,768]{2,1,0:T(8,128)(2,1)S(1)} %copy-done.1, bf16[16,512,512]{2,1,0:T(8,128)(2,1)} %blocks.7), custom_call_target="tpu_custom_call" | custom-call | flops 1610612736 | bytes 3145728 | tf_op jit(solution)/shard_map/outer_terms/pallas_call | solution.py:140
  133.6 7.0 %all-to-all-done.refs_0_ = bf16[8,96,256]{2,1,0:T(8,128)(2,1)S(1)} async-done(((bf16[8,96,256]{2,1,0:T(8,128)(2,1)}), bf16[8,96,256]{2,1,0:T(8,128)(2,1)S(1)}, u32[]{:S(2)}, u32[]{:S(2)}) %all-to-all-start) | async-done | bytes 393248 | tf_op jit(solution)/shard_map/all_to_all | solution.py:344
  140.6 4.4 %cross_terms.3 = (bf16[2,384,512]{2,1,0:T(8,128)(2,1)S(1)}, f32[2,384,512]{2,1,0:T(8,128)S(1)}) custom-call(s32[8]{0:T(128)S(1)} %stack.32.meta, s32[8,8]{1,0:T(8,128)S(1)} %copy-done.10, f32[2,768,512]{2,1,0:T(8,128)} %outer_terms.7.base, bf16[8,8,64,512]{3,2,1,0:T(8,128)(2,1)} %window.3, bf16[8,96,256]{2,1,0:T(8,128)(2,1)S(1)} %all-to-all-done.refs_0_), custom_call_target="tpu_custom_call" | custom-call | tf_op jit(solution)/shard_map/cross_terms/pallas_call | solution.py:184
  145.0 1.5 collective-permute-start.12
  146.5 6.2 %outer_terms.6.base = f32[2,768,512]{2,1,0:T(8,128)} custom-call(s32[8]{0:T(128)S(1)} %stack.32.meta, s32[16]{0:T(128)S(1)} %copy-done.11, s32[16]{0:T(128)S(1)} %copy-done.12, bf16[2,512,768]{2,1,0:T(8,128)(2,1)S(1)} %copy-done, bf16[8,64,768]{2,1,0:T(8,128)(2,1)S(1)} %copy-done.1, bf16[16,512,512]{2,1,0:T(8,128)(2,1)} %blocks.7), custom_call_target="tpu_custom_call" | custom-call | flops 1610612736 | bytes 3145728 | tf_op jit(solution)/shard_map/outer_terms/pallas_call | solution.py:140
  152.7 3.9 %cross_terms.2 = (bf16[2,384,512]{2,1,0:T(8,128)(2,1)S(1)}, f32[2,384,512]{2,1,0:T(8,128)S(1)}) custom-call(s32[8]{0:T(128)S(1)} %stack.32.meta, s32[8,8]{1,0:T(8,128)S(1)} %copy-done.10, f32[2,768,512]{2,1,0:T(8,128)} %outer_terms.6.base, bf16[8,8,64,512]{3,2,1,0:T(8,128)(2,1)} %window.3, bf16[8,96,256]{2,1,0:T(8,128)(2,1)S(1)} %all-to-all-done.refs_0_), custom_call_target="tpu_custom_call" | custom-call | tf_op jit(solution)/shard_map/cross_terms/pallas_call | solution.py:184
  157.3 17.3 %collective-permute-done.12.got = bf16[2,384,512]{2,1,0:T(8,128)(2,1)S(1)} collective-permute-done((bf16[2,384,512]{2,1,0:T(8,128)(2,1)S(1)}, bf16[2,384,512]{2,1,0:T(8,128)(2,1)S(1)}, u32[]{:S(2)}, u32[]{:S(2)}) %collective-permute-start.12) | collective-permute-done | bytes 786464 | tf_op jit(solution)/shard_map/ppermute | solution.py:211
  175.3 1.8 collective-permute-start.13
  177.1 2.3 collective-permute-start.14
  179.7 11.4 %collective-permute-done.8.got = bf16[2,384,512]{2,1,0:T(8,128)(2,1)S(1)} collective-permute-done((bf16[2,384,512]{2,1,0:T(8,128)(2,1)S(1)}, bf16[2,384,512]{2,1,0:T(8,128)(2,1)S(1)}, u32[]{:S(2)}, u32[]{:S(2)}) %collective-permute-start.8) | collective-permute-done | bytes 786464 | tf_op jit(solution)/shard_map/ppermute | solution.py:211
  191.8 2.5 %collective-permute-start.10 = (bf16[2,96,512]{2,1,0:T(8,128)(2,1)S(1)}, bf16[2,96,512]{2,1,0:T(8,128)(2,1)S(1)}, u32[]{:S(2)}, u32[]{:S(2)}) collective-permute-start(bf16[2,96,512]{2,1,0:T(8,128)(2,1)S(1)} %get-tuple-element.49), channel_id=1, source_target_pairs={{0,8},{2,10},{4,12},{6,14},{8,0},{10,2},{12,4},{14,6},{1,9},{3,11}... | collective-permute-start | bytes 589832 | tf_op jit(solution)/shard_map/ppermute | solution.py:227
  194.3 1.4 collective-permute-start.11
  195.8 15.6 %collective-permute-done.10.refs_2_ = bf16[2,96,512]{2,1,0:T(8,128)(2,1)S(1)} collective-permute-done((bf16[2,96,512]{2,1,0:T(8,128)(2,1)S(1)}, bf16[2,96,512]{2,1,0:T(8,128)(2,1)S(1)}, u32[]{:S(2)}, u32[]{:S(2)}) %collective-permute-start.10) | collective-permute-done | bytes 196640 | tf_op jit(solution)/shard_map/ppermute | solution.py:227
  211.4 5.5 %solve_stage.3 = bf16[8,96,256]{2,1,0:T(8,128)(2,1)} custom-call(s32[8,8]{1,0:T(8,128)S(1)} %copy-done.10, bf16[16,10,32,512]{3,2,1,0:T(8,128)(2,1)} %bitcast.20, f32[2,96,512]{2,1,0:T(8,128)S(1)} %get-tuple-element.47.refs_0_, bf16[2,96,512]{2,1,0:T(8,128)(2,1)S(1)} %collective-permute-done.9.refs_1_, ...), custom_call_target="tpu_custom_call" | custom-call | tf_op jit(solution)/shard_map/solve_stage/pallas_call | solution.py:273
  216.9 4.7 %all-to-all-start.1 = ((bf16[8,96,256]{2,1,0:T(8,128)(2,1)}), bf16[8,96,256]{2,1,0:T(8,128)(2,1)S(1)}, u32[]{:S(2)}, u32[]{:S(2)}) async-start(bf16[8,96,256]{2,1,0:T(8,128)(2,1)} %solve_stage.3), calls=%async_computation.1 | async-start | bytes 786432 | tf_op jit(solution)/shard_map/all_to_all | solution.py:344
  221.6 11.6 %all-to-all-done.1 = bf16[8,96,256]{2,1,0:T(8,128)(2,1)S(1)} async-done(((bf16[8,96,256]{2,1,0:T(8,128)(2,1)}), bf16[8,96,256]{2,1,0:T(8,128)(2,1)S(1)}, u32[]{:S(2)}, u32[]{:S(2)}) %all-to-all-start.1) | async-done | bytes 393248 | tf_op jit(solution)/shard_map/all_to_all | solution.py:344
  (54 shorter events, 12.9 us)
Async XLA Ops:
  6.5 104.9 %all-gather.5.cloned.1.call-start = ((), (), s32[]{:S(2)}) async-start(), calls=%async_computation.2 | async-start | bytes 5570560 | tf_op jit(solution)/shard_map/all_gather | solution.py:75
  8.1 14.7 %copy-start.1 = (bf16[8,64,768]{2,1,0:T(8,128)(2,1)S(1)}, bf16[8,64,768]{2,1,0:T(8,128)(2,1)}, u32[]{:S(2)}) copy-start(bf16[8,64,768]{2,1,0:T(8,128)(2,1)} %draws.7) | copy-start | bytes 2359300
  8.1 14.7 %copy-start.11 = (s32[16]{0:T(128)S(1)}, s32[16]{0:T(128)}, u32[]{:S(2)}) copy-start(s32[16]{0:T(128)} %row_ref.7) | copy-start | bytes 196
  8.1 14.7 %copy-start.12 = (s32[16]{0:T(128)S(1)}, s32[16]{0:T(128)}, u32[]{:S(2)}) copy-start(s32[16]{0:T(128)} %col_ref.7) | copy-start | bytes 196
  22.0 173.8 %all-gather.7.cloned.1.call-start = ((), (), s32[]{:S(2)}) async-start(), calls=%async_computation.3 | async-start | bytes 5570560 | tf_op jit(solution)/shard_map/all_gather | solution.py:75
  27.6 25.5 %collective-permute-start.4 = (bf16[2,384,512]{2,1,0:T(8,128)(2,1)S(1)}, bf16[2,384,512]{2,1,0:T(8,128)(2,1)S(1)}, u32[]{:S(2)}, u32[]{:S(2)}) collective-permute-start(bf16[2,384,512]{2,1,0:T(8,128)(2,1)S(1)} %get-tuple-element.39), channel_id=1, source_target_pairs={{0,2},{2,0},{4,6},{6,4},{8,10},{10,8},{12,14},{14,12},{1,3},{3,1},... | collective-permute-start | bytes 2359304 | tf_op jit(solution)/shard_map/ppermute | solution.py:211
  38.6 72.8 %copy-start.10 = (s32[8,8]{1,0:T(8,128)S(1)}, s32[8,8]{1,0:T(8,128)}, u32[]{:S(2)}) copy-start(s32[8,8]{1,0:T(8,128)} %pattern.7) | copy-start | bytes 772
  38.6 43.6 %collective-permute-start = (bf16[2,384,512]{2,1,0:T(8,128)(2,1)S(1)}, bf16[2,384,512]{2,1,0:T(8,128)(2,1)S(1)}, u32[]{:S(2)}, u32[]{:S(2)}) collective-permute-start(bf16[2,384,512]{2,1,0:T(8,128)(2,1)S(1)} %get-tuple-element.33), channel_id=1, source_target_pairs={{0,2},{2,0},{4,6},{6,4},{8,10},{10,8},{12,14},{14,12},{1,3},{3,1},... | collective-permute-start | bytes 2359304 | tf_op jit(solution)/shard_map/ppermute | solution.py:211
  53.7 34.4 %collective-permute-start.5 = (bf16[2,96,512]{2,1,0:T(8,128)(2,1)S(1)}, bf16[2,96,512]{2,1,0:T(8,128)(2,1)S(1)}, u32[]{:S(2)}, u32[]{:S(2)}) collective-permute-start(bf16[2,96,512]{2,1,0:T(8,128)(2,1)S(1)} %get-tuple-element.41), channel_id=1, source_target_pairs={{0,4},{2,6},{4,0},{6,2},{8,12},{10,14},{12,8},{14,10},{1,5},{3,7},... | collective-permute-start | bytes 589832 | tf_op jit(solution)/shard_map/ppermute | solution.py:227
  57.8 32.2 %collective-permute-start.6 = (bf16[2,96,512]{2,1,0:T(8,128)(2,1)S(1)}, bf16[2,96,512]{2,1,0:T(8,128)(2,1)S(1)}, u32[]{:S(2)}, u32[]{:S(2)}) collective-permute-start(bf16[2,96,512]{2,1,0:T(8,128)(2,1)S(1)} %get-tuple-element.42), channel_id=1, source_target_pairs={{0,8},{2,10},{4,12},{6,14},{8,0},{10,2},{12,4},{14,6},{1,9},{3,11}... | collective-permute-start | bytes 589832 | tf_op jit(solution)/shard_map/ppermute | solution.py:227
  59.0 31.0 %collective-permute-start.7 = (bf16[2,96,512]{2,1,0:T(8,128)(2,1)S(1)}, bf16[2,96,512]{2,1,0:T(8,128)(2,1)S(1)}, u32[]{:S(2)}, u32[]{:S(2)}) collective-permute-start(bf16[2,96,512]{2,1,0:T(8,128)(2,1)S(1)} %get-tuple-element.43), channel_id=1, source_target_pairs={{0,12},{2,14},{4,8},{6,10},{8,4},{10,6},{12,0},{14,2},{1,13},{3,15... | collective-permute-start | bytes 589832 | tf_op jit(solution)/shard_map/ppermute | solution.py:227
  82.8 14.7 %collective-permute-start.1 = (bf16[2,96,512]{2,1,0:T(8,128)(2,1)S(1)}, bf16[2,96,512]{2,1,0:T(8,128)(2,1)S(1)}, u32[]{:S(2)}, u32[]{:S(2)}) collective-permute-start(bf16[2,96,512]{2,1,0:T(8,128)(2,1)S(1)} %get-tuple-element.35), channel_id=1, source_target_pairs={{0,4},{2,6},{4,0},{6,2},{8,12},{10,14},{12,8},{14,10},{1,5},{3,7},... | collective-permute-start | bytes 589832 | tf_op jit(solution)/shard_map/ppermute | solution.py:227
  87.5 22.5 %collective-permute-start.2 = (bf16[2,96,512]{2,1,0:T(8,128)(2,1)S(1)}, bf16[2,96,512]{2,1,0:T(8,128)(2,1)S(1)}, u32[]{:S(2)}, u32[]{:S(2)}) collective-permute-start(bf16[2,96,512]{2,1,0:T(8,128)(2,1)S(1)} %get-tuple-element.36), channel_id=1, source_target_pairs={{0,8},{2,10},{4,12},{6,14},{8,0},{10,2},{12,4},{14,6},{1,9},{3,11}... | collective-permute-start | bytes 589832 | tf_op jit(solution)/shard_map/ppermute | solution.py:227
  88.1 22.6 %collective-permute-start.3 = (bf16[2,96,512]{2,1,0:T(8,128)(2,1)S(1)}, bf16[2,96,512]{2,1,0:T(8,128)(2,1)S(1)}, u32[]{:S(2)}, u32[]{:S(2)}) collective-permute-start(bf16[2,96,512]{2,1,0:T(8,128)(2,1)S(1)} %get-tuple-element.37), channel_id=1, source_target_pairs={{0,12},{2,14},{4,8},{6,10},{8,4},{10,6},{12,0},{14,2},{1,13},{3,15... | collective-permute-start | bytes 589832 | tf_op jit(solution)/shard_map/ppermute | solution.py:227
  90.0 0.7 copy-start.2
  97.5 0.7 copy-start.4
  110.1 0.7 copy-start.6
  111.4 0.9 copy-start.3
  112.3 0.9 copy-start.5
  113.3 0.9 copy-start.7
  114.2 0.9 copy-start.9
  115.1 10.9 %copy-start = (bf16[2,512,768]{2,1,0:T(8,128)(2,1)S(1)}, bf16[2,512,768]{2,1,0:T(8,128)(2,1)}, u32[]{:S(2)}) copy-start(bf16[2,512,768]{2,1,0:T(8,128)(2,1)} %known.7) | copy-start | bytes 4718596
  120.6 20.0 %all-to-all-start = ((bf16[8,96,256]{2,1,0:T(8,128)(2,1)}), bf16[8,96,256]{2,1,0:T(8,128)(2,1)S(1)}, u32[]{:S(2)}, u32[]{:S(2)}) async-start(bf16[8,96,256]{2,1,0:T(8,128)(2,1)} %solve_stage.2), calls=%async_computation | async-start | bytes 786432 | tf_op jit(solution)/shard_map/all_to_all | solution.py:344
  145.0 29.6 %collective-permute-start.12 = (bf16[2,384,512]{2,1,0:T(8,128)(2,1)S(1)}, bf16[2,384,512]{2,1,0:T(8,128)(2,1)S(1)}, u32[]{:S(2)}, u32[]{:S(2)}) collective-permute-start(bf16[2,384,512]{2,1,0:T(8,128)(2,1)S(1)} %get-tuple-element.52), channel_id=1, source_target_pairs={{0,2},{2,0},{4,6},{6,4},{8,10},{10,8},{12,14},{14,12},{1,3},{3,1},... | collective-permute-start | bytes 2359304 | tf_op jit(solution)/shard_map/ppermute | solution.py:211
  156.7 34.4 %collective-permute-start.8 = (bf16[2,384,512]{2,1,0:T(8,128)(2,1)S(1)}, bf16[2,384,512]{2,1,0:T(8,128)(2,1)S(1)}, u32[]{:S(2)}, u32[]{:S(2)}) collective-permute-start(bf16[2,384,512]{2,1,0:T(8,128)(2,1)S(1)} %get-tuple-element.46), channel_id=1, source_target_pairs={{0,2},{2,0},{4,6},{6,4},{8,10},{10,8},{12,14},{14,12},{1,3},{3,1},... | collective-permute-start | bytes 2359304 | tf_op jit(solution)/shard_map/ppermute | solution.py:211
  175.3 20.5 %collective-permute-start.13 = (bf16[2,96,512]{2,1,0:T(8,128)(2,1)S(1)}, bf16[2,96,512]{2,1,0:T(8,128)(2,1)S(1)}, u32[]{:S(2)}, u32[]{:S(2)}) collective-permute-start(bf16[2,96,512]{2,1,0:T(8,128)(2,1)S(1)} %get-tuple-element.54), channel_id=1, source_target_pairs={{0,4},{2,6},{4,0},{6,2},{8,12},{10,14},{12,8},{14,10},{1,5},{3,7},... | collective-permute-start | bytes 589832 | tf_op jit(solution)/shard_map/ppermute | solution.py:227
  177.1 18.7 %collective-permute-start.14 = (bf16[2,96,512]{2,1,0:T(8,128)(2,1)S(1)}, bf16[2,96,512]{2,1,0:T(8,128)(2,1)S(1)}, u32[]{:S(2)}, u32[]{:S(2)}) collective-permute-start(bf16[2,96,512]{2,1,0:T(8,128)(2,1)S(1)} %get-tuple-element.55), channel_id=1, source_target_pairs={{0,8},{2,10},{4,12},{6,14},{8,0},{10,2},{12,4},{14,6},{1,9},{3,11}... | collective-permute-start | bytes 589832 | tf_op jit(solution)/shard_map/ppermute | solution.py:227
  179.4 16.4 %collective-permute-start.15 = (bf16[2,96,512]{2,1,0:T(8,128)(2,1)S(1)}, bf16[2,96,512]{2,1,0:T(8,128)(2,1)S(1)}, u32[]{:S(2)}, u32[]{:S(2)}) collective-permute-start(bf16[2,96,512]{2,1,0:T(8,128)(2,1)S(1)} %get-tuple-element.56), channel_id=1, source_target_pairs={{0,12},{2,14},{4,8},{6,10},{8,4},{10,6},{12,0},{14,2},{1,13},{3,15... | collective-permute-start | bytes 589832 | tf_op jit(solution)/shard_map/ppermute | solution.py:227
  191.8 19.6 %collective-permute-start.10 = (bf16[2,96,512]{2,1,0:T(8,128)(2,1)S(1)}, bf16[2,96,512]{2,1,0:T(8,128)(2,1)S(1)}, u32[]{:S(2)}, u32[]{:S(2)}) collective-permute-start(bf16[2,96,512]{2,1,0:T(8,128)(2,1)S(1)} %get-tuple-element.49), channel_id=1, source_target_pairs={{0,8},{2,10},{4,12},{6,14},{8,0},{10,2},{12,4},{14,6},{1,9},{3,11}... | collective-permute-start | bytes 589832 | tf_op jit(solution)/shard_map/ppermute | solution.py:227
  194.3 17.1 %collective-permute-start.11 = (bf16[2,96,512]{2,1,0:T(8,128)(2,1)S(1)}, bf16[2,96,512]{2,1,0:T(8,128)(2,1)S(1)}, u32[]{:S(2)}, u32[]{:S(2)}) collective-permute-start(bf16[2,96,512]{2,1,0:T(8,128)(2,1)S(1)} %get-tuple-element.50), channel_id=1, source_target_pairs={{0,12},{2,14},{4,8},{6,10},{8,4},{10,6},{12,0},{14,2},{1,13},{3,15... | collective-permute-start | bytes 589832 | tf_op jit(solution)/shard_map/ppermute | solution.py:227
  195.7 15.7 %collective-permute-start.9 = (bf16[2,96,512]{2,1,0:T(8,128)(2,1)S(1)}, bf16[2,96,512]{2,1,0:T(8,128)(2,1)S(1)}, u32[]{:S(2)}, u32[]{:S(2)}) collective-permute-start(bf16[2,96,512]{2,1,0:T(8,128)(2,1)S(1)} %get-tuple-element.48), channel_id=1, source_target_pairs={{0,4},{2,6},{4,0},{6,2},{8,12},{10,14},{12,8},{14,10},{1,5},{3,7},... | collective-permute-start | bytes 589832 | tf_op jit(solution)/shard_map/ppermute | solution.py:227
  216.9 16.4 %all-to-all-start.1 = ((bf16[8,96,256]{2,1,0:T(8,128)(2,1)}), bf16[8,96,256]{2,1,0:T(8,128)(2,1)S(1)}, u32[]{:S(2)}, u32[]{:S(2)}) async-start(bf16[8,96,256]{2,1,0:T(8,128)(2,1)} %solve_stage.3), calls=%async_computation.1 | async-start | bytes 786432 | tf_op jit(solution)/shard_map/all_to_all | solution.py:344
  (1 other events, 0.7 us)
Sparse Core Ops, SparseCore 0:
  22.1 86.9 all-gather.4
  111.4 70.6 all-gather.6

commit v2 on v1

v2 whole, which is shorter than its diff:
```python
import functools

import jax
import jax.numpy as jnp
from jax import lax
from jax.experimental import pallas as pl
from jax.experimental.pallas import tpu as pltpu
from jax.sharding import PartitionSpec as P

F32, BF16 = jnp.float32, jnp.bfloat16
VMEM_LIMIT = 50 * 1024 * 1024
STAGES = ((7, 6, 5, 4), (3, 2, 1, 0))
CHUNKS = (((7, 6), (5, 4)), ((3, 2), (1,), (0,)))

SMEM_SPEC = pl.BlockSpec(memory_space=pltpu.SMEM)
VMEM_SPEC = pl.BlockSpec(memory_space=pltpu.VMEM)
ANY_SPEC = pl.BlockSpec(memory_space=pl.ANY)


def params(**extra):
    return pltpu.CompilerParams(vmem_limit_bytes=VMEM_LIMIT, **extra)


def stage_blocks(columns):
    blocks = []
    for place, k in enumerate(columns):
        blocks += [(j, k) for j in columns[:place]] + [(k, k)]
    return blocks


def weights_kernel(stages, meta, window_ref, diag_ref, *refs):
    outs, (turned, sems) = refs[-2 - len(stages) : -2], refs[-2:]
    half, rows = outs[0].shape[2], window_ref.shape[2]
    start = pl.multiple_of(meta[2] * half, half)
    copies = []

    def move(source, target):
        copy = pltpu.make_async_copy(source, target, sems.at[len(copies)])
        copy.start()
        copies.append(copy)

    blocks = [
        (out.at[0, place], j, k)
        for out, columns in zip(outs, stages)
        for place, (j, k) in enumerate(stage_blocks(columns))
    ]
    for target, j, k in blocks:
        if j != k:
            move(window_ref.at[j, k, pl.ds(start, half)], target)
    lane = lax.broadcasted_iota(jnp.int32, (half, rows), 1)
    pick = jnp.where(lane == lax.broadcasted_iota(jnp.int32, (half, rows), 0) + start, 1.0, 0.0)
    pick = pick.astype(BF16)
    for target, j, k in blocks:
        if j == k:
            turned[k] = lax.dot_general(
                pick, diag_ref[k], (((1,), (1,)), ((), ())), preferred_element_type=F32
            ).astype(BF16)
            move(turned.at[k], target)
    for copy in copies:
        copy.wait()


def own_weights(meta, window_blocks, diag_inverse, columns, after):
    count, super_size, rows = diag_inverse.shape
    blocks = len(stage_blocks(columns))
    return pl.pallas_call(
        functools.partial(weights_kernel, (columns,)),
        out_shape=jax.ShapeDtypeStruct((1, blocks, rows // 2, super_size), BF16),
        in_specs=[SMEM_SPEC, ANY_SPEC, VMEM_SPEC] + [ANY_SPEC] * len(after),
        out_specs=ANY_SPEC,
        scratch_shapes=[
            pltpu.VMEM((count, rows // 2, super_size), BF16),
            pltpu.SemaphoreType.DMA((blocks,)),
        ],
        compiler_params=params(),
        name="own_weights",
    )(meta, window_blocks, diag_inverse, *after)


def join_kernel(left, right, *refs):
    out, sems = refs[-2:]
    half = out.shape[0] // 2
    copies = [
        pltpu.make_async_copy(source, out.at[pl.ds(i * half, half)], sems.at[i])
        for i, source in enumerate((left, right))
    ]
    for copy in copies:
        copy.start()
    for copy in copies:
        copy.wait()


def join(left, right, after):
    return pl.pallas_call(
        join_kernel,
        out_shape=jax.ShapeDtypeStruct((2 * left.shape[0], *left.shape[1:]), left.dtype),
        in_specs=[ANY_SPEC] * (2 + len(after)),
        out_specs=ANY_SPEC,
        scratch_shapes=[pltpu.SemaphoreType.DMA((2,))],
        compiler_params=params(),
        name="join",
    )(left, right, *after)


def hold_kernel(source, *refs):
    out, sem = refs[-2:]
    copy = pltpu.make_async_copy(source, out, sem)
    copy.start()
    copy.wait()


def hold(source, after):
    return pl.pallas_call(
        hold_kernel,
        out_shape=jax.ShapeDtypeStruct(source.shape, source.dtype),
        in_specs=[ANY_SPEC] * (1 + len(after)),
        out_specs=ANY_SPEC,
        scratch_shapes=[pltpu.SemaphoreType.DMA],
        compiler_params=params(),
        name="hold",
    )(source, *after)


def z_move(part, d, owners):
    return lax.ppermute(part, "own", [(o, o ^ (2 * d)) for o in range(owners)])


def x_move(part, owners):
    return lax.ppermute(part, "own", [(o, o ^ 1) for o in range(owners)])


def other_core(parts):
    return [lax.ppermute(w, "tile", [(0, 1), (1, 0)]) for w in parts]


def store_split(total, kk, side, send, keep):
    rows = send.shape[1]
    send[kk] = total[pl.ds(pl.multiple_of((1 - side) * rows, rows), rows)].astype(BF16)
    keep[kk] = total[pl.ds(pl.multiple_of(side * rows, rows), rows)]


def outer_kernel(columns, split, meta, row_ref, col_ref, known, draws, blocks, *refs):
    outs, (turned, slab, total, sems) = refs[-4 - (2 if split else 1) : -4], refs[-4:]
    high, low = columns[0], columns[-1]
    count, rows_dev = blocks.shape[0], known.shape[0]

    def block_copy(b):
        return pltpu.make_async_copy(blocks.at[b], slab.at[b], sems.at[b])

    def start(b, _):
        @pl.when((col_ref[b] >= low) & (col_ref[b] <= high))
        def _():
            block_copy(b).start()

        return 0

    lax.fori_loop(0, count, start, 0)
    for r in range(rows_dev):
        turned[r] = known[r].T
    rows = draws.shape[1]
    place = lax.broadcasted_iota(jnp.int32, (rows, total.shape[1]), 0) + meta[0] * rows
    lane = lax.broadcasted_iota(jnp.int32, (rows, total.shape[1]), 1)
    spread = jnp.where(place == lane, 1.0, 0.0).astype(BF16)

    def column(kk, _):
        k = high - kk
        total[...] = jnp.dot(draws[k].T, spread, preferred_element_type=F32)

        def block(b, _):
            @pl.when(col_ref[b] == k)
            def _():
                block_copy(b).wait()
                source = row_ref[b] - meta[0] * rows_dev
                total[...] -= jnp.dot(turned[source], slab[b], preferred_element_type=F32)

            return 0

        lax.fori_loop(0, count, block, 0)
        if split:
            store_split(total, kk, meta[1], *outs)
        else:
            outs[0][kk] = total[...]
        return 0

    lax.fori_loop(0, len(columns), column, 0)


def outer_terms(
    meta, outer_row, outer_col, known, right_side, outer_blocks, columns, split, after
):
    rows_dev, super_size, samples = known.shape
    count, n = outer_blocks.shape[0], len(columns)
    if split:
        shapes = [
            jax.ShapeDtypeStruct((n, samples // 2, super_size), BF16),
            jax.ShapeDtypeStruct((n, samples // 2, super_size), F32),
        ]
    else:
        shapes = [jax.ShapeDtypeStruct((n, samples, super_size), F32)]
    return pl.pallas_call(
        functools.partial(outer_kernel, columns, split),
        out_shape=shapes,
        in_specs=[SMEM_SPEC] * 3
        + [VMEM_SPEC, VMEM_SPEC, ANY_SPEC]
        + [ANY_SPEC] * len(after),
        out_specs=[VMEM_SPEC] * len(shapes),
        scratch_shapes=[
            pltpu.VMEM((rows_dev, samples, super_size), BF16),
            pltpu.VMEM((count, super_size, super_size), BF16),
            pltpu.VMEM((samples, super_size), F32),
            pltpu.SemaphoreType.DMA((count,)),
        ],
        compiler_params=params(),
        name="outer_terms",
    )(meta, outer_row, outer_col, known, right_side, outer_blocks, *after)


def cross_kernel(chunk, offset, before, meta, pattern, base, window, *refs):
    solved, (send, keep, joined, total, blocks, sems) = refs[: len(before)], refs[-6:]
    piece, depth = solved[0].shape[1], solved[0].shape[0] // 2
    rows = window.shape[2]
    earlier = [j for columns in before for j in columns]
    copies = []
    for kk, k in enumerate(chunk):
        for index, j in enumerate(earlier):
            copy = pltpu.make_async_copy(
                window.at[j, k], blocks.at[kk, pl.ds(index * rows, rows)], sems.at[kk, index]
            )
            copy.start()
            copies.append(copy)
    lanes = 0
    for ref in solved:
        width = ref.shape[2]
        for o in range(2 * depth):
            start = ((o % 2) * depth + o // 2) * piece
            joined[start : start + piece, lanes : lanes + width] = ref[o]
        lanes += width
    for copy in copies:
        copy.wait()
    for kk, k in enumerate(chunk):
        for index, j in enumerate(earlier):
            here = pl.ds(index * rows, rows)
            blocks[kk, here] = blocks[kk, here] * pattern[j, k].astype(F32).astype(BF16)
        total[...] = base[kk] - jnp.dot(joined[...], blocks[kk], preferred_element_type=F32)
        store_split(total, kk, meta[1], send, keep)


def cross_terms(meta, pattern, base, window_blocks, solved, chunk, offset, before, after):
    _, samples, super_size = base.shape
    n = len(chunk)
    rows = window_blocks.shape[2]
    earlier = sum(len(c) for c in before)
    return pl.pallas_call(
        functools.partial(cross_kernel, chunk, offset, before),
        out_shape=[
            jax.ShapeDtypeStruct((n, samples // 2, super_size), BF16),
            jax.ShapeDtypeStruct((n, samples // 2, super_size), F32),
        ],
        grid=(1,),
        in_specs=[
            SMEM_SPEC,
            SMEM_SPEC,
            pl.BlockSpec((n, samples, super_size), lambda i: (offset // n, 0, 0)),
            ANY_SPEC,
        ]
        + [VMEM_SPEC] * len(solved)
        + [ANY_SPEC] * len(after),
        out_specs=[VMEM_SPEC] * 2,
        scratch_shapes=[
            pltpu.VMEM((samples, rows * earlier), BF16),
            pltpu.VMEM((samples, super_size), F32),
            pltpu.VMEM((n, rows * earlier, super_size), BF16),
            pltpu.SemaphoreType.DMA((n, earlier)),
        ],
        compiler_params=params(),
        name="cross_terms",
    )(meta, pattern, base, window_blocks, *solved, *after)


def pair_kernel(meta, keep, got, *refs):
    send, mine = refs[-2:]
    piece = send.shape[2]
    for kk in range(keep.shape[0]):
        for d in range(4):
            rows = pl.ds(pl.multiple_of(meta[4 + d] * piece, piece), piece)
            out = mine if d % 2 == 0 else send
            out[d // 2, kk] = (keep[kk, rows] + got[kk, rows].astype(F32)).astype(out.dtype)


def pair_sum(meta, keep, got, owners, after):
    n, half, super_size = keep.shape
    shape = (2, n, half // (owners // 2), super_size)
    return pl.pallas_call(
        pair_kernel,
        out_shape=[jax.ShapeDtypeStruct(shape, BF16), jax.ShapeDtypeStruct(shape, F32)],
        in_specs=[SMEM_SPEC, VMEM_SPEC, VMEM_SPEC] + [ANY_SPEC] * len(after),
        out_specs=[VMEM_SPEC] * 2,
        compiler_params=params(),
        name="pair_sum",
    )(meta, keep, got, *after)


def line_kernel(mine, got, *refs):
    send, keep = refs[-2:]
    keep[...] = mine[0] + got[0].astype(F32)
    send[...] = (mine[1] + got[1].astype(F32)).astype(BF16)


def line_sum(mine, got, after):
    return pl.pallas_call(
        line_kernel,
        out_shape=[
            jax.ShapeDtypeStruct(mine.shape[1:], BF16),
            jax.ShapeDtypeStruct(mine.shape[1:], F32),
        ],
        in_specs=[VMEM_SPEC] * 2 + [ANY_SPEC] * len(after),
        out_specs=[VMEM_SPEC] * 2,
        compiler_params=params(),
        name="line_sum",
    )(mine, got, *after)


def solve_kernel(columns, ready, groups, whole, first, meta, pattern, *refs):
    weights, refs = refs[:4], refs[4:]
    count = 2 * len(groups)
    parts, solved = refs[:count], refs[count : count + len(ready)]
    out, slab, sems = refs[-3:]
    size = slab.shape[3]
    starts = [0]
    for k in [k for group in groups for k in group]:
        starts.append(starts[-1] + columns.index(k) + 1)
    cuts = [(0, starts[1]), (starts[1], starts[-1])] if len(starts) > 2 else [(0, starts[1])]
    copies = {}
    for cut, (low, high) in enumerate(cuts):
        for which, source in enumerate(weights):
            for e, d in enumerate((0, 2, 1, 3)):
                x = meta[1] if which % 2 == 0 else 1 - meta[1]
                t = meta[2] if which < 2 else 1 - meta[2]
                copy = pltpu.make_async_copy(
                    source.at[e, pl.ds(first + low, high - low)],
                    slab.at[pl.ds(low, high - low), (meta[4 + d] * 2 + x) * 2 + t],
                    sems.at[cut, 4 * which + e],
                )
                copy.start()
                copies.setdefault(low, []).append(copy)
    done = {}
    for ref, group in zip(solved, ready):
        for index, j in enumerate(group):
            done[j] = ref[index]
    place = 0

    def next_block():
        for copy in copies.pop(place, ()):
            copy.wait()
        return slab[place].reshape(size, size)

    for g, group in enumerate(groups):
        for index, k in enumerate(group):
            value = parts[2 * g][index] + parts[2 * g + 1][index].astype(F32)
            for j in list(done):
                value = value - pattern[j, k].astype(F32) * jnp.dot(
                    done[j], next_block(), preferred_element_type=F32
                )
                place += 1
            done[k] = lax.dot_general(
                value.astype(BF16),
                next_block(),
                (((1,), (1,)), ((), ())),
                preferred_element_type=F32,
            ).astype(BF16)
            place += 1
    if not whole:
        for index, k in enumerate([k for group in groups for k in group]):
            out[index] = done[k]
    else:
        width = size // out.shape[0]
        for index, k in enumerate(columns):
            for o in range(out.shape[0]):
                here = done[k][:, o * width : (o + 1) * width]
                out[o, :, index * width : (index + 1) * width] = here


def solve(
    meta, pattern, weights, columns, ready, solved, groups, parts, whole, owners, after=()
):
    _, _, rows, super_size = weights[0].shape
    piece = parts[0][0].shape[1]
    before, n = sum(len(g) for g in ready), sum(len(g) for g in groups)
    first, count = before * (before + 1) // 2, n * before + n * (n + 1) // 2
    if whole:
        shape = (owners, piece, super_size // owners * len(columns))
    else:
        shape = (n, piece, super_size)
    flat = [p for part in parts for p in part]
    return pl.pallas_call(
        functools.partial(solve_kernel, columns, ready, groups, whole, first),
        out_shape=jax.ShapeDtypeStruct(shape, BF16),
        in_specs=[SMEM_SPEC] * 2
        + [ANY_SPEC] * 4
        + [VMEM_SPEC] * (len(flat) + len(solved))
        + [ANY_SPEC] * len(after),
        out_specs=VMEM_SPEC,
        scratch_shapes=[
            pltpu.VMEM((count, 2 * owners, rows, super_size), BF16),
            pltpu.SemaphoreType.DMA((2, 2 * owners)),
        ],
        compiler_params=params(),
        name="solve",
    )(meta, pattern, *weights, *flat, *solved, *after)


def place_kernel(stages, *refs):
    solved, (out, joined) = refs[: len(stages)], refs[len(stages) :]
    owners, piece = solved[0].shape[0], solved[0].shape[1]
    rows = out.shape[1]
    for ref, columns in zip(solved, stages):
        for at in range(0, len(columns), 2):
            first = min(at, len(columns) - 2)
            for o in range(owners):
                start = ((o % 2) * (owners // 2) + o // 2) * piece
                joined[start : start + piece] = ref[o, :, first * rows : (first + 2) * rows]
            flipped = joined[...].T
            out[columns[first]] = flipped[:rows]
            out[columns[first + 1]] = flipped[rows:]


def place_rows(solved, stages, columns, rows):
    owners, piece, _ = solved[0].shape
    return pl.pallas_call(
        functools.partial(place_kernel, stages),
        out_shape=jax.ShapeDtypeStruct((columns, rows, owners * piece), BF16),
        in_specs=[VMEM_SPEC] * len(solved),
        out_specs=VMEM_SPEC,
        scratch_shapes=[pltpu.VMEM((owners * piece, 2 * rows), BF16)],
        compiler_params=params(),
        name="place_rows",
    )(*solved)


def staged_body(
    owners,
    known,
    outer_blocks,
    outer_row,
    outer_col,
    right_side,
    window_blocks,
    window_pattern,
    diag_inverse,
):
    own = lax.axis_index("own")
    z, x = own // 2, own % 2
    meta = jnp.stack([own, x, lax.axis_index("tile"), z, z, z ^ 1, z ^ 2, z ^ 3]).astype(jnp.int32)
    first, last = STAGES
    outer = functools.partial(
        outer_terms, meta, outer_row, outer_col, known, right_side, outer_blocks
    )
    weigh = functools.partial(own_weights, meta, window_blocks, diag_inverse)
    own_0 = weigh(first, ())
    opposite_0 = z_move(own_0, 2, owners)
    send_a, keep_a = outer(CHUNKS[0][0], True, (own_0,))
    got_a = x_move(send_a, owners)
    send_b, keep_b = outer(CHUNKS[0][1], True, (send_a,))
    got_b = x_move(send_b, owners)
    (base,) = outer(last, False, (send_b,))
    near_0 = join(own_0, opposite_0, (base,))
    far_0 = z_move(near_0, 1, owners)
    own_1 = weigh(last, (near_0,))
    opposite_1 = z_move(own_1, 2, owners)
    line_a, mine_a = pair_sum(meta, keep_a, got_a, owners, (own_1,))
    across_a = z_move(line_a, 1, owners)
    line_b, mine_b = pair_sum(meta, keep_b, got_b, owners, (line_a,))
    across_b = z_move(line_b, 1, owners)
    line_0 = join(near_0, far_0, (line_b,))
    beside_0 = x_move(line_0, owners)
    end_a, total_a = line_sum(mine_a, across_a, (line_0,))
    last_a = z_move(end_a, 2, owners)
    end_b, total_b = line_sum(mine_b, across_b, (end_a,))
    last_b = z_move(end_b, 2, owners)
    near_1 = join(own_1, opposite_1, (end_b,))
    far_1 = z_move(near_1, 1, owners)
    line_1 = join(near_1, far_1, (beside_0,))
    beside_1 = x_move(line_1, owners)
    weights = [line_0, beside_0, *other_core([line_0, hold(beside_0, (near_1,))])]
    done = solve(
        meta,
        window_pattern,
        weights,
        first,
        (),
        (),
        CHUNKS[0],
        ((total_a, last_a), (total_b, last_b)),
        True,
        owners,
        (line_1,),
    )
    rows_0 = lax.all_to_all(done, "own", 0, 0, tiled=True)
    moved, at = [], 0
    for chunk in CHUNKS[1]:
        send, keep = cross_terms(
            meta, window_pattern, base, window_blocks, (rows_0,), chunk, at, (first,), ()
        )
        moved.append((keep, x_move(send, owners)))
        at += len(chunk)
    parts, after = [], ()
    for keep, got in moved:
        line, mine = pair_sum(meta, keep, got, owners, after)
        end, total = line_sum(mine, z_move(line, 1, owners), ())
        parts.append((total, z_move(end, 2, owners)))
    weights = [line_1, beside_1, *other_core([line_1, beside_1])]
    solved = []
    for index, chunk in enumerate(CHUNKS[1]):
        out = solve(
            meta,
            window_pattern,
            weights,
            last,
            CHUNKS[1][:index],
            solved,
            (chunk,),
            parts[index : index + 1],
            index == len(CHUNKS[1]) - 1,
            owners,
        )
        solved.append(out)
    rows_1 = lax.all_to_all(solved[-1], "own", 0, 0, tiled=True)
    return place_rows([rows_0, rows_1], STAGES, right_side.shape[0], right_side.shape[1])


def plain_body(
    known,
    outer_blocks,
    outer_row,
    outer_col,
    right_side,
    window_blocks,
    window_pattern,
    diag_inverse,
):
    owner_index = lax.axis_index("own")
    columns = right_side.shape[0]
    rows_dev = right_side.shape[1]
    super_size = window_blocks.shape[3]
    sample_count = known.shape[2]
    local_row = outer_row - owner_index * known.shape[0]

    def add_block(block_index, totals):
        factor_block = lax.dynamic_index_in_dim(outer_blocks, block_index, 0, keepdims=False)
        source_row = lax.dynamic_index_in_dim(local_row, block_index, 0, keepdims=False)
        target_col = lax.dynamic_index_in_dim(outer_col, block_index, 0, keepdims=False)
        source = lax.dynamic_index_in_dim(known, source_row, 0, keepdims=False)
        product = lax.dot_general(
            factor_block, source, (((0,), (0,)), ((), ())), preferred_element_type=F32
        )
        current = lax.dynamic_index_in_dim(totals, target_col, 0, keepdims=False)
        return lax.dynamic_update_index_in_dim(totals, current + product, target_col, 0)

    outer_sum = lax.fori_loop(
        0,
        outer_blocks.shape[0],
        add_block,
        jnp.zeros((columns, super_size, sample_count), F32),
    )
    solved = jnp.zeros((columns, rows_dev, sample_count), BF16)
    for column in reversed(range(columns)):
        local_term = lax.dynamic_update_slice(
            jnp.zeros((super_size, sample_count), F32),
            right_side[column].astype(F32),
            (owner_index * rows_dev, jnp.zeros((), jnp.int32)),
        )
        pattern_mask = window_pattern[:, column].astype(BF16)
        weighted = solved * pattern_mask[:, None, None]
        window_term = jnp.einsum(
            "jrc,jrs->cs", window_blocks[:, column], weighted, preferred_element_type=F32
        )
        residual = lax.psum(local_term - outer_sum[column] - window_term, "own")
        values = lax.dot_general(
            diag_inverse[column],
            residual.astype(BF16),
            (((0,), (0,)), ((), ())),
            preferred_element_type=F32,
        )
        solved = solved.at[column].set(values.astype(BF16))
    return solved


def solution(mesh):
    owners = mesh.shape["own"]
    body = functools.partial(staged_body, owners) if owners == 8 else plain_body
    return jax.shard_map(
        body,
        mesh=mesh,
        in_specs=(
            P(("grp", "own"), None, "tile"),
            P(("grp", "own"), None, None),
            P(("grp", "own")),
            P(("grp", "own")),
            P("grp", "own", "tile"),
            P("grp", None, "own", None),
            P("grp", None),
            P("grp", None, "own"),
        ),
        out_specs=P("grp", "own", "tile"),
        check_vma=False,
    )
```

time: 242 us -> 221 us (0.913)
  blocking collectives: 0 us -> 28.6 us
  waiting for transfers between devices: 119 us -> 101 us
  between operations: 13.6 us -> 0.33 us
  starting transfers between devices: 38 us -> 31.2 us
  Pallas kernels: 62.9 us -> 56.3 us
  local copies, waits for them, and re-layouts: 8.07 us -> 3.09 us
    all_to_all x0 -> x2, blocking collectives: none -> 28.6 us  [the longest x1 14.6 us: staged_body(): rows_0 = lax.all_to_all(done, 'own', 0, 0, tiled=True)]
    all_to_all x2 -> x0, waiting for transfers between devices: 18.6 us -> none  [staged_body(): solved.append(lax.all_to_all(mine, 'own', 0, 0, tiled=True))]
    all_to_all x2 -> x0, starting transfers between devices: 10.1 us -> none  [staged_body(): solved.append(lax.all_to_all(mine, 'own', 0, 0, tiled=True))]
    unnamed x27 -> x21, local copies, waits for them, and re-layouts: 7.93 us -> 3 us
    pallas_call x9 -> x24, Pallas kernels: 35.8 us -> 31.4 us  [the longest x4 13.3 us: solve(): pl.pallas_call(functools.partial(solve_kernel, columns, ready, groups, wh...]
    ppermute x16 -> x25, starting transfers between devices: 27.8 us -> 31.2 us  [the longest x14 22 us: z_move(): return lax.ppermute(part, 'own', [(o, o ^ 2 * d) for o in range(owners)])]
    pallas_call x4 -> x3, Pallas kernels: 25.9 us -> 23.8 us  [outer_terms(): pl.pallas_call(functools.partial(outer_kernel, columns, split), out_shape...]
    ppermute x16 -> x25, waiting for transfers between devices: 99.4 us -> 101 us  [the longest x14 65.9 us: z_move(): return lax.ppermute(part, 'own', [(o, o ^ 2 * d) for o in range(owners)])]
  transfers between devices with their start and end apart: 20 -> 25, of which waited for: 9 -> 12; matrix products, arithmetic and copies ran while one was open for 0% -> 0% of each run, Pallas kernels for 18% -> 23%
where the time goes in v2:
time: 221 us
  waiting for transfers between devices  101 us (46%)
  Pallas kernels  56.3 us (25%)
  starting transfers between devices  31.2 us (14%)
  blocking collectives  28.6 us (13%)
  local copies, waits for them, and re-layouts  3.09 us (1%)
    ppermute x14, waiting for transfers between devices, z_move(): return lax.ppermute(part, 'own', [(o, o ^ 2 * d) for o in range(owners)])  65.9 us
    ppermute x7, waiting for transfers between devices, x_move(): return lax.ppermute(part, 'own', [(o, o ^ 1) for o in range(owners)])  35.4 us
    pallas_call x3, Pallas kernels, outer_terms(): pl.pallas_call(functools.partial(outer_kernel, columns, split), out_shape...  23.8 us
    ppermute x14, starting transfers between devices, z_move(): return lax.ppermute(part, 'own', [(o, o ^ 2 * d) for o in range(owners)])  22 us
    all_to_all x1, blocking collectives, staged_body(): rows_0 = lax.all_to_all(done, 'own', 0, 0, tiled=True)  14.6 us
    all_to_all x1, blocking collectives, staged_body(): rows_1 = lax.all_to_all(solved[-1], 'own', 0, 0, tiled=True)  14 us
    pallas_call x4, Pallas kernels, solve(): pl.pallas_call(functools.partial(solve_kernel, columns, ready, groups, wh...  13.3 us
    pallas_call x3, Pallas kernels, cross_terms(): pl.pallas_call(functools.partial(cross_kernel, chunk, offset, before), ou...  9.46 us
  transfers between devices with their start and end apart: 25, of which 12 were waited for; matrix products, arithmetic and copies ran while one was open for 0% of the time, Pallas kernels for 23%

profile of v2, /device:TPU:0, one launch (start us, length us, event | category | flops | bytes accessed | tf_op | source)
XLA Modules:
  0.0 220.9 jit_solution(8552435171029549748)
XLA Ops:
  0.0 1.5 copy.9.diag_ref
  3.1 4.1 %collective-permute-start = (bf16[1,10,32,512]{3,2,1,0:T(8,128)(2,1)S(1)}, bf16[1,10,32,512]{3,2,1,0:T(8,128)(2,1)S(1)}, u32[]{:S(2)}, u32[]{:S(2)}) collective-permute-start(bf16[1,10,32,512]{3,2,1,0:T(8,128)(2,1)S(1)} %own_weights.2.refs_0_.left), channel_id=1, source_target_pairs={{0,8},{2,10},{4,12},{6,14},{8,0},{10,2},{12,4},{14,6},{1,9},{3,11}... | collective-permute-start | bytes 983048 | tf_op jit(solution)/shard_map/ppermute | solution.py:125
  7.2 6.0 %outer_terms.3 = (bf16[2,384,512]{2,1,0:T(8,128)(2,1)S(1)}, f32[2,384,512]{2,1,0:T(8,128)S(1)}) custom-call(s32[8]{0:T(128)S(1)} %stack.32.meta, s32[16]{0:T(128)S(1)} %copy-done.4, s32[16]{0:T(128)S(1)} %copy-done.5, bf16[2,512,768]{2,1,0:T(8,128)(2,1)} %known.5, bf16[8,64,768]{2,1,0:T(8,128)(2,1)S(1)} %copy-done.2, bf16[16,512,512]{2,1,0:T(8,128)(2,1)} %blocks.5, ...), custom_call_target="tpu_custom_call" | custom-call | tf_op jit(solution)/shard_map/outer_terms/pallas_call | solution.py:200
  14.7 6.0 %outer_terms.4 = (bf16[2,384,512]{2,1,0:T(8,128)(2,1)S(1)}, f32[2,384,512]{2,1,0:T(8,128)S(1)}) custom-call(s32[8]{0:T(128)S(1)} %stack.32.meta, s32[16]{0:T(128)S(1)} %copy-done.4, s32[16]{0:T(128)S(1)} %copy-done.5, bf16[2,512,768]{2,1,0:T(8,128)(2,1)} %known.5, bf16[8,64,768]{2,1,0:T(8,128)(2,1)S(1)} %copy-done.2, bf16[16,512,512]{2,1,0:T(8,128)(2,1)} %blocks.5, ...), custom_call_target="tpu_custom_call" | custom-call | tf_op jit(solution)/shard_map/outer_terms/pallas_call | solution.py:200
  21.3 11.8 %outer_terms.5.refs_0_.base = f32[4,768,512]{2,1,0:T(8,128)} custom-call(s32[8]{0:T(128)S(1)} %stack.32.meta, s32[16]{0:T(128)S(1)} %copy-done.4, s32[16]{0:T(128)S(1)} %copy-done.5, bf16[2,512,768]{2,1,0:T(8,128)(2,1)S(1)} %copy-done, bf16[8,64,768]{2,1,0:T(8,128)(2,1)S(1)} %copy-done.2, bf16[16,512,512]{2,1,0:T(8,128)(2,1)} %blocks.5, ...), custom_call_target="tpu_custom_call" | custom-call | tf_op jit(solution)/shard_map/outer_terms/pallas_call | solution.py:200
  33.3 2.1 collective-permute-start.1
  37.6 11.5 %collective-permute-done.2.got = bf16[2,384,512]{2,1,0:T(8,128)(2,1)S(1)} collective-permute-done((bf16[2,384,512]{2,1,0:T(8,128)(2,1)S(1)}, bf16[2,384,512]{2,1,0:T(8,128)(2,1)S(1)}, u32[]{:S(2)}, u32[]{:S(2)}) %collective-permute-start.2) | collective-permute-done | bytes 786464 | tf_op jit(solution)/shard_map/ppermute | solution.py:129
  50.3 1.8 collective-permute-start.4
  52.2 2.3 %collective-permute-start.8 = (bf16[2,2,96,512]{3,2,1,0:T(8,128)(2,1)S(1)}, bf16[2,2,96,512]{3,2,1,0:T(8,128)(2,1)S(1)}, u32[]{:S(2)}, u32[]{:S(2)}) collective-permute-start(bf16[2,2,96,512]{3,2,1,0:T(8,128)(2,1)S(1)} %get-tuple-element.39.refs_0_), channel_id=1, source_target_pairs={{0,4},{2,6},{4,0},{6,2},{8,12},{10,14},{12,8},{14,10},{1,5},{3,7},... | collective-permute-start | bytes 1179656 | tf_op jit(solution)/shard_map/ppermute | solution.py:125
  55.1 16.4 %collective-permute-done.8.got = bf16[2,2,96,512]{3,2,1,0:T(8,128)(2,1)S(1)} collective-permute-done((bf16[2,2,96,512]{3,2,1,0:T(8,128)(2,1)S(1)}, bf16[2,2,96,512]{3,2,1,0:T(8,128)(2,1)S(1)}, u32[]{:S(2)}, u32[]{:S(2)}) %collective-permute-start.8) | collective-permute-done | bytes 393248 | tf_op jit(solution)/shard_map/ppermute | solution.py:125
  71.6 5.9 %collective-permute-done.7.got = bf16[2,2,96,512]{3,2,1,0:T(8,128)(2,1)S(1)} collective-permute-done((bf16[2,2,96,512]{3,2,1,0:T(8,128)(2,1)S(1)}, bf16[2,2,96,512]{3,2,1,0:T(8,128)(2,1)S(1)}, u32[]{:S(2)}, u32[]{:S(2)}) %collective-permute-start.7) | collective-permute-done | bytes 393248 | tf_op jit(solution)/shard_map/ppermute | solution.py:125
  77.9 1.8 collective-permute-done.4.source.refs_0_.refs_1_
  79.9 2.7 %collective-permute-start.12 = (bf16[2,10,32,512]{3,2,1,0:T(8,128)(2,1)S(1)}, bf16[2,10,32,512]{3,2,1,0:T(8,128)(2,1)S(1)}, u32[]{:S(2)}, u32[]{:S(2)}) collective-permute-start(bf16[2,10,32,512]{3,2,1,0:T(8,128)(2,1)S(1)} %join.6.refs_0_.left), channel_id=1, source_target_pairs={{0,4},{2,6},{4,0},{6,2},{8,12},{10,14},{12,8},{14,10},{1,5},{3,7},... | collective-permute-start | bytes 1966088 | tf_op jit(solution)/shard_map/ppermute | solution.py:125
  82.6 15.3 %collective-permute-done.12.right = bf16[2,10,32,512]{3,2,1,0:T(8,128)(2,1)S(1)} collective-permute-done((bf16[2,10,32,512]{3,2,1,0:T(8,128)(2,1)S(1)}, bf16[2,10,32,512]{3,2,1,0:T(8,128)(2,1)S(1)}, u32[]{:S(2)}, u32[]{:S(2)}) %collective-permute-start.12) | collective-permute-done | bytes 655392 | tf_op jit(solution)/shard_map/ppermute | solution.py:125
  100.9 2.5 %collective-permute-start.10 = (bf16[2,96,512]{2,1,0:T(8,128)(2,1)S(1)}, bf16[2,96,512]{2,1,0:T(8,128)(2,1)S(1)}, u32[]{:S(2)}, u32[]{:S(2)}) collective-permute-start(bf16[2,96,512]{2,1,0:T(8,128)(2,1)S(1)} %get-tuple-element.43.refs_0_), channel_id=1, source_target_pairs={{0,8},{2,10},{4,12},{6,14},{8,0},{10,2},{12,4},{14,6},{1,9},{3,11}... | collective-permute-start | bytes 589832 | tf_op jit(solution)/shard_map/ppermute | solution.py:125
  103.4 13.9 %collective-permute-done.11.refs_7_ = bf16[2,96,512]{2,1,0:T(8,128)(2,1)S(1)} collective-permute-done((bf16[2,96,512]{2,1,0:T(8,128)(2,1)S(1)}, bf16[2,96,512]{2,1,0:T(8,128)(2,1)S(1)}, u32[]{:S(2)}, u32[]{:S(2)}) %collective-permute-start.11) | collective-permute-done | bytes 196640 | tf_op jit(solution)/shard_map/ppermute | solution.py:125
  117.4 3.1 %collective-permute-done.10.refs_5_ = bf16[2,96,512]{2,1,0:T(8,128)(2,1)S(1)} collective-permute-done((bf16[2,96,512]{2,1,0:T(8,128)(2,1)S(1)}, bf16[2,96,512]{2,1,0:T(8,128)(2,1)S(1)}, u32[]{:S(2)}, u32[]{:S(2)}) %collective-permute-start.10) | collective-permute-done | bytes 196640 | tf_op jit(solution)/shard_map/ppermute | solution.py:125
  121.9 4.6 %solve.4 = bf16[8,96,256]{2,1,0:T(8,128)(2,1)S(1)} custom-call(s32[8]{0:T(128)S(1)} %stack.32.meta, s32[8,8]{1,0:T(8,128)S(1)} %copy-done.3, bf16[4,10,32,512]{3,2,1,0:T(8,128)(2,1)S(1)} %join.5.refs_0_, bf16[4,10,32,512]{3,2,1,0:T(8,128)(2,1)} %copy-done.1, bf16[4,10,32,512]{3,2,1,0:T(8,128)(2,1)} %copy-done.8, bf16[4,10,32,512]{3,2,1,0:T(8,128)(2,1)} %copy-done.9, ...), custom_call_target="tpu_custom_call" | custom-call | tf_op jit(solution)/shard_map/solve/pallas_call | solution.py:395
  126.5 14.6 %all_to_all.10.refs_0_ = bf16[8,96,256]{2,1,0:T(8,128)(2,1)S(1)} all-to-all(bf16[8,96,256]{2,1,0:T(8,128)(2,1)S(1)} %solve.4), channel_id=1, replica_groups=mesh['grp'=2,'own'=8,'tile'=2] {'own'}, dimensions={0} | all-to-all | bytes 786432 | tf_op jit(solution)/shard_map/all_to_all | solution.py:498
  141.2 3.8 %cross_terms.4 = (bf16[2,384,512]{2,1,0:T(8,128)(2,1)S(1)}, f32[2,384,512]{2,1,0:T(8,128)S(1)}) custom-call(s32[8]{0:T(128)S(1)} %stack.32.meta, s32[8,8]{1,0:T(8,128)S(1)} %copy-done.3, f32[4,768,512]{2,1,0:T(8,128)} %outer_terms.5.refs_0_.base, bf16[8,8,64,512]{3,2,1,0:T(8,128)(2,1)} %window.5, bf16[8,96,256]{2,1,0:T(8,128)(2,1)S(1)} %all_to_all.10.refs_0_), custom_call_target="tpu_custom_call" | custom-call | tf_op jit(solution)/shard_map/cross_terms/pallas_call | solution.py:253
  146.6 2.8 %cross_terms.5 = (bf16[1,384,512]{2,1,0:T(8,128)(2,1)S(1)}, f32[1,384,512]{2,1,0:T(8,128)S(1)}) custom-call(s32[8]{0:T(128)S(1)} %stack.32.meta, s32[8,8]{1,0:T(8,128)S(1)} %copy-done.3, f32[4,768,512]{2,1,0:T(8,128)} %outer_terms.5.refs_0_.base, bf16[8,8,64,512]{3,2,1,0:T(8,128)(2,1)} %window.5, bf16[8,96,256]{2,1,0:T(8,128)(2,1)S(1)} %all_to_all.10.refs_0_), custom_call_target="tpu_custom_call" | custom-call | tf_op jit(solution)/shard_map/cross_terms/pallas_call | solution.py:253
  150.5 2.9 %cross_terms.3 = (bf16[1,384,512]{2,1,0:T(8,128)(2,1)S(1)}, f32[1,384,512]{2,1,0:T(8,128)S(1)}) custom-call(s32[8]{0:T(128)S(1)} %stack.32.meta, s32[8,8]{1,0:T(8,128)S(1)} %copy-done.3, f32[4,768,512]{2,1,0:T(8,128)} %outer_terms.5.refs_0_.base, bf16[8,8,64,512]{3,2,1,0:T(8,128)(2,1)} %window.5, bf16[8,96,256]{2,1,0:T(8,128)(2,1)S(1)} %all_to_all.10.refs_0_), custom_call_target="tpu_custom_call" | custom-call | tf_op jit(solution)/shard_map/cross_terms/pallas_call | solution.py:253
  154.5 11.0 %collective-permute-done.19.got = bf16[2,384,512]{2,1,0:T(8,128)(2,1)S(1)} collective-permute-done((bf16[2,384,512]{2,1,0:T(8,128)(2,1)S(1)}, bf16[2,384,512]{2,1,0:T(8,128)(2,1)S(1)}, u32[]{:S(2)}, u32[]{:S(2)}) %collective-permute-start.19) | collective-permute-done | bytes 786464 | tf_op jit(solution)/shard_map/ppermute | solution.py:129
  167.1 6.8 %collective-permute-done.22.got = bf16[1,384,512]{2,1,0:T(8,128)(2,1)S(1)} collective-permute-done((bf16[1,384,512]{2,1,0:T(8,128)(2,1)S(1)}, bf16[1,384,512]{2,1,0:T(8,128)(2,1)S(1)}, u32[]{:S(2)}, u32[]{:S(2)}) %collective-permute-start.22) | collective-permute-done | bytes 393248 | tf_op jit(solution)/shard_map/ppermute | solution.py:129
  175.5 4.2 %collective-permute-done.16.got = bf16[1,384,512]{2,1,0:T(8,128)(2,1)S(1)} collective-permute-done((bf16[1,384,512]{2,1,0:T(8,128)(2,1)S(1)}, bf16[1,384,512]{2,1,0:T(8,128)(2,1)S(1)}, u32[]{:S(2)}, u32[]{:S(2)}) %collective-permute-start.16) | collective-permute-done | bytes 393248 | tf_op jit(solution)/shard_map/ppermute | solution.py:129
  181.3 1.8 collective-permute-start.21
  184.4 4.3 %collective-permute-done.17.got = bf16[2,1,96,512]{3,2,1,0:T(8,128)(2,1)S(1)} collective-permute-done((bf16[2,1,96,512]{3,2,1,0:T(8,128)(2,1)S(1)}, bf16[2,1,96,512]{3,2,1,0:T(8,128)(2,1)S(1)}, u32[]{:S(2)}, u32[]{:S(2)}) %collective-permute-start.17) | collective-permute-done | bytes 196640 | tf_op jit(solution)/shard_map/ppermute | solution.py:125
  190.1 6.9 %collective-permute-done.21.refs_5_ = bf16[2,96,512]{2,1,0:T(8,128)(2,1)S(1)} collective-permute-done((bf16[2,96,512]{2,1,0:T(8,128)(2,1)S(1)}, bf16[2,96,512]{2,1,0:T(8,128)(2,1)S(1)}, u32[]{:S(2)}, u32[]{:S(2)}) %collective-permute-start.21) | collective-permute-done | bytes 196640 | tf_op jit(solution)/shard_map/ppermute | solution.py:125
  197.0 2.8 %solve.5.refs_6_ = bf16[2,96,512]{2,1,0:T(8,128)(2,1)S(1)} custom-call(s32[8]{0:T(128)S(1)} %stack.32.meta, s32[8,8]{1,0:T(8,128)S(1)} %copy-done.3, bf16[4,10,32,512]{3,2,1,0:T(8,128)(2,1)} %join.7.refs_8_.refs_0_, bf16[4,10,32,512]{3,2,1,0:T(8,128)(2,1)S(1)} %collective-permute-done.13.refs_1_, bf16[4,10,32,512]{3,2,1,0:T(8,128)(2,1)} %copy-done.6, ...), custom_call_target="tpu_custom_call" | custom-call | tf_op jit(solution)/shard_map/solve/pallas_call | solution.py:395
  199.8 2.8 %solve.6.refs_7_ = bf16[1,96,512]{2,1,0:T(8,128)(2,1)S(1)} custom-call(s32[8]{0:T(128)S(1)} %stack.32.meta, s32[8,8]{1,0:T(8,128)S(1)} %copy-done.3, bf16[4,10,32,512]{3,2,1,0:T(8,128)(2,1)} %join.7.refs_8_.refs_0_, bf16[4,10,32,512]{3,2,1,0:T(8,128)(2,1)S(1)} %collective-permute-done.13.refs_1_, bf16[4,10,32,512]{3,2,1,0:T(8,128)(2,1)} %copy-done.6, ...), custom_call_target="tpu_custom_call" | custom-call | tf_op jit(solution)/shard_map/solve/pallas_call | solution.py:395
  202.6 3.1 %solve.7 = bf16[8,96,256]{2,1,0:T(8,128)(2,1)S(1)} custom-call(s32[8]{0:T(128)S(1)} %stack.32.meta, s32[8,8]{1,0:T(8,128)S(1)} %copy-done.3, bf16[4,10,32,512]{3,2,1,0:T(8,128)(2,1)} %join.7.refs_8_.refs_0_, bf16[4,10,32,512]{3,2,1,0:T(8,128)(2,1)S(1)} %collective-permute-done.13.refs_1_, bf16[4,10,32,512]{3,2,1,0:T(8,128)(2,1)} %copy-done.6, ...), custom_call_target="tpu_custom_call" | custom-call | tf_op jit(solution)/shard_map/solve/pallas_call | solution.py:395
  205.7 14.0 %all_to_all.11.refs_1_ = bf16[8,96,256]{2,1,0:T(8,128)(2,1)S(1)} all-to-all(bf16[8,96,256]{2,1,0:T(8,128)(2,1)S(1)} %solve.7), channel_id=1, replica_groups=mesh['grp'=2,'own'=8,'tile'=2] {'own'}, dimensions={0} | all-to-all | bytes 786432 | tf_op jit(solution)/shard_map/all_to_all | solution.py:527
  (70 shorter events, 25.3 us)
Async XLA Ops:
  1.6 5.6 %copy-start.2 = (bf16[8,64,768]{2,1,0:T(8,128)(2,1)S(1)}, bf16[8,64,768]{2,1,0:T(8,128)(2,1)}, u32[]{:S(2)}) copy-start(bf16[8,64,768]{2,1,0:T(8,128)(2,1)} %draws.5) | copy-start | bytes 2359300
  1.6 5.6 %copy-start.4 = (s32[16]{0:T(128)S(1)}, s32[16]{0:T(128)}, u32[]{:S(2)}) copy-start(s32[16]{0:T(128)} %row_ref.5) | copy-start | bytes 196
  3.1 29.9 %collective-permute-start = (bf16[1,10,32,512]{3,2,1,0:T(8,128)(2,1)S(1)}, bf16[1,10,32,512]{3,2,1,0:T(8,128)(2,1)S(1)}, u32[]{:S(2)}, u32[]{:S(2)}) collective-permute-start(bf16[1,10,32,512]{3,2,1,0:T(8,128)(2,1)S(1)} %own_weights.2.refs_0_.left), channel_id=1, source_target_pairs={{0,8},{2,10},{4,12},{6,14},{8,0},{10,2},{12,4},{14,6},{1,9},{3,11}... | collective-permute-start | bytes 983048 | tf_op jit(solution)/shard_map/ppermute | solution.py:125
  13.2 8.1 %copy-start = (bf16[2,512,768]{2,1,0:T(8,128)(2,1)S(1)}, bf16[2,512,768]{2,1,0:T(8,128)(2,1)}, u32[]{:S(2)}) copy-start(bf16[2,512,768]{2,1,0:T(8,128)(2,1)} %known.5) | copy-start | bytes 4718596
  13.2 23.7 %collective-permute-start.3 = (bf16[2,384,512]{2,1,0:T(8,128)(2,1)S(1)}, bf16[2,384,512]{2,1,0:T(8,128)(2,1)S(1)}, u32[]{:S(2)}, u32[]{:S(2)}) collective-permute-start(bf16[2,384,512]{2,1,0:T(8,128)(2,1)S(1)} %get-tuple-element.35.refs_0_), channel_id=1, source_target_pairs={{0,2},{2,0},{4,6},{6,4},{8,10},{10,8},{12,14},{14,12},{1,3},{3,1},... | collective-permute-start | bytes 2359304 | tf_op jit(solution)/shard_map/ppermute | solution.py:129
  20.7 28.5 %collective-permute-start.2 = (bf16[2,384,512]{2,1,0:T(8,128)(2,1)S(1)}, bf16[2,384,512]{2,1,0:T(8,128)(2,1)S(1)}, u32[]{:S(2)}, u32[]{:S(2)}) collective-permute-start(bf16[2,384,512]{2,1,0:T(8,128)(2,1)S(1)} %get-tuple-element.36.refs_0_), channel_id=1, source_target_pairs={{0,2},{2,0},{4,6},{6,4},{8,10},{10,8},{12,14},{14,12},{1,3},{3,1},... | collective-permute-start | bytes 2359304 | tf_op jit(solution)/shard_map/ppermute | solution.py:129
  33.3 16.6 %collective-permute-start.1 = (bf16[2,10,32,512]{3,2,1,0:T(8,128)(2,1)S(1)}, bf16[2,10,32,512]{3,2,1,0:T(8,128)(2,1)S(1)}, u32[]{:S(2)}, u32[]{:S(2)}) collective-permute-start(bf16[2,10,32,512]{3,2,1,0:T(8,128)(2,1)S(1)} %join.4.refs_0_.left), channel_id=1, source_target_pairs={{0,4},{2,6},{4,0},{6,2},{8,12},{10,14},{12,8},{14,10},{1,5},{3,7},... | collective-permute-start | bytes 1966088 | tf_op jit(solution)/shard_map/ppermute | solution.py:125
  50.3 29.4 %collective-permute-start.4 = (bf16[4,10,32,512]{3,2,1,0:T(8,128)(2,1)S(1)}, bf16[4,10,32,512]{3,2,1,0:T(8,128)(2,1)S(1)}, u32[]{:S(2)}, u32[]{:S(2)}) collective-permute-start(bf16[4,10,32,512]{3,2,1,0:T(8,128)(2,1)S(1)} %join.5.refs_0_), channel_id=1, source_target_pairs={{0,2},{2,0},{4,6},{6,4},{8,10},{10,8},{12,14},{14,12},{1,3},{3,1},... | collective-permute-start | bytes 3932168 | tf_op jit(solution)/shard_map/ppermute | solution.py:129
  52.2 19.4 %collective-permute-start.8 = (bf16[2,2,96,512]{3,2,1,0:T(8,128)(2,1)S(1)}, bf16[2,2,96,512]{3,2,1,0:T(8,128)(2,1)S(1)}, u32[]{:S(2)}, u32[]{:S(2)}) collective-permute-start(bf16[2,2,96,512]{3,2,1,0:T(8,128)(2,1)S(1)} %get-tuple-element.39.refs_0_), channel_id=1, source_target_pairs={{0,4},{2,6},{4,0},{6,2},{8,12},{10,14},{12,8},{14,10},{1,5},{3,7},... | collective-permute-start | bytes 1179656 | tf_op jit(solution)/shard_map/ppermute | solution.py:125
  54.5 23.1 %collective-permute-start.7 = (bf16[2,2,96,512]{3,2,1,0:T(8,128)(2,1)S(1)}, bf16[2,2,96,512]{3,2,1,0:T(8,128)(2,1)S(1)}, u32[]{:S(2)}, u32[]{:S(2)}) collective-permute-start(bf16[2,2,96,512]{3,2,1,0:T(8,128)(2,1)S(1)} %get-tuple-element.40.refs_0_), channel_id=1, source_target_pairs={{0,4},{2,6},{4,0},{6,2},{8,12},{10,14},{12,8},{14,10},{1,5},{3,7},... | collective-permute-start | bytes 1179656 | tf_op jit(solution)/shard_map/ppermute | solution.py:125
  54.5 23.1 %collective-permute-start.6 = (bf16[1,10,32,512]{3,2,1,0:T(8,128)(2,1)S(1)}, bf16[1,10,32,512]{3,2,1,0:T(8,128)(2,1)S(1)}, u32[]{:S(2)}, u32[]{:S(2)}) collective-permute-start(bf16[1,10,32,512]{3,2,1,0:T(8,128)(2,1)S(1)} %own_weights.3.refs_0_.left), channel_id=1, source_target_pairs={{0,8},{2,10},{4,12},{6,14},{8,0},{10,2},{12,4},{14,6},{1,9},{3,11}... | collective-permute-start | bytes 983048 | tf_op jit(solution)/shard_map/ppermute | solution.py:125
  55.1 65.3 %collective-permute-start.5 = (bf16[4,10,32,512]{3,2,1,0:T(8,128)(2,1)S(1)}, bf16[4,10,32,512]{3,2,1,0:T(8,128)(2,1)S(1)}, u32[]{:S(2)}, u32[]{:S(2)}) collective-permute-start(bf16[4,10,32,512]{3,2,1,0:T(8,128)(2,1)S(1)} %join.5.refs_0_), channel_id=1, source_target_pairs={{0,1},{1,0},{2,3},{3,2},{4,5},{5,4},{6,7},{7,6},{8,9},{9,8},{10,11... | collective-permute-start | bytes 3932168 | tf_op jit(solution)/shard_map/ppermute | solution.py:133
  79.7 18.2 %copy-start.1 = (bf16[4,10,32,512]{3,2,1,0:T(8,128)(2,1)}, bf16[4,10,32,512]{3,2,1,0:T(8,128)(2,1)S(1)}, u32[]{:S(2)}) copy-start(bf16[4,10,32,512]{3,2,1,0:T(8,128)(2,1)S(1)} %collective-permute-done.4.source.refs_0_.refs_1_) | copy-start | bytes 3932164
  79.8 42.1 %copy-start.3 = (s32[8,8]{1,0:T(8,128)S(1)}, s32[8,8]{1,0:T(8,128)}, u32[]{:S(2)}) copy-start(s32[8,8]{1,0:T(8,128)} %pattern.13) | copy-start | bytes 772
  79.8 40.6 %collective-permute-start.9 = (bf16[4,10,32,512]{3,2,1,0:T(8,128)(2,1)S(1)}, bf16[4,10,32,512]{3,2,1,0:T(8,128)(2,1)S(1)}, u32[]{:S(2)}, u32[]{:S(2)}) collective-permute-start(bf16[4,10,32,512]{3,2,1,0:T(8,128)(2,1)S(1)} %hold.1), channel_id=1, source_target_pairs={{0,1},{1,0},{2,3},{3,2},{4,5},{5,4},{6,7},{7,6},{8,9},{9,8},{10,11... | collective-permute-start | bytes 3932168 | tf_op jit(solution)/shard_map/ppermute | solution.py:133
  79.9 18.0 %collective-permute-start.12 = (bf16[2,10,32,512]{3,2,1,0:T(8,128)(2,1)S(1)}, bf16[2,10,32,512]{3,2,1,0:T(8,128)(2,1)S(1)}, u32[]{:S(2)}, u32[]{:S(2)}) collective-permute-start(bf16[2,10,32,512]{3,2,1,0:T(8,128)(2,1)S(1)} %join.6.refs_0_.left), channel_id=1, source_target_pairs={{0,4},{2,6},{4,0},{6,2},{8,12},{10,14},{12,8},{14,10},{1,5},{3,7},... | collective-permute-start | bytes 1966088 | tf_op jit(solution)/shard_map/ppermute | solution.py:125
  99.0 47.0 %collective-permute-start.13 = (bf16[4,10,32,512]{3,2,1,0:T(8,128)(2,1)}, bf16[4,10,32,512]{3,2,1,0:T(8,128)(2,1)S(1)}, u32[]{:S(2)}, u32[]{:S(2)}) collective-permute-start(bf16[4,10,32,512]{3,2,1,0:T(8,128)(2,1)} %join.7.refs_8_.refs_0_), channel_id=1, source_target_pairs={{0,2},{2,0},{4,6},{6,4},{8,10},{10,8},{12,14},{14,12},{1,3},{3,1},... | collective-permute-start | bytes 3932168 | tf_op jit(solution)/shard_map/ppermute | solution.py:129
  100.5 16.9 %collective-permute-start.11 = (bf16[2,96,512]{2,1,0:T(8,128)(2,1)S(1)}, bf16[2,96,512]{2,1,0:T(8,128)(2,1)S(1)}, u32[]{:S(2)}, u32[]{:S(2)}) collective-permute-start(bf16[2,96,512]{2,1,0:T(8,128)(2,1)S(1)} %get-tuple-element.44.refs_0_), channel_id=1, source_target_pairs={{0,8},{2,10},{4,12},{6,14},{8,0},{10,2},{12,4},{14,6},{1,9},{3,11}... | collective-permute-start | bytes 589832 | tf_op jit(solution)/shard_map/ppermute | solution.py:125
  100.9 19.5 %collective-permute-start.10 = (bf16[2,96,512]{2,1,0:T(8,128)(2,1)S(1)}, bf16[2,96,512]{2,1,0:T(8,128)(2,1)S(1)}, u32[]{:S(2)}, u32[]{:S(2)}) collective-permute-start(bf16[2,96,512]{2,1,0:T(8,128)(2,1)S(1)} %get-tuple-element.43.refs_0_), channel_id=1, source_target_pairs={{0,8},{2,10},{4,12},{6,14},{8,0},{10,2},{12,4},{14,6},{1,9},{3,11}... | collective-permute-start | bytes 589832 | tf_op jit(solution)/shard_map/ppermute | solution.py:125
  144.9 20.5 %collective-permute-start.19 = (bf16[2,384,512]{2,1,0:T(8,128)(2,1)S(1)}, bf16[2,384,512]{2,1,0:T(8,128)(2,1)S(1)}, u32[]{:S(2)}, u32[]{:S(2)}) collective-permute-start(bf16[2,384,512]{2,1,0:T(8,128)(2,1)S(1)} %get-tuple-element.54), channel_id=1, source_target_pairs={{0,2},{2,0},{4,6},{6,4},{8,10},{10,8},{12,14},{14,12},{1,3},{3,1},... | collective-permute-start | bytes 2359304 | tf_op jit(solution)/shard_map/ppermute | solution.py:129
  146.1 44.0 %collective-permute-start.14 = (bf16[4,10,32,512]{3,2,1,0:T(8,128)(2,1)}, bf16[4,10,32,512]{3,2,1,0:T(8,128)(2,1)S(1)}, u32[]{:S(2)}, u32[]{:S(2)}) collective-permute-start(bf16[4,10,32,512]{3,2,1,0:T(8,128)(2,1)} %join.7.refs_8_.refs_0_), channel_id=1, source_target_pairs={{0,1},{1,0},{2,3},{3,2},{4,5},{5,4},{6,7},{7,6},{8,9},{9,8},{10,11... | collective-permute-start | bytes 3932168 | tf_op jit(solution)/shard_map/ppermute | solution.py:133
  146.1 44.0 %collective-permute-start.15 = (bf16[4,10,32,512]{3,2,1,0:T(8,128)(2,1)S(1)}, bf16[4,10,32,512]{3,2,1,0:T(8,128)(2,1)S(1)}, u32[]{:S(2)}, u32[]{:S(2)}) collective-permute-start(bf16[4,10,32,512]{3,2,1,0:T(8,128)(2,1)S(1)} %collective-permute-done.13.refs_1_), channel_id=1, source_target_pairs={{0,1},{1,0},{2,3},{3,2},{4,5},{5,4},{6,7},{7,6},{8,9},{9,8},{10,11... | collective-permute-start | bytes 3932168 | tf_op jit(solution)/shard_map/ppermute | solution.py:133
  149.4 24.4 %collective-permute-start.22 = (bf16[1,384,512]{2,1,0:T(8,128)(2,1)S(1)}, bf16[1,384,512]{2,1,0:T(8,128)(2,1)S(1)}, u32[]{:S(2)}, u32[]{:S(2)}) collective-permute-start(bf16[1,384,512]{2,1,0:T(8,128)(2,1)S(1)} %get-tuple-element.60), channel_id=1, source_target_pairs={{0,2},{2,0},{4,6},{6,4},{8,10},{10,8},{12,14},{14,12},{1,3},{3,1},... | collective-permute-start | bytes 1179656 | tf_op jit(solution)/shard_map/ppermute | solution.py:129
  153.3 26.4 %collective-permute-start.16 = (bf16[1,384,512]{2,1,0:T(8,128)(2,1)S(1)}, bf16[1,384,512]{2,1,0:T(8,128)(2,1)S(1)}, u32[]{:S(2)}, u32[]{:S(2)}) collective-permute-start(bf16[1,384,512]{2,1,0:T(8,128)(2,1)S(1)} %get-tuple-element.48), channel_id=1, source_target_pairs={{0,2},{2,0},{4,6},{6,4},{8,10},{10,8},{12,14},{14,12},{1,3},{3,1},... | collective-permute-start | bytes 1179656 | tf_op jit(solution)/shard_map/ppermute | solution.py:129
  166.1 15.1 %collective-permute-start.20 = (bf16[2,2,96,512]{3,2,1,0:T(8,128)(2,1)S(1)}, bf16[2,2,96,512]{3,2,1,0:T(8,128)(2,1)S(1)}, u32[]{:S(2)}, u32[]{:S(2)}) collective-permute-start(bf16[2,2,96,512]{3,2,1,0:T(8,128)(2,1)S(1)} %get-tuple-element.56), channel_id=1, source_target_pairs={{0,4},{2,6},{4,0},{6,2},{8,12},{10,14},{12,8},{14,10},{1,5},{3,7},... | collective-permute-start | bytes 1179656 | tf_op jit(solution)/shard_map/ppermute | solution.py:125
  174.5 8.7 %collective-permute-start.23 = (bf16[2,1,96,512]{3,2,1,0:T(8,128)(2,1)S(1)}, bf16[2,1,96,512]{3,2,1,0:T(8,128)(2,1)S(1)}, u32[]{:S(2)}, u32[]{:S(2)}) collective-permute-start(bf16[2,1,96,512]{3,2,1,0:T(8,128)(2,1)S(1)} %get-tuple-element.62), channel_id=1, source_target_pairs={{0,4},{2,6},{4,0},{6,2},{8,12},{10,14},{12,8},{14,10},{1,5},{3,7},... | collective-permute-start | bytes 589832 | tf_op jit(solution)/shard_map/ppermute | solution.py:125
  180.3 8.5 %collective-permute-start.17 = (bf16[2,1,96,512]{3,2,1,0:T(8,128)(2,1)S(1)}, bf16[2,1,96,512]{3,2,1,0:T(8,128)(2,1)S(1)}, u32[]{:S(2)}, u32[]{:S(2)}) collective-permute-start(bf16[2,1,96,512]{3,2,1,0:T(8,128)(2,1)S(1)} %get-tuple-element.50), channel_id=1, source_target_pairs={{0,4},{2,6},{4,0},{6,2},{8,12},{10,14},{12,8},{14,10},{1,5},{3,7},... | collective-permute-start | bytes 589832 | tf_op jit(solution)/shard_map/ppermute | solution.py:125
  181.3 15.6 %collective-permute-start.21 = (bf16[2,96,512]{2,1,0:T(8,128)(2,1)S(1)}, bf16[2,96,512]{2,1,0:T(8,128)(2,1)S(1)}, u32[]{:S(2)}, u32[]{:S(2)}) collective-permute-start(bf16[2,96,512]{2,1,0:T(8,128)(2,1)S(1)} %get-tuple-element.58), channel_id=1, source_target_pairs={{0,8},{2,10},{4,12},{6,14},{8,0},{10,2},{12,4},{14,6},{1,9},{3,11}... | collective-permute-start | bytes 589832 | tf_op jit(solution)/shard_map/ppermute | solution.py:125
  183.2 16.6 %collective-permute-start.24 = (bf16[1,96,512]{2,1,0:T(8,128)(2,1)S(1)}, bf16[1,96,512]{2,1,0:T(8,128)(2,1)S(1)}, u32[]{:S(2)}, u32[]{:S(2)}) collective-permute-start(bf16[1,96,512]{2,1,0:T(8,128)(2,1)S(1)} %get-tuple-element.64), channel_id=1, source_target_pairs={{0,8},{2,10},{4,12},{6,14},{8,0},{10,2},{12,4},{14,6},{1,9},{3,11}... | collective-permute-start | bytes 294920 | tf_op jit(solution)/shard_map/ppermute | solution.py:125
  188.8 13.8 %collective-permute-start.18 = (bf16[1,96,512]{2,1,0:T(8,128)(2,1)S(1)}, bf16[1,96,512]{2,1,0:T(8,128)(2,1)S(1)}, u32[]{:S(2)}, u32[]{:S(2)}) collective-permute-start(bf16[1,96,512]{2,1,0:T(8,128)(2,1)S(1)} %get-tuple-element.52), channel_id=1, source_target_pairs={{0,8},{2,10},{4,12},{6,14},{8,0},{10,2},{12,4},{14,6},{1,9},{3,11}... | collective-permute-start | bytes 294920 | tf_op jit(solution)/shard_map/ppermute | solution.py:125
  190.1 6.9 %copy-start.6 = (bf16[4,10,32,512]{3,2,1,0:T(8,128)(2,1)}, bf16[4,10,32,512]{3,2,1,0:T(8,128)(2,1)S(1)}, u32[]{:S(2)}) copy-start(bf16[4,10,32,512]{3,2,1,0:T(8,128)(2,1)S(1)} %collective-permute-done.14.refs_2_) | copy-start | bytes 3932164
  190.1 6.9 %copy-start.7 = (bf16[4,10,32,512]{3,2,1,0:T(8,128)(2,1)}, bf16[4,10,32,512]{3,2,1,0:T(8,128)(2,1)S(1)}, u32[]{:S(2)}) copy-start(bf16[4,10,32,512]{3,2,1,0:T(8,128)(2,1)S(1)} %collective-permute-done.15.refs_3_) | copy-start | bytes 3932164
  (3 other events, 8.2 us)

commit v3 on v2

--- a/solution.py
+++ b/solution.py
@@ -29,8 +29,8 @@
 
 
 def weights_kernel(stages, meta, window_ref, diag_ref, *refs):
-    outs, (turned, sems) = refs[-2 - len(stages) : -2], refs[-2:]
-    half, rows = outs[0].shape[2], window_ref.shape[2]
+    out, turned, sems = refs[-3:]
+    half, rows = out.shape[2], window_ref.shape[2]
     start = pl.multiple_of(meta[2] * half, half)
     copies = []
 
@@ -39,11 +39,8 @@
         copy.start()
         copies.append(copy)
 
-    blocks = [
-        (out.at[0, place], j, k)
-        for out, columns in zip(outs, stages)
-        for place, (j, k) in enumerate(stage_blocks(columns))
-    ]
+    pairs = [pair for columns in stages for pair in stage_blocks(columns)]
+    blocks = [(out.at[0, place], j, k) for place, (j, k) in enumerate(pairs)]
     for target, j, k in blocks:
         if j != k:
             move(window_ref.at[j, k, pl.ds(start, half)], target)
@@ -60,11 +57,11 @@
         copy.wait()
 
 
-def own_weights(meta, window_blocks, diag_inverse, columns, after):
+def own_weights(meta, window_blocks, diag_inverse, stages, after):
     count, super_size, rows = diag_inverse.shape
-    blocks = len(stage_blocks(columns))
-    return pl.pallas_call(
-        functools.partial(weights_kernel, (columns,)),
+    blocks = sum(len(stage_blocks(columns)) for columns in stages)
+    return pl.pallas_call(
+        functools.partial(weights_kernel, stages),
         out_shape=jax.ShapeDtypeStruct((1, blocks, rows // 2, super_size), BF16),
         in_specs=[SMEM_SPEC, ANY_SPEC, VMEM_SPEC] + [ANY_SPEC] * len(after),
         out_specs=ANY_SPEC,
@@ -77,11 +74,11 @@
     )(meta, window_blocks, diag_inverse, *after)
 
 
-def join_kernel(left, right, *refs):
+def join_kernel(first, left, right, *refs):
     out, sems = refs[-2:]
-    half = out.shape[0] // 2
+    half, here = out.shape[0] // 2, pl.ds(first, out.shape[1])
     copies = [
-        pltpu.make_async_copy(source, out.at[pl.ds(i * half, half)], sems.at[i])
+        pltpu.make_async_copy(source.at[:, here], out.at[pl.ds(i * half, half)], sems.at[i])
         for i, source in enumerate((left, right))
     ]
     for copy in copies:
@@ -90,10 +87,12 @@
         copy.wait()
 
 
-def join(left, right, after):
-    return pl.pallas_call(
-        join_kernel,
-        out_shape=jax.ShapeDtypeStruct((2 * left.shape[0], *left.shape[1:]), left.dtype),
+def join(left, right, after, first=0, count=None):
+    count = left.shape[1] if count is None else count
+    shape = (2 * left.shape[0], count, *left.shape[2:])
+    return pl.pallas_call(
+        functools.partial(join_kernel, first),
+        out_shape=jax.ShapeDtypeStruct(shape, left.dtype),
         in_specs=[ANY_SPEC] * (2 + len(after)),
         out_specs=ANY_SPEC,
         scratch_shapes=[pltpu.SemaphoreType.DMA((2,))],
@@ -320,8 +319,8 @@
     )(mine, got, *after)
 
 
-def solve_kernel(columns, ready, groups, whole, first, meta, pattern, *refs):
-    weights, refs = refs[:4], refs[4:]
+def solve_kernel(columns, ready, groups, whole, first, origins, meta, pattern, *refs):
+    weights, refs = refs[: len(origins)], refs[len(origins) :]
     count = 2 * len(groups)
     parts, solved = refs[:count], refs[count : count + len(ready)]
     out, slab, sems = refs[-3:]
@@ -332,14 +331,14 @@
     cuts = [(0, starts[1]), (starts[1], starts[-1])] if len(starts) > 2 else [(0, starts[1])]
     copies = {}
     for cut, (low, high) in enumerate(cuts):
-        for which, source in enumerate(weights):
-            for e, d in enumerate((0, 2, 1, 3)):
-                x = meta[1] if which % 2 == 0 else 1 - meta[1]
-                t = meta[2] if which < 2 else 1 - meta[2]
+        for which, (source, (flip_x, flip_core, distances)) in enumerate(zip(weights, origins)):
+            for e, d in enumerate(distances):
+                x = 1 - meta[1] if flip_x else meta[1]
+                t = 1 - meta[2] if flip_core else meta[2]
                 copy = pltpu.make_async_copy(
                     source.at[e, pl.ds(first + low, high - low)],
                     slab.at[pl.ds(low, high - low), (meta[4 + d] * 2 + x) * 2 + t],
-                    sems.at[cut, 4 * which + e],
+                    sems.at[cut, len(distances) * which + e],
                 )
                 copy.start()
                 copies.setdefault(low, []).append(copy)
@@ -383,7 +382,8 @@
 def solve(
     meta, pattern, weights, columns, ready, solved, groups, parts, whole, owners, after=()
 ):
-    _, _, rows, super_size = weights[0].shape
+    arrays, origins = zip(*weights)
+    _, _, rows, super_size = arrays[0].shape
     piece = parts[0][0].shape[1]
     before, n = sum(len(g) for g in ready), sum(len(g) for g in groups)
     first, count = before * (before + 1) // 2, n * before + n * (n + 1) // 2
@@ -393,10 +393,10 @@
         shape = (n, piece, super_size)
     flat = [p for part in parts for p in part]
     return pl.pallas_call(
-        functools.partial(solve_kernel, columns, ready, groups, whole, first),
+        functools.partial(solve_kernel, columns, ready, groups, whole, first, origins),
         out_shape=jax.ShapeDtypeStruct(shape, BF16),
         in_specs=[SMEM_SPEC] * 2
-        + [ANY_SPEC] * 4
+        + [ANY_SPEC] * len(arrays)
         + [VMEM_SPEC] * (len(flat) + len(solved))
         + [ANY_SPEC] * len(after),
         out_specs=VMEM_SPEC,
@@ -406,7 +406,7 @@
         ],
         compiler_params=params(),
         name="solve",
-    )(meta, pattern, *weights, *flat, *solved, *after)
+    )(meta, pattern, *arrays, *flat, *solved, *after)
 
 
 def place_kernel(stages, *refs):
@@ -455,19 +455,17 @@
     outer = functools.partial(
         outer_terms, meta, outer_row, outer_col, known, right_side, outer_blocks
     )
-    weigh = functools.partial(own_weights, meta, window_blocks, diag_inverse)
-    own_0 = weigh(first, ())
-    opposite_0 = z_move(own_0, 2, owners)
-    send_a, keep_a = outer(CHUNKS[0][0], True, (own_0,))
+    count_0, count_1 = len(stage_blocks(first)), len(stage_blocks(last))
+    own_rows = own_weights(meta, window_blocks, diag_inverse, STAGES, ())
+    opposite = z_move(own_rows, 2, owners)
+    send_a, keep_a = outer(CHUNKS[0][0], True, (own_rows,))
     got_a = x_move(send_a, owners)
     send_b, keep_b = outer(CHUNKS[0][1], True, (send_a,))
     got_b = x_move(send_b, owners)
     (base,) = outer(last, False, (send_b,))
-    near_0 = join(own_0, opposite_0, (base,))
+    near_0 = join(own_rows, opposite, (base,), 0, count_0)
     far_0 = z_move(near_0, 1, owners)
-    own_1 = weigh(last, (near_0,))
-    opposite_1 = z_move(own_1, 2, owners)
-    line_a, mine_a = pair_sum(meta, keep_a, got_a, owners, (own_1,))
+    line_a, mine_a = pair_sum(meta, keep_a, got_a, owners, (near_0,))
     across_a = z_move(line_a, 1, owners)
     line_b, mine_b = pair_sum(meta, keep_b, got_b, owners, (line_a,))
     across_b = z_move(line_b, 1, owners)
@@ -477,11 +475,17 @@
     last_a = z_move(end_a, 2, owners)
     end_b, total_b = line_sum(mine_b, across_b, (end_a,))
     last_b = z_move(end_b, 2, owners)
-    near_1 = join(own_1, opposite_1, (end_b,))
+    near_1 = join(own_rows, opposite, (last_b,), count_0, count_1)
     far_1 = z_move(near_1, 1, owners)
-    line_1 = join(near_1, far_1, (beside_0,))
-    beside_1 = x_move(line_1, owners)
-    weights = [line_0, beside_0, *other_core([line_0, hold(beside_0, (near_1,))])]
+    x_near_1 = x_move(near_1, owners)
+    core_line, core_beside = other_core([line_0, hold(beside_0, (end_b, last_a))])
+    line = (0, 2, 1, 3)
+    weights = [
+        (line_0, (False, False, line)),
+        (beside_0, (True, False, line)),
+        (core_line, (False, True, line)),
+        (core_beside, (True, True, line)),
+    ]
     done = solve(
         meta,
         window_pattern,
@@ -493,38 +497,32 @@
         ((total_a, last_a), (total_b, last_b)),
         True,
         owners,
-        (line_1,),
+        (near_1,),
     )
+    x_far_1 = x_move(hold(far_1, (x_near_1,)), owners)
     rows_0 = lax.all_to_all(done, "own", 0, 0, tiled=True)
     moved, at = [], 0
     for chunk in CHUNKS[1]:
         send, keep = cross_terms(
-            meta, window_pattern, base, window_blocks, (rows_0,), chunk, at, (first,), ()
+            meta, window_pattern, base, window_blocks, (rows_0,), chunk, at, (first,), (x_far_1,) if at else (x_near_1,)
         )
         moved.append((keep, x_move(send, owners)))
         at += len(chunk)
-    parts, after = [], ()
-    for keep, got in moved:
-        line, mine = pair_sum(meta, keep, got, owners, after)
-        end, total = line_sum(mine, z_move(line, 1, owners), ())
+    parts, ends = [], []
+    for index, (keep, got) in enumerate(moved):
+        part, kept = pair_sum(meta, keep, got, owners, ends[: max(index - 1, 0)])
+        before = [moved_end for _, moved_end in parts[: max(index - 1, 0)]]
+        end, total = line_sum(kept, z_move(part, 1, owners), before)
+        ends.append(end)
         parts.append((total, z_move(end, 2, owners)))
-    weights = [line_1, beside_1, *other_core([line_1, beside_1])]
-    solved = []
-    for index, chunk in enumerate(CHUNKS[1]):
-        out = solve(
-            meta,
-            window_pattern,
-            weights,
-            last,
-            CHUNKS[1][:index],
-            solved,
-            (chunk,),
-            parts[index : index + 1],
-            index == len(CHUNKS[1]) - 1,
-            owners,
-        )
-        solved.append(out)
-    rows_1 = lax.all_to_all(solved[-1], "own", 0, 0, tiled=True)
+    mine = [join(near_1, far_1, moved[0][:1]), join(x_near_1, x_far_1, moved[-1][:1])]
+    weights = [
+        (array, (i % 2 > 0, i > 1, line)) for i, array in enumerate(mine + other_core(mine))
+    ]
+    solve_last = functools.partial(solve, meta, window_pattern, weights, last)
+    half = solve_last((), (), CHUNKS[1][:1], parts[:1], False, owners)
+    done = solve_last(CHUNKS[1][:1], (half,), CHUNKS[1][1:], parts[1:], True, owners)
+    rows_1 = lax.all_to_all(done, "own", 0, 0, tiled=True)
     return place_rows([rows_0, rows_1], STAGES, right_side.shape[0], right_side.shape[1])
 
 

time: 221 us -> 204 us (0.923)
  waiting for transfers between devices: 101 us -> 87.1 us
  blocking collectives: 28.6 us -> 15.1 us
  starting transfers between devices: 31.2 us -> 38.7 us
  local copies, waits for them, and re-layouts: 3.09 us -> 6.53 us
    ppermute x14 -> x13, waiting for transfers between devices: 65.9 us -> 37.9 us  [z_move(): return lax.ppermute(part, 'own', [(o, o ^ 2 * d) for o in range(owners)])]
    all_to_all x2 -> x1, blocking collectives: 28.6 us -> 15.1 us  [staged_body(): rows_1 = lax.all_to_all(done, 'own', 0, 0, tiled=True)]
    ppermute x7 -> x8, waiting for transfers between devices: 35.4 us -> 44.7 us  [x_move(): return lax.ppermute(part, 'own', [(o, o ^ 1) for o in range(owners)])]
    all_to_all x0 -> x1, starting transfers between devices: none -> 4.67 us  [staged_body(): rows_0 = lax.all_to_all(done, 'own', 0, 0, tiled=True)]
    all_to_all x0 -> x1, waiting for transfers between devices: none -> 4.52 us  [staged_body(): rows_0 = lax.all_to_all(done, 'own', 0, 0, tiled=True)]
    ppermute x14 -> x13, starting transfers between devices: 22 us -> 26.3 us  [z_move(): return lax.ppermute(part, 'own', [(o, o ^ 2 * d) for o in range(owners)])]
    unnamed x21 -> x23, local copies, waits for them, and re-layouts: 3 us -> 6.44 us
    ppermute x7 -> x8, starting transfers between devices: 8.65 us -> 7.11 us  [x_move(): return lax.ppermute(part, 'own', [(o, o ^ 1) for o in range(owners)])]
  transfers between devices with their start and end apart: 25 -> 26, of which waited for: 12 -> 16; matrix products, arithmetic and copies ran while one was open for 0% -> 0% of each run, Pallas kernels for 23% -> 24%
where the time goes in v3:
time: 204 us
  waiting for transfers between devices  87.1 us (43%)
  Pallas kernels  55.8 us (27%)
  starting transfers between devices  38.7 us (19%)
  blocking collectives  15.1 us (7%)
  local copies, waits for them, and re-layouts  6.53 us (3%)
    ppermute x8, waiting for transfers between devices, x_move(): return lax.ppermute(part, 'own', [(o, o ^ 1) for o in range(owners)])  44.7 us
    ppermute x13, waiting for transfers between devices, z_move(): return lax.ppermute(part, 'own', [(o, o ^ 2 * d) for o in range(owners)])  37.9 us
    ppermute x13, starting transfers between devices, z_move(): return lax.ppermute(part, 'own', [(o, o ^ 2 * d) for o in range(owners)])  26.3 us
    pallas_call x3, Pallas kernels, outer_terms(): pl.pallas_call(functools.partial(outer_kernel, columns, split), out_shape...  23.4 us
    all_to_all x1, blocking collectives, staged_body(): rows_1 = lax.all_to_all(done, 'own', 0, 0, tiled=True)  15.1 us
    pallas_call x3, Pallas kernels, solve(): pl.pallas_call(functools.partial(solve_kernel, columns, ready, groups, wh...  12.3 us
    pallas_call x3, Pallas kernels, cross_terms(): pl.pallas_call(functools.partial(cross_kernel, chunk, offset, before), ou...  9.46 us
    ppermute x8, starting transfers between devices, x_move(): return lax.ppermute(part, 'own', [(o, o ^ 1) for o in range(owners)])  7.11 us
  transfers between devices with their start and end apart: 26, of which 16 were waited for; matrix products, arithmetic and copies ran while one was open for 0% of the time, Pallas kernels for 24%

profile of v3, /device:TPU:0, one launch (start us, length us, event | category | flops | bytes accessed | tf_op | source)
XLA Modules:
  0.0 203.5 jit_solution(5872351120824149988)
XLA Ops:
  1.6 2.2 %own_weights.1.refs_0_.left = bf16[1,20,32,512]{3,2,1,0:T(8,128)(2,1)S(1)} custom-call(s32[8]{0:T(128)S(1)} %stack.32.meta, bf16[8,8,64,512]{3,2,1,0:T(8,128)(2,1)} %window.5, bf16[8,512,64]{2,1,0:T(8,128)(2,1)S(1)} %copy.9.diag_ref), custom_call_target="tpu_custom_call" | custom-call | tf_op jit(solution)/shard_map/own_weights/pallas_call | solution.py:63
  3.9 4.1 %collective-permute-start = (bf16[1,20,32,512]{3,2,1,0:T(8,128)(2,1)S(1)}, bf16[1,20,32,512]{3,2,1,0:T(8,128)(2,1)S(1)}, u32[]{:S(2)}, u32[]{:S(2)}) collective-permute-start(bf16[1,20,32,512]{3,2,1,0:T(8,128)(2,1)S(1)} %own_weights.1.refs_0_.left), channel_id=1, source_target_pairs={{0,8},{2,10},{4,12},{6,14},{8,0},{10,2},{12,4},{14,6},{1,9},{3,11}... | collective-permute-start | bytes 1966088 | tf_op jit(solution)/shard_map/ppermute | solution.py:124
  8.0 6.6 %outer_terms.3 = (bf16[2,384,512]{2,1,0:T(8,128)(2,1)S(1)}, f32[2,384,512]{2,1,0:T(8,128)S(1)}) custom-call(s32[8]{0:T(128)S(1)} %stack.32.meta, s32[16]{0:T(128)S(1)} %copy-done.7, s32[16]{0:T(128)S(1)} %copy-done.8, bf16[2,512,768]{2,1,0:T(8,128)(2,1)} %known.5, bf16[8,64,768]{2,1,0:T(8,128)(2,1)S(1)} %copy-done.1, bf16[16,512,512]{2,1,0:T(8,128)(2,1)} %blocks.5, ...), custom_call_target="tpu_custom_call" | custom-call | tf_op jit(solution)/shard_map/outer_terms/pallas_call | solution.py:199
  15.8 2.1 %collective-permute-start.3 = (bf16[2,384,512]{2,1,0:T(8,128)(2,1)S(1)}, bf16[2,384,512]{2,1,0:T(8,128)(2,1)S(1)}, u32[]{:S(2)}, u32[]{:S(2)}) collective-permute-start(bf16[2,384,512]{2,1,0:T(8,128)(2,1)S(1)} %get-tuple-element.35.refs_0_), channel_id=1, source_target_pairs={{0,2},{2,0},{4,6},{6,4},{8,10},{10,8},{12,14},{14,12},{1,3},{3,1},... | collective-permute-start | bytes 2359304 | tf_op jit(solution)/shard_map/ppermute | solution.py:128
  17.8 7.0 %outer_terms.4 = (bf16[2,384,512]{2,1,0:T(8,128)(2,1)S(1)}, f32[2,384,512]{2,1,0:T(8,128)S(1)}) custom-call(s32[8]{0:T(128)S(1)} %stack.32.meta, s32[16]{0:T(128)S(1)} %copy-done.7, s32[16]{0:T(128)S(1)} %copy-done.8, bf16[2,512,768]{2,1,0:T(8,128)(2,1)} %known.5, bf16[8,64,768]{2,1,0:T(8,128)(2,1)S(1)} %copy-done.1, bf16[16,512,512]{2,1,0:T(8,128)(2,1)} %blocks.5, ...), custom_call_target="tpu_custom_call" | custom-call | tf_op jit(solution)/shard_map/outer_terms/pallas_call | solution.py:199
  24.9 9.9 %outer_terms.5.refs_0_.base = f32[4,768,512]{2,1,0:T(8,128)} custom-call(s32[8]{0:T(128)S(1)} %stack.32.meta, s32[16]{0:T(128)S(1)} %copy-done.7, s32[16]{0:T(128)S(1)} %copy-done.8, bf16[2,512,768]{2,1,0:T(8,128)(2,1)S(1)} %copy-done, bf16[8,64,768]{2,1,0:T(8,128)(2,1)S(1)} %copy-done.1, bf16[16,512,512]{2,1,0:T(8,128)(2,1)} %blocks.5, ...), custom_call_target="tpu_custom_call" | custom-call | tf_op jit(solution)/shard_map/outer_terms/pallas_call | solution.py:199
  40.4 11.6 %collective-permute-done.2.got = bf16[2,384,512]{2,1,0:T(8,128)(2,1)S(1)} collective-permute-done((bf16[2,384,512]{2,1,0:T(8,128)(2,1)S(1)}, bf16[2,384,512]{2,1,0:T(8,128)(2,1)S(1)}, u32[]{:S(2)}, u32[]{:S(2)}) %collective-permute-start.2) | collective-permute-done | bytes 786464 | tf_op jit(solution)/shard_map/ppermute | solution.py:128
  57.0 10.0 %collective-permute-done.7.got = bf16[2,2,96,512]{3,2,1,0:T(8,128)(2,1)S(1)} collective-permute-done((bf16[2,2,96,512]{3,2,1,0:T(8,128)(2,1)S(1)}, bf16[2,2,96,512]{3,2,1,0:T(8,128)(2,1)S(1)}, u32[]{:S(2)}, u32[]{:S(2)}) %collective-permute-start.7) | collective-permute-done | bytes 393248 | tf_op jit(solution)/shard_map/ppermute | solution.py:124
  67.1 4.4 %collective-permute-start.8 = (bf16[2,96,512]{2,1,0:T(8,128)(2,1)S(1)}, bf16[2,96,512]{2,1,0:T(8,128)(2,1)S(1)}, u32[]{:S(2)}, u32[]{:S(2)}) collective-permute-start(bf16[2,96,512]{2,1,0:T(8,128)(2,1)S(1)} %get-tuple-element.43.refs_0_), channel_id=1, source_target_pairs={{0,8},{2,10},{4,12},{6,14},{8,0},{10,2},{12,4},{14,6},{1,9},{3,11}... | collective-permute-start | bytes 589832 | tf_op jit(solution)/shard_map/ppermute | solution.py:124
  71.5 5.7 %collective-permute-done.6.got = bf16[2,2,96,512]{3,2,1,0:T(8,128)(2,1)S(1)} collective-permute-done((bf16[2,2,96,512]{3,2,1,0:T(8,128)(2,1)S(1)}, bf16[2,2,96,512]{3,2,1,0:T(8,128)(2,1)S(1)}, u32[]{:S(2)}, u32[]{:S(2)}) %collective-permute-start.6) | collective-permute-done | bytes 393248 | tf_op jit(solution)/shard_map/ppermute | solution.py:124
  77.3 5.4 %collective-permute-done.4.source.refs_1_ = bf16[4,10,32,512]{3,2,1,0:T(8,128)(2,1)S(1)} collective-permute-done((bf16[4,10,32,512]{3,2,1,0:T(8,128)(2,1)S(1)}, bf16[4,10,32,512]{3,2,1,0:T(8,128)(2,1)S(1)}, u32[]{:S(2)}, u32[]{:S(2)}) %collective-permute-start.4) | collective-permute-done | bytes 1310752 | tf_op jit(solution)/shard_map/ppermute | solution.py:128
  83.8 4.0 %collective-permute-start.10 = (bf16[2,96,512]{2,1,0:T(8,128)(2,1)S(1)}, bf16[2,96,512]{2,1,0:T(8,128)(2,1)S(1)}, u32[]{:S(2)}, u32[]{:S(2)}) collective-permute-start(bf16[2,96,512]{2,1,0:T(8,128)(2,1)S(1)} %get-tuple-element.44.refs_0_), channel_id=1, source_target_pairs={{0,8},{2,10},{4,12},{6,14},{8,0},{10,2},{12,4},{14,6},{1,9},{3,11}... | collective-permute-start | bytes 589832 | tf_op jit(solution)/shard_map/ppermute | solution.py:124
  87.8 9.8 %collective-permute-done.10.refs_0_.refs_7_ = bf16[2,96,512]{2,1,0:T(8,128)(2,1)S(1)} collective-permute-done((bf16[2,96,512]{2,1,0:T(8,128)(2,1)S(1)}, bf16[2,96,512]{2,1,0:T(8,128)(2,1)S(1)}, u32[]{:S(2)}, u32[]{:S(2)}) %collective-permute-start.10) | collective-permute-done | bytes 196640 | tf_op jit(solution)/shard_map/ppermute | solution.py:124
  101.7 5.4 %solve.3 = bf16[8,96,256]{2,1,0:T(8,128)(2,1)} custom-call(s32[8]{0:T(128)S(1)} %stack.32.meta, s32[8,8]{1,0:T(8,128)S(1)} %copy-done.6, bf16[4,10,32,512]{3,2,1,0:T(8,128)(2,1)S(1)} %join.6.refs_0_, bf16[4,10,32,512]{3,2,1,0:T(8,128)(2,1)} %copy-done.4, bf16[4,10,32,512]{3,2,1,0:T(8,128)(2,1)} %copy-done.9, bf16[4,10,32,512]{3,2,1,0:T(8,128)(2,1)} %copy-done.10, ...), custom_call_target="tpu_custom_call" | custom-call | tf_op jit(solution)/shard_map/solve/pallas_call | solution.py:395
  107.0 4.7 %all-to-all-start = ((bf16[8,96,256]{2,1,0:T(8,128)(2,1)}), bf16[8,96,256]{2,1,0:T(8,128)(2,1)S(1)}, u32[]{:S(2)}, u32[]{:S(2)}) async-start(bf16[8,96,256]{2,1,0:T(8,128)(2,1)} %solve.3), calls=%async_computation | async-start | bytes 786432 | tf_op jit(solution)/shard_map/all_to_all | solution.py:503
  111.7 3.3 %collective-permute-done.12.refs_1_.refs_0_.left = bf16[2,10,32,512]{3,2,1,0:T(8,128)(2,1)S(1)} collective-permute-done((bf16[2,10,32,512]{3,2,1,0:T(8,128)(2,1)S(1)}, bf16[2,10,32,512]{3,2,1,0:T(8,128)(2,1)S(1)}, u32[]{:S(2)}, u32[]{:S(2)}) %collective-permute-start.12) | collective-permute-done | bytes 655392 | tf_op jit(solution)/shard_map/ppermute | solution.py:128
  115.0 2.9 %collective-permute-done.11.right.source = bf16[2,10,32,512]{3,2,1,0:T(8,128)(2,1)S(1)} collective-permute-done((bf16[2,10,32,512]{3,2,1,0:T(8,128)(2,1)S(1)}, bf16[2,10,32,512]{3,2,1,0:T(8,128)(2,1)S(1)}, u32[]{:S(2)}, u32[]{:S(2)}) %collective-permute-start.11) | collective-permute-done | bytes 655392 | tf_op jit(solution)/shard_map/ppermute | solution.py:124
  118.9 4.5 %all-to-all-done.refs_0_ = bf16[8,96,256]{2,1,0:T(8,128)(2,1)S(1)} async-done(((bf16[8,96,256]{2,1,0:T(8,128)(2,1)}), bf16[8,96,256]{2,1,0:T(8,128)(2,1)S(1)}, u32[]{:S(2)}, u32[]{:S(2)}) %all-to-all-start) | async-done | bytes 393248 | tf_op jit(solution)/shard_map/all_to_all | solution.py:503
  123.4 3.8 %cross_terms.3 = (bf16[2,384,512]{2,1,0:T(8,128)(2,1)S(1)}, f32[2,384,512]{2,1,0:T(8,128)S(1)}) custom-call(s32[8]{0:T(128)S(1)} %stack.32.meta, s32[8,8]{1,0:T(8,128)S(1)} %copy-done.6, f32[4,768,512]{2,1,0:T(8,128)} %outer_terms.5.refs_0_.base, bf16[8,8,64,512]{3,2,1,0:T(8,128)(2,1)} %window.5, bf16[8,96,256]{2,1,0:T(8,128)(2,1)S(1)} %all-to-all-done.refs_0_, ...), custom_call_target="tpu_custom_call" | custom-call | tf_op jit(solution)/shard_map/cross_terms/pallas_call | solution.py:252
  129.4 7.9 %collective-permute-done.13.refs_1_.right = bf16[2,10,32,512]{3,2,1,0:T(8,128)(2,1)S(1)} collective-permute-done((bf16[2,10,32,512]{3,2,1,0:T(8,128)(2,1)}, bf16[2,10,32,512]{3,2,1,0:T(8,128)(2,1)S(1)}, u32[]{:S(2)}, u32[]{:S(2)}) %collective-permute-start.13) | collective-permute-done | bytes 655392 | tf_op jit(solution)/shard_map/ppermute | solution.py:128
  137.3 2.8 %cross_terms.4 = (bf16[1,384,512]{2,1,0:T(8,128)(2,1)S(1)}, f32[1,384,512]{2,1,0:T(8,128)S(1)}) custom-call(s32[8]{0:T(128)S(1)} %stack.32.meta, s32[8,8]{1,0:T(8,128)S(1)} %copy-done.6, f32[4,768,512]{2,1,0:T(8,128)} %outer_terms.5.refs_0_.base, bf16[8,8,64,512]{3,2,1,0:T(8,128)(2,1)} %window.5, bf16[8,96,256]{2,1,0:T(8,128)(2,1)S(1)} %all-to-all-done.refs_0_, ...), custom_call_target="tpu_custom_call" | custom-call | tf_op jit(solution)/shard_map/cross_terms/pallas_call | solution.py:252
  141.6 2.8 %cross_terms.5 = (bf16[1,384,512]{2,1,0:T(8,128)(2,1)S(1)}, f32[1,384,512]{2,1,0:T(8,128)S(1)}) custom-call(s32[8]{0:T(128)S(1)} %stack.32.meta, s32[8,8]{1,0:T(8,128)S(1)} %copy-done.6, f32[4,768,512]{2,1,0:T(8,128)} %outer_terms.5.refs_0_.base, bf16[8,8,64,512]{3,2,1,0:T(8,128)(2,1)} %window.5, bf16[8,96,256]{2,1,0:T(8,128)(2,1)S(1)} %all-to-all-done.refs_0_, ...), custom_call_target="tpu_custom_call" | custom-call | tf_op jit(solution)/shard_map/cross_terms/pallas_call | solution.py:252
  144.6 9.5 %collective-permute-done.20.got = bf16[2,384,512]{2,1,0:T(8,128)(2,1)S(1)} collective-permute-done((bf16[2,384,512]{2,1,0:T(8,128)(2,1)S(1)}, bf16[2,384,512]{2,1,0:T(8,128)(2,1)S(1)}, u32[]{:S(2)}, u32[]{:S(2)}) %collective-permute-start.20) | collective-permute-done | bytes 786464 | tf_op jit(solution)/shard_map/ppermute | solution.py:128
  155.5 7.0 %collective-permute-done.16.got = bf16[1,384,512]{2,1,0:T(8,128)(2,1)S(1)} collective-permute-done((bf16[1,384,512]{2,1,0:T(8,128)(2,1)S(1)}, bf16[1,384,512]{2,1,0:T(8,128)(2,1)S(1)}, u32[]{:S(2)}, u32[]{:S(2)}) %collective-permute-start.16) | collective-permute-done | bytes 393248 | tf_op jit(solution)/shard_map/ppermute | solution.py:128
  163.2 3.5 %collective-permute-done.21.got = bf16[2,2,96,512]{3,2,1,0:T(8,128)(2,1)S(1)} collective-permute-done((bf16[2,2,96,512]{3,2,1,0:T(8,128)(2,1)S(1)}, bf16[2,2,96,512]{3,2,1,0:T(8,128)(2,1)S(1)}, u32[]{:S(2)}, u32[]{:S(2)}) %collective-permute-start.21) | collective-permute-done | bytes 393248 | tf_op jit(solution)/shard_map/ppermute | solution.py:124
  168.6 2.6 %collective-permute-start.22 = (bf16[2,1,96,512]{3,2,1,0:T(8,128)(2,1)S(1)}, bf16[2,1,96,512]{3,2,1,0:T(8,128)(2,1)S(1)}, u32[]{:S(2)}, u32[]{:S(2)}) collective-permute-start(bf16[2,1,96,512]{3,2,1,0:T(8,128)(2,1)S(1)} %get-tuple-element.61), channel_id=1, source_target_pairs={{0,4},{2,6},{4,0},{6,2},{8,12},{10,14},{12,8},{14,10},{1,5},{3,7},... | collective-permute-start | bytes 589832 | tf_op jit(solution)/shard_map/ppermute | solution.py:124
  171.3 2.7 %collective-permute-start.18 = (bf16[1,96,512]{2,1,0:T(8,128)(2,1)S(1)}, bf16[1,96,512]{2,1,0:T(8,128)(2,1)S(1)}, u32[]{:S(2)}, u32[]{:S(2)}) collective-permute-start(bf16[1,96,512]{2,1,0:T(8,128)(2,1)S(1)} %get-tuple-element.54), channel_id=1, source_target_pairs={{0,8},{2,10},{4,12},{6,14},{8,0},{10,2},{12,4},{14,6},{1,9},{3,11}... | collective-permute-start | bytes 294920 | tf_op jit(solution)/shard_map/ppermute | solution.py:124
  174.0 3.2 %collective-permute-done.23.refs_0_.refs_5_ = bf16[2,96,512]{2,1,0:T(8,128)(2,1)S(1)} collective-permute-done((bf16[2,96,512]{2,1,0:T(8,128)(2,1)S(1)}, bf16[2,96,512]{2,1,0:T(8,128)(2,1)S(1)}, u32[]{:S(2)}, u32[]{:S(2)}) %collective-permute-start.23) | collective-permute-done | bytes 196640 | tf_op jit(solution)/shard_map/ppermute | solution.py:124
  177.6 2.7 %collective-permute-start.24 = (bf16[1,96,512]{2,1,0:T(8,128)(2,1)S(1)}, bf16[1,96,512]{2,1,0:T(8,128)(2,1)S(1)}, u32[]{:S(2)}, u32[]{:S(2)}) collective-permute-start(bf16[1,96,512]{2,1,0:T(8,128)(2,1)S(1)} %get-tuple-element.63), channel_id=1, source_target_pairs={{0,8},{2,10},{4,12},{6,14},{8,0},{10,2},{12,4},{14,6},{1,9},{3,11}... | collective-permute-start | bytes 294920 | tf_op jit(solution)/shard_map/ppermute | solution.py:124
  180.3 3.2 %solve.4.refs_8_ = bf16[2,96,512]{2,1,0:T(8,128)(2,1)S(1)} custom-call(s32[8]{0:T(128)S(1)} %stack.32.meta, s32[8,8]{1,0:T(8,128)S(1)} %copy-done.6, bf16[4,10,32,512]{3,2,1,0:T(8,128)(2,1)S(1)} %join.8.refs_0_, bf16[4,10,32,512]{3,2,1,0:T(8,128)(2,1)S(1)} %join.9.refs_1_, bf16[4,10,32,512]{3,2,1,0:T(8,128)(2,1)} %collective-permute-done.14.refs_2_, ...), custom_call_target="tpu_custom_call" | custom-call | tf_op jit(solution)/shard_map/solve/pallas_call | solution.py:395
  183.5 3.7 %solve.5 = bf16[8,96,256]{2,1,0:T(8,128)(2,1)S(1)} custom-call(s32[8]{0:T(128)S(1)} %stack.32.meta, s32[8,8]{1,0:T(8,128)S(1)} %copy-done.6, bf16[4,10,32,512]{3,2,1,0:T(8,128)(2,1)S(1)} %join.8.refs_0_, bf16[4,10,32,512]{3,2,1,0:T(8,128)(2,1)S(1)} %join.9.refs_1_, bf16[4,10,32,512]{3,2,1,0:T(8,128)(2,1)} %collective-permute-done.14.refs_2_, ...), custom_call_target="tpu_custom_call" | custom-call | tf_op jit(solution)/shard_map/solve/pallas_call | solution.py:395
  187.3 15.1 %all_to_all.10.refs_1_ = bf16[8,96,256]{2,1,0:T(8,128)(2,1)S(1)} all-to-all(bf16[8,96,256]{2,1,0:T(8,128)(2,1)S(1)} %solve.5), channel_id=1, replica_groups=mesh['grp'=2,'own'=8,'tile'=2] {'own'}, dimensions={0} | all-to-all | bytes 786432 | tf_op jit(solution)/shard_map/all_to_all | solution.py:525
  (73 shorter events, 29.1 us)
Async XLA Ops:
  1.6 6.4 %copy-start.1 = (bf16[8,64,768]{2,1,0:T(8,128)(2,1)S(1)}, bf16[8,64,768]{2,1,0:T(8,128)(2,1)}, u32[]{:S(2)}) copy-start(bf16[8,64,768]{2,1,0:T(8,128)(2,1)} %draws.5) | copy-start | bytes 2359300
  1.6 6.4 %copy-start.7 = (s32[16]{0:T(128)S(1)}, s32[16]{0:T(128)}, u32[]{:S(2)}) copy-start(s32[16]{0:T(128)} %row_ref.5) | copy-start | bytes 196
  1.6 6.4 %copy-start.8 = (s32[16]{0:T(128)S(1)}, s32[16]{0:T(128)}, u32[]{:S(2)}) copy-start(s32[16]{0:T(128)} %col_ref.5) | copy-start | bytes 196
  3.9 32.9 %collective-permute-start = (bf16[1,20,32,512]{3,2,1,0:T(8,128)(2,1)S(1)}, bf16[1,20,32,512]{3,2,1,0:T(8,128)(2,1)S(1)}, u32[]{:S(2)}, u32[]{:S(2)}) collective-permute-start(bf16[1,20,32,512]{3,2,1,0:T(8,128)(2,1)S(1)} %own_weights.1.refs_0_.left), channel_id=1, source_target_pairs={{0,8},{2,10},{4,12},{6,14},{8,0},{10,2},{12,4},{14,6},{1,9},{3,11}... | collective-permute-start | bytes 1966088 | tf_op jit(solution)/shard_map/ppermute | solution.py:124
  15.8 9.1 %copy-start = (bf16[2,512,768]{2,1,0:T(8,128)(2,1)S(1)}, bf16[2,512,768]{2,1,0:T(8,128)(2,1)}, u32[]{:S(2)}) copy-start(bf16[2,512,768]{2,1,0:T(8,128)(2,1)} %known.5) | copy-start | bytes 4718596
  15.8 23.0 %collective-permute-start.3 = (bf16[2,384,512]{2,1,0:T(8,128)(2,1)S(1)}, bf16[2,384,512]{2,1,0:T(8,128)(2,1)S(1)}, u32[]{:S(2)}, u32[]{:S(2)}) collective-permute-start(bf16[2,384,512]{2,1,0:T(8,128)(2,1)S(1)} %get-tuple-element.35.refs_0_), channel_id=1, source_target_pairs={{0,2},{2,0},{4,6},{6,4},{8,10},{10,8},{12,14},{14,12},{1,3},{3,1},... | collective-permute-start | bytes 2359304 | tf_op jit(solution)/shard_map/ppermute | solution.py:128
  24.8 27.1 %collective-permute-start.2 = (bf16[2,384,512]{2,1,0:T(8,128)(2,1)S(1)}, bf16[2,384,512]{2,1,0:T(8,128)(2,1)S(1)}, u32[]{:S(2)}, u32[]{:S(2)}) collective-permute-start(bf16[2,384,512]{2,1,0:T(8,128)(2,1)S(1)} %get-tuple-element.36.refs_0_), channel_id=1, source_target_pairs={{0,2},{2,0},{4,6},{6,4},{8,10},{10,8},{12,14},{14,12},{1,3},{3,1},... | collective-permute-start | bytes 2359304 | tf_op jit(solution)/shard_map/ppermute | solution.py:128
  37.0 16.0 %collective-permute-start.1 = (bf16[2,10,32,512]{3,2,1,0:T(8,128)(2,1)S(1)}, bf16[2,10,32,512]{3,2,1,0:T(8,128)(2,1)S(1)}, u32[]{:S(2)}, u32[]{:S(2)}) collective-permute-start(bf16[2,10,32,512]{3,2,1,0:T(8,128)(2,1)S(1)} %join.5.refs_0_.left), channel_id=1, source_target_pairs={{0,4},{2,6},{4,0},{6,2},{8,12},{10,14},{12,8},{14,10},{1,5},{3,7},... | collective-permute-start | bytes 1966088 | tf_op jit(solution)/shard_map/ppermute | solution.py:124
  53.4 29.4 %collective-permute-start.4 = (bf16[4,10,32,512]{3,2,1,0:T(8,128)(2,1)S(1)}, bf16[4,10,32,512]{3,2,1,0:T(8,128)(2,1)S(1)}, u32[]{:S(2)}, u32[]{:S(2)}) collective-permute-start(bf16[4,10,32,512]{3,2,1,0:T(8,128)(2,1)S(1)} %join.6.refs_0_), channel_id=1, source_target_pairs={{0,2},{2,0},{4,6},{6,4},{8,10},{10,8},{12,14},{14,12},{1,3},{3,1},... | collective-permute-start | bytes 3932168 | tf_op jit(solution)/shard_map/ppermute | solution.py:128
  55.0 12.1 %collective-permute-start.7 = (bf16[2,2,96,512]{3,2,1,0:T(8,128)(2,1)S(1)}, bf16[2,2,96,512]{3,2,1,0:T(8,128)(2,1)S(1)}, u32[]{:S(2)}, u32[]{:S(2)}) collective-permute-start(bf16[2,2,96,512]{3,2,1,0:T(8,128)(2,1)S(1)} %get-tuple-element.39.refs_0_), channel_id=1, source_target_pairs={{0,4},{2,6},{4,0},{6,2},{8,12},{10,14},{12,8},{14,10},{1,5},{3,7},... | collective-permute-start | bytes 1179656 | tf_op jit(solution)/shard_map/ppermute | solution.py:124
  56.4 20.8 %collective-permute-start.6 = (bf16[2,2,96,512]{3,2,1,0:T(8,128)(2,1)S(1)}, bf16[2,2,96,512]{3,2,1,0:T(8,128)(2,1)S(1)}, u32[]{:S(2)}, u32[]{:S(2)}) collective-permute-start(bf16[2,2,96,512]{3,2,1,0:T(8,128)(2,1)S(1)} %get-tuple-element.40.refs_0_), channel_id=1, source_target_pairs={{0,4},{2,6},{4,0},{6,2},{8,12},{10,14},{12,8},{14,10},{1,5},{3,7},... | collective-permute-start | bytes 1179656 | tf_op jit(solution)/shard_map/ppermute | solution.py:124
  67.1 10.2 %collective-permute-start.8 = (bf16[2,96,512]{2,1,0:T(8,128)(2,1)S(1)}, bf16[2,96,512]{2,1,0:T(8,128)(2,1)S(1)}, u32[]{:S(2)}, u32[]{:S(2)}) collective-permute-start(bf16[2,96,512]{2,1,0:T(8,128)(2,1)S(1)} %get-tuple-element.43.refs_0_), channel_id=1, source_target_pairs={{0,8},{2,10},{4,12},{6,14},{8,0},{10,2},{12,4},{14,6},{1,9},{3,11}... | collective-permute-start | bytes 589832 | tf_op jit(solution)/shard_map/ppermute | solution.py:124
  71.5 28.6 %collective-permute-start.5 = (bf16[4,10,32,512]{3,2,1,0:T(8,128)(2,1)S(1)}, bf16[4,10,32,512]{3,2,1,0:T(8,128)(2,1)S(1)}, u32[]{:S(2)}, u32[]{:S(2)}) collective-permute-start(bf16[4,10,32,512]{3,2,1,0:T(8,128)(2,1)S(1)} %join.6.refs_0_), channel_id=1, source_target_pairs={{0,1},{1,0},{2,3},{3,2},{4,5},{5,4},{6,7},{7,6},{8,9},{9,8},{10,11... | collective-permute-start | bytes 3932168 | tf_op jit(solution)/shard_map/ppermute | solution.py:132
  83.8 17.8 %copy-start.6 = (s32[8,8]{1,0:T(8,128)S(1)}, s32[8,8]{1,0:T(8,128)}, u32[]{:S(2)}) copy-start(s32[8,8]{1,0:T(8,128)} %pattern.11) | copy-start | bytes 772
  83.8 16.2 %collective-permute-start.9 = (bf16[4,10,32,512]{3,2,1,0:T(8,128)(2,1)S(1)}, bf16[4,10,32,512]{3,2,1,0:T(8,128)(2,1)S(1)}, u32[]{:S(2)}, u32[]{:S(2)}) collective-permute-start(bf16[4,10,32,512]{3,2,1,0:T(8,128)(2,1)S(1)} %hold.2), channel_id=1, source_target_pairs={{0,1},{1,0},{2,3},{3,2},{4,5},{5,4},{6,7},{7,6},{8,9},{9,8},{10,11... | collective-permute-start | bytes 3932168 | tf_op jit(solution)/shard_map/ppermute | solution.py:132
  83.8 13.8 %collective-permute-start.10 = (bf16[2,96,512]{2,1,0:T(8,128)(2,1)S(1)}, bf16[2,96,512]{2,1,0:T(8,128)(2,1)S(1)}, u32[]{:S(2)}, u32[]{:S(2)}) collective-permute-start(bf16[2,96,512]{2,1,0:T(8,128)(2,1)S(1)} %get-tuple-element.44.refs_0_), channel_id=1, source_target_pairs={{0,8},{2,10},{4,12},{6,14},{8,0},{10,2},{12,4},{14,6},{1,9},{3,11}... | collective-permute-start | bytes 589832 | tf_op jit(solution)/shard_map/ppermute | solution.py:124
  97.8 17.2 %collective-permute-start.12 = (bf16[2,10,32,512]{3,2,1,0:T(8,128)(2,1)S(1)}, bf16[2,10,32,512]{3,2,1,0:T(8,128)(2,1)S(1)}, u32[]{:S(2)}, u32[]{:S(2)}) collective-permute-start(bf16[2,10,32,512]{3,2,1,0:T(8,128)(2,1)S(1)} %join.7.refs_8_.left), channel_id=1, source_target_pairs={{0,2},{2,0},{4,6},{6,4},{8,10},{10,8},{12,14},{14,12},{1,3},{3,1},... | collective-permute-start | bytes 1966088 | tf_op jit(solution)/shard_map/ppermute | solution.py:128
  99.4 18.5 %collective-permute-start.11 = (bf16[2,10,32,512]{3,2,1,0:T(8,128)(2,1)S(1)}, bf16[2,10,32,512]{3,2,1,0:T(8,128)(2,1)S(1)}, u32[]{:S(2)}, u32[]{:S(2)}) collective-permute-start(bf16[2,10,32,512]{3,2,1,0:T(8,128)(2,1)S(1)} %join.7.refs_8_.left), channel_id=1, source_target_pairs={{0,4},{2,6},{4,0},{6,2},{8,12},{10,14},{12,8},{14,10},{1,5},{3,7},... | collective-permute-start | bytes 1966088 | tf_op jit(solution)/shard_map/ppermute | solution.py:124
  107.0 16.4 %all-to-all-start = ((bf16[8,96,256]{2,1,0:T(8,128)(2,1)}), bf16[8,96,256]{2,1,0:T(8,128)(2,1)S(1)}, u32[]{:S(2)}, u32[]{:S(2)}) async-start(bf16[8,96,256]{2,1,0:T(8,128)(2,1)} %solve.3), calls=%async_computation | async-start | bytes 786432 | tf_op jit(solution)/shard_map/all_to_all | solution.py:503
  118.8 18.5 %collective-permute-start.13 = (bf16[2,10,32,512]{3,2,1,0:T(8,128)(2,1)}, bf16[2,10,32,512]{3,2,1,0:T(8,128)(2,1)S(1)}, u32[]{:S(2)}, u32[]{:S(2)}) collective-permute-start(bf16[2,10,32,512]{3,2,1,0:T(8,128)(2,1)} %hold.3), channel_id=1, source_target_pairs={{0,2},{2,0},{4,6},{6,4},{8,10},{10,8},{12,14},{14,12},{1,3},{3,1},... | collective-permute-start | bytes 1966088 | tf_op jit(solution)/shard_map/ppermute | solution.py:128
  128.4 25.8 %collective-permute-start.20 = (bf16[2,384,512]{2,1,0:T(8,128)(2,1)S(1)}, bf16[2,384,512]{2,1,0:T(8,128)(2,1)S(1)}, u32[]{:S(2)}, u32[]{:S(2)}) collective-permute-start(bf16[2,384,512]{2,1,0:T(8,128)(2,1)S(1)} %get-tuple-element.56), channel_id=1, source_target_pairs={{0,2},{2,0},{4,6},{6,4},{8,10},{10,8},{12,14},{14,12},{1,3},{3,1},... | collective-permute-start | bytes 2359304 | tf_op jit(solution)/shard_map/ppermute | solution.py:128
  140.6 39.8 %collective-permute-start.15 = (bf16[4,10,32,512]{3,2,1,0:T(8,128)(2,1)S(1)}, bf16[4,10,32,512]{3,2,1,0:T(8,128)(2,1)}, u32[]{:S(2)}, u32[]{:S(2)}) collective-permute-start(bf16[4,10,32,512]{3,2,1,0:T(8,128)(2,1)S(1)} %join.9.refs_1_), channel_id=1, source_target_pairs={{0,1},{1,0},{2,3},{3,2},{4,5},{5,4},{6,7},{7,6},{8,9},{9,8},{10,11... | collective-permute-start | bytes 3932168 | tf_op jit(solution)/shard_map/ppermute | solution.py:132
  141.1 13.0 %copy-start.3 = (f32[2,384,512]{2,1,0:T(8,128)S(1)}, f32[2,384,512]{2,1,0:T(8,128)}, u32[]{:S(2)}) copy-start(f32[2,384,512]{2,1,0:T(8,128)} %copy-done.2) | copy-start | bytes 4718596
  141.1 39.2 %collective-permute-start.14 = (bf16[4,10,32,512]{3,2,1,0:T(8,128)(2,1)S(1)}, bf16[4,10,32,512]{3,2,1,0:T(8,128)(2,1)}, u32[]{:S(2)}, u32[]{:S(2)}) collective-permute-start(bf16[4,10,32,512]{3,2,1,0:T(8,128)(2,1)S(1)} %join.8.refs_0_), channel_id=1, source_target_pairs={{0,1},{1,0},{2,3},{3,2},{4,5},{5,4},{6,7},{7,6},{8,9},{9,8},{10,11... | collective-permute-start | bytes 3932168 | tf_op jit(solution)/shard_map/ppermute | solution.py:132
  144.5 18.0 %collective-permute-start.16 = (bf16[1,384,512]{2,1,0:T(8,128)(2,1)S(1)}, bf16[1,384,512]{2,1,0:T(8,128)(2,1)S(1)}, u32[]{:S(2)}, u32[]{:S(2)}) collective-permute-start(bf16[1,384,512]{2,1,0:T(8,128)(2,1)S(1)} %get-tuple-element.50), channel_id=1, source_target_pairs={{0,2},{2,0},{4,6},{6,4},{8,10},{10,8},{12,14},{14,12},{1,3},{3,1},... | collective-permute-start | bytes 1179656 | tf_op jit(solution)/shard_map/ppermute | solution.py:128
  154.8 11.9 %collective-permute-start.21 = (bf16[2,2,96,512]{3,2,1,0:T(8,128)(2,1)S(1)}, bf16[2,2,96,512]{3,2,1,0:T(8,128)(2,1)S(1)}, u32[]{:S(2)}, u32[]{:S(2)}) collective-permute-start(bf16[2,2,96,512]{3,2,1,0:T(8,128)(2,1)S(1)} %get-tuple-element.58), channel_id=1, source_target_pairs={{0,4},{2,6},{4,0},{6,2},{8,12},{10,14},{12,8},{14,10},{1,5},{3,7},... | collective-permute-start | bytes 1179656 | tf_op jit(solution)/shard_map/ppermute | solution.py:124
  154.9 13.1 %collective-permute-start.19 = (bf16[1,384,512]{2,1,0:T(8,128)(2,1)S(1)}, bf16[1,384,512]{2,1,0:T(8,128)(2,1)S(1)}, u32[]{:S(2)}, u32[]{:S(2)}) collective-permute-start(bf16[1,384,512]{2,1,0:T(8,128)(2,1)S(1)} %get-tuple-element.55), channel_id=1, source_target_pairs={{0,2},{2,0},{4,6},{6,4},{8,10},{10,8},{12,14},{14,12},{1,3},{3,1},... | collective-permute-start | bytes 1179656 | tf_op jit(solution)/shard_map/ppermute | solution.py:128
  163.2 8.1 %collective-permute-start.17 = (bf16[2,1,96,512]{3,2,1,0:T(8,128)(2,1)S(1)}, bf16[2,1,96,512]{3,2,1,0:T(8,128)(2,1)S(1)}, u32[]{:S(2)}, u32[]{:S(2)}) collective-permute-start(bf16[2,1,96,512]{3,2,1,0:T(8,128)(2,1)S(1)} %get-tuple-element.52), channel_id=1, source_target_pairs={{0,4},{2,6},{4,0},{6,2},{8,12},{10,14},{12,8},{14,10},{1,5},{3,7},... | collective-permute-start | bytes 589832 | tf_op jit(solution)/shard_map/ppermute | solution.py:124
  166.8 10.4 %collective-permute-start.23 = (bf16[2,96,512]{2,1,0:T(8,128)(2,1)S(1)}, bf16[2,96,512]{2,1,0:T(8,128)(2,1)S(1)}, u32[]{:S(2)}, u32[]{:S(2)}) collective-permute-start(bf16[2,96,512]{2,1,0:T(8,128)(2,1)S(1)} %get-tuple-element.59.refs_0_), channel_id=1, source_target_pairs={{0,8},{2,10},{4,12},{6,14},{8,0},{10,2},{12,4},{14,6},{1,9},{3,11}... | collective-permute-start | bytes 589832 | tf_op jit(solution)/shard_map/ppermute | solution.py:124
  168.6 9.0 %collective-permute-start.22 = (bf16[2,1,96,512]{3,2,1,0:T(8,128)(2,1)S(1)}, bf16[2,1,96,512]{3,2,1,0:T(8,128)(2,1)S(1)}, u32[]{:S(2)}, u32[]{:S(2)}) collective-permute-start(bf16[2,1,96,512]{3,2,1,0:T(8,128)(2,1)S(1)} %get-tuple-element.61), channel_id=1, source_target_pairs={{0,4},{2,6},{4,0},{6,2},{8,12},{10,14},{12,8},{14,10},{1,5},{3,7},... | collective-permute-start | bytes 589832 | tf_op jit(solution)/shard_map/ppermute | solution.py:124
  171.3 12.2 %collective-permute-start.18 = (bf16[1,96,512]{2,1,0:T(8,128)(2,1)S(1)}, bf16[1,96,512]{2,1,0:T(8,128)(2,1)S(1)}, u32[]{:S(2)}, u32[]{:S(2)}) collective-permute-start(bf16[1,96,512]{2,1,0:T(8,128)(2,1)S(1)} %get-tuple-element.54), channel_id=1, source_target_pairs={{0,8},{2,10},{4,12},{6,14},{8,0},{10,2},{12,4},{14,6},{1,9},{3,11}... | collective-permute-start | bytes 294920 | tf_op jit(solution)/shard_map/ppermute | solution.py:124
  177.6 5.9 %collective-permute-start.24 = (bf16[1,96,512]{2,1,0:T(8,128)(2,1)S(1)}, bf16[1,96,512]{2,1,0:T(8,128)(2,1)S(1)}, u32[]{:S(2)}, u32[]{:S(2)}) collective-permute-start(bf16[1,96,512]{2,1,0:T(8,128)(2,1)S(1)} %get-tuple-element.63), channel_id=1, source_target_pairs={{0,8},{2,10},{4,12},{6,14},{8,0},{10,2},{12,4},{14,6},{1,9},{3,11}... | collective-permute-start | bytes 294920 | tf_op jit(solution)/shard_map/ppermute | solution.py:124
  (5 other events, 6.2 us)

commit v4 on v3

--- a/solution.py
+++ b/solution.py
@@ -10,7 +10,7 @@
 F32, BF16 = jnp.float32, jnp.bfloat16
 VMEM_LIMIT = 50 * 1024 * 1024
 STAGES = ((7, 6, 5, 4), (3, 2, 1, 0))
-CHUNKS = (((7, 6), (5, 4)), ((3, 2), (1,), (0,)))
+CHUNKS = (((7, 6, 5), (4,)), ((3, 2), (1,), (0,)))
 
 SMEM_SPEC = pl.BlockSpec(memory_space=pltpu.SMEM)
 VMEM_SPEC = pl.BlockSpec(memory_space=pltpu.VMEM)
@@ -29,7 +29,7 @@
 
 
 def weights_kernel(stages, meta, window_ref, diag_ref, *refs):
-    out, turned, sems = refs[-3:]
+    out, diag, turned, sems = refs[-4:]
     half, rows = out.shape[2], window_ref.shape[2]
     start = pl.multiple_of(meta[2] * half, half)
     copies = []
@@ -44,13 +44,16 @@
     for target, j, k in blocks:
         if j != k:
             move(window_ref.at[j, k, pl.ds(start, half)], target)
+    load = pltpu.make_async_copy(diag_ref, diag, sems.at[len(blocks)])
+    load.start()
     lane = lax.broadcasted_iota(jnp.int32, (half, rows), 1)
     pick = jnp.where(lane == lax.broadcasted_iota(jnp.int32, (half, rows), 0) + start, 1.0, 0.0)
     pick = pick.astype(BF16)
+    load.wait()
     for target, j, k in blocks:
         if j == k:
             turned[k] = lax.dot_general(
-                pick, diag_ref[k], (((1,), (1,)), ((), ())), preferred_element_type=F32
+                pick, diag[k], (((1,), (1,)), ((), ())), preferred_element_type=F32
             ).astype(BF16)
             move(turned.at[k], target)
     for copy in copies:
@@ -63,11 +66,12 @@
     return pl.pallas_call(
         functools.partial(weights_kernel, stages),
         out_shape=jax.ShapeDtypeStruct((1, blocks, rows // 2, super_size), BF16),
-        in_specs=[SMEM_SPEC, ANY_SPEC, VMEM_SPEC] + [ANY_SPEC] * len(after),
+        in_specs=[SMEM_SPEC, ANY_SPEC, ANY_SPEC] + [ANY_SPEC] * len(after),
         out_specs=ANY_SPEC,
         scratch_shapes=[
+            pltpu.VMEM(diag_inverse.shape, BF16),
             pltpu.VMEM((count, rows // 2, super_size), BF16),
-            pltpu.SemaphoreType.DMA((blocks,)),
+            pltpu.SemaphoreType.DMA((blocks + 1,)),
         ],
         compiler_params=params(),
         name="own_weights",
@@ -322,8 +326,15 @@
 def solve_kernel(columns, ready, groups, whole, first, origins, meta, pattern, *refs):
     weights, refs = refs[: len(origins)], refs[len(origins) :]
     count = 2 * len(groups)
-    parts, solved = refs[:count], refs[count : count + len(ready)]
-    out, slab, sems = refs[-3:]
+    sources, solved = refs[:count], refs[count : count + len(ready)]
+    parts = refs[-count - 1 : -1]
+    out, slab, sems = refs[-count - 4], refs[-count - 3], refs[-count - 2]
+    loads = [
+        pltpu.make_async_copy(source, part, refs[-1].at[i])
+        for i, (source, part) in enumerate(zip(sources, parts))
+    ]
+    for load in loads:
+        load.start()
     size = slab.shape[3]
     starts = [0]
     for k in [k for group in groups for k in group]:
@@ -347,6 +358,8 @@
         for index, j in enumerate(group):
             done[j] = ref[index]
     place = 0
+    for load in loads:
+        load.wait()
 
     def next_block():
         for copy in copies.pop(place, ()):
@@ -397,12 +410,15 @@
         out_shape=jax.ShapeDtypeStruct(shape, BF16),
         in_specs=[SMEM_SPEC] * 2
         + [ANY_SPEC] * len(arrays)
-        + [VMEM_SPEC] * (len(flat) + len(solved))
+        + [ANY_SPEC] * len(flat)
+        + [VMEM_SPEC] * len(solved)
         + [ANY_SPEC] * len(after),
         out_specs=VMEM_SPEC,
         scratch_shapes=[
             pltpu.VMEM((count, 2 * owners, rows, super_size), BF16),
             pltpu.SemaphoreType.DMA((2, 2 * owners)),
+            *[pltpu.VMEM(p.shape, p.dtype) for p in flat],
+            pltpu.SemaphoreType.DMA((len(flat),)),
         ],
         compiler_params=params(),
         name="solve",
@@ -475,7 +491,7 @@
     last_a = z_move(end_a, 2, owners)
     end_b, total_b = line_sum(mine_b, across_b, (end_a,))
     last_b = z_move(end_b, 2, owners)
-    near_1 = join(own_rows, opposite, (last_b,), count_0, count_1)
+    near_1 = join(own_rows, opposite, (last_b, beside_0), count_0, count_1)
     far_1 = z_move(near_1, 1, owners)
     x_near_1 = x_move(near_1, owners)
     core_line, core_beside = other_core([line_0, hold(beside_0, (end_b, last_a))])

time: 204 us -> 199 us (0.975)
  Pallas kernels: 55.8 us -> 60.3 us
  starting transfers between devices: 38.7 us -> 34.2 us
  local copies, waits for them, and re-layouts: 6.53 us -> 4.37 us
    ppermute x8, waiting for transfers between devices: 44.7 us -> 37.7 us  [x_move(): return lax.ppermute(part, 'own', [(o, o ^ 1) for o in range(owners)])]
    ppermute x13, starting transfers between devices: 26.3 us -> 20.2 us  [z_move(): return lax.ppermute(part, 'own', [(o, o ^ 2 * d) for o in range(owners)])]
    ppermute x13, waiting for transfers between devices: 37.9 us -> 42.5 us  [z_move(): return lax.ppermute(part, 'own', [(o, o ^ 2 * d) for o in range(owners)])]
    pallas_call x3, Pallas kernels: 23.4 us -> 25.8 us  [outer_terms(): pl.pallas_call(functools.partial(outer_kernel, columns, split), out_shape...]
    unnamed x23 -> x21, local copies, waits for them, and re-layouts: 6.44 us -> 4.28 us
  transfers between devices with their start and end apart: 26 -> 26, of which waited for: 16 -> 18; matrix products, arithmetic and copies ran while one was open for 0% -> 0% of each run, Pallas kernels for 24% -> 26%
where the time goes in v4:
time: 199 us; the launch traced here: 198 us
  waiting for transfers between devices  85.2 us (43%)
  Pallas kernels  60.3 us (30%)
  starting transfers between devices  34.2 us (17%)
  blocking collectives  13.5 us (7%)
  local copies, waits for them, and re-layouts  4.37 us (2%)
    ppermute x13, waiting for transfers between devices, z_move(): return lax.ppermute(part, 'own', [(o, o ^ 2 * d) for o in range(owners)])  42.5 us
    ppermute x8, waiting for transfers between devices, x_move(): return lax.ppermute(part, 'own', [(o, o ^ 1) for o in range(owners)])  37.7 us
    pallas_call x3, Pallas kernels, outer_terms(): pl.pallas_call(functools.partial(outer_kernel, columns, split), out_shape...  25.8 us
    ppermute x13, starting transfers between devices, z_move(): return lax.ppermute(part, 'own', [(o, o ^ 2 * d) for o in range(owners)])  20.2 us
    pallas_call x3, Pallas kernels, solve(): pl.pallas_call(functools.partial(solve_kernel, columns, ready, groups, wh...  14.1 us
    all_to_all x1, blocking collectives, staged_body(): rows_1 = lax.all_to_all(done, 'own', 0, 0, tiled=True)  13.5 us
    pallas_call x3, Pallas kernels, cross_terms(): pl.pallas_call(functools.partial(cross_kernel, chunk, offset, before), ou...  9.46 us
    ppermute x8, starting transfers between devices, x_move(): return lax.ppermute(part, 'own', [(o, o ^ 1) for o in range(owners)])  8.64 us
  transfers between devices with their start and end apart: 26, of which 18 were waited for; matrix products, arithmetic and copies ran while one was open for 0% of the time, Pallas kernels for 26%

profile of v4, /device:TPU:0, one launch (start us, length us, event | category | flops | bytes accessed | tf_op | source)
XLA Modules:
  0.0 197.9 jit_solution(11758763618146138260)
XLA Ops:
  1.6 2.3 %own_weights.1.refs_0_.left = bf16[1,20,32,512]{3,2,1,0:T(8,128)(2,1)S(1)} custom-call(s32[8]{0:T(128)S(1)} %stack.32.meta, bf16[8,8,64,512]{3,2,1,0:T(8,128)(2,1)} %window.5, bf16[8,512,64]{2,1,0:T(8,128)(2,1)S(1)} %copy.9.diag_ref), custom_call_target="tpu_custom_call" | custom-call | tf_op jit(solution)/shard_map/own_weights/pallas_call | solution.py:66
  4.0 4.1 %collective-permute-start = (bf16[1,20,32,512]{3,2,1,0:T(8,128)(2,1)S(1)}, bf16[1,20,32,512]{3,2,1,0:T(8,128)(2,1)S(1)}, u32[]{:S(2)}, u32[]{:S(2)}) collective-permute-start(bf16[1,20,32,512]{3,2,1,0:T(8,128)(2,1)S(1)} %own_weights.1.refs_0_.left), channel_id=1, source_target_pairs={{0,8},{2,10},{4,12},{6,14},{8,0},{10,2},{12,4},{14,6},{1,9},{3,11}... | collective-permute-start | bytes 1966088 | tf_op jit(solution)/shard_map/ppermute | solution.py:128
  8.1 8.7 %outer_terms.3 = (bf16[3,384,512]{2,1,0:T(8,128)(2,1)S(1)}, f32[3,384,512]{2,1,0:T(8,128)}) custom-call(s32[8]{0:T(128)S(1)} %stack.32.meta, s32[16]{0:T(128)S(1)} %copy-done.6, s32[16]{0:T(128)S(1)} %copy-done.7, bf16[2,512,768]{2,1,0:T(8,128)(2,1)} %known.5, bf16[8,64,768]{2,1,0:T(8,128)(2,1)S(1)} %copy-done.2, bf16[16,512,512]{2,1,0:T(8,128)(2,1)} %blocks.5, ...), custom_call_target="tpu_custom_call" | custom-call | tf_op jit(solution)/shard_map/outer_terms/pallas_call | solution.py:203
  16.9 1.9 collective-permute-start.3
  18.8 4.0 %outer_terms.4 = (bf16[1,384,512]{2,1,0:T(8,128)(2,1)S(1)}, f32[1,384,512]{2,1,0:T(8,128)S(1)}) custom-call(s32[8]{0:T(128)S(1)} %stack.32.meta, s32[16]{0:T(128)S(1)} %copy-done.6, s32[16]{0:T(128)S(1)} %copy-done.7, bf16[2,512,768]{2,1,0:T(8,128)(2,1)} %known.5, bf16[8,64,768]{2,1,0:T(8,128)(2,1)S(1)} %copy-done.2, bf16[16,512,512]{2,1,0:T(8,128)(2,1)} %blocks.5, ...), custom_call_target="tpu_custom_call" | custom-call | tf_op jit(solution)/shard_map/outer_terms/pallas_call | solution.py:203
  22.8 13.0 %outer_terms.5.refs_0_.base = f32[4,768,512]{2,1,0:T(8,128)} custom-call(s32[8]{0:T(128)S(1)} %stack.32.meta, s32[16]{0:T(128)S(1)} %copy-done.6, s32[16]{0:T(128)S(1)} %copy-done.7, bf16[2,512,768]{2,1,0:T(8,128)(2,1)S(1)} %copy-done, bf16[8,64,768]{2,1,0:T(8,128)(2,1)S(1)} %copy-done.2, bf16[16,512,512]{2,1,0:T(8,128)(2,1)} %blocks.5, ...), custom_call_target="tpu_custom_call" | custom-call | tf_op jit(solution)/shard_map/outer_terms/pallas_call | solution.py:203
  39.4 6.4 %collective-permute-done.3.got = bf16[3,384,512]{2,1,0:T(8,128)(2,1)S(1)} collective-permute-done((bf16[3,384,512]{2,1,0:T(8,128)(2,1)S(1)}, bf16[3,384,512]{2,1,0:T(8,128)(2,1)S(1)}, u32[]{:S(2)}, u32[]{:S(2)}) %collective-permute-start.3) | collective-permute-done | bytes 1179680 | tf_op jit(solution)/shard_map/ppermute | solution.py:132
  47.7 5.2 %collective-permute-done.2.got = bf16[1,384,512]{2,1,0:T(8,128)(2,1)S(1)} collective-permute-done((bf16[1,384,512]{2,1,0:T(8,128)(2,1)S(1)}, bf16[1,384,512]{2,1,0:T(8,128)(2,1)S(1)}, u32[]{:S(2)}, u32[]{:S(2)}) %collective-permute-start.2) | collective-permute-done | bytes 393248 | tf_op jit(solution)/shard_map/ppermute | solution.py:132
  55.8 2.3 %collective-permute-start.7 = (bf16[2,3,96,512]{3,2,1,0:T(8,128)(2,1)S(1)}, bf16[2,3,96,512]{3,2,1,0:T(8,128)(2,1)S(1)}, u32[]{:S(2)}, u32[]{:S(2)}) collective-permute-start(bf16[2,3,96,512]{3,2,1,0:T(8,128)(2,1)S(1)} %get-tuple-element.39.refs_0_), channel_id=1, source_target_pairs={{0,4},{2,6},{4,0},{6,2},{8,12},{10,14},{12,8},{14,10},{1,5},{3,7},... | collective-permute-start | bytes 1769480 | tf_op jit(solution)/shard_map/ppermute | solution.py:128
  58.1 11.9 %collective-permute-done.7.got = bf16[2,3,96,512]{3,2,1,0:T(8,128)(2,1)S(1)} collective-permute-done((bf16[2,3,96,512]{3,2,1,0:T(8,128)(2,1)S(1)}, bf16[2,3,96,512]{3,2,1,0:T(8,128)(2,1)S(1)}, u32[]{:S(2)}, u32[]{:S(2)}) %collective-permute-start.7) | collective-permute-done | bytes 589856 | tf_op jit(solution)/shard_map/ppermute | solution.py:128
  70.1 2.7 %collective-permute-start.8 = (bf16[3,96,512]{2,1,0:T(8,128)(2,1)S(1)}, bf16[3,96,512]{2,1,0:T(8,128)(2,1)S(1)}, u32[]{:S(2)}, u32[]{:S(2)}) collective-permute-start(bf16[3,96,512]{2,1,0:T(8,128)(2,1)S(1)} %get-tuple-element.43.refs_0_), channel_id=1, source_target_pairs={{0,8},{2,10},{4,12},{6,14},{8,0},{10,2},{12,4},{14,6},{1,9},{3,11}... | collective-permute-start | bytes 884744 | tf_op jit(solution)/shard_map/ppermute | solution.py:128
  74.2 7.6 %collective-permute-done.6.got = bf16[2,1,96,512]{3,2,1,0:T(8,128)(2,1)S(1)} collective-permute-done((bf16[2,1,96,512]{3,2,1,0:T(8,128)(2,1)S(1)}, bf16[2,1,96,512]{3,2,1,0:T(8,128)(2,1)S(1)}, u32[]{:S(2)}, u32[]{:S(2)}) %collective-permute-start.6) | collective-permute-done | bytes 196640 | tf_op jit(solution)/shard_map/ppermute | solution.py:128
  81.8 2.8 %collective-permute-done.8.refs_1_.refs_5_ = bf16[3,96,512]{2,1,0:T(8,128)(2,1)S(1)} collective-permute-done((bf16[3,96,512]{2,1,0:T(8,128)(2,1)S(1)}, bf16[3,96,512]{2,1,0:T(8,128)(2,1)S(1)}, u32[]{:S(2)}, u32[]{:S(2)}) %collective-permute-start.8) | collective-permute-done | bytes 294944 | tf_op jit(solution)/shard_map/ppermute | solution.py:128
  84.8 2.3 %collective-permute-start.10 = (bf16[1,96,512]{2,1,0:T(8,128)(2,1)S(1)}, bf16[1,96,512]{2,1,0:T(8,128)(2,1)S(1)}, u32[]{:S(2)}, u32[]{:S(2)}) collective-permute-start(bf16[1,96,512]{2,1,0:T(8,128)(2,1)S(1)} %get-tuple-element.44.refs_0_), channel_id=1, source_target_pairs={{0,8},{2,10},{4,12},{6,14},{8,0},{10,2},{12,4},{14,6},{1,9},{3,11}... | collective-permute-start | bytes 294920 | tf_op jit(solution)/shard_map/ppermute | solution.py:128
  87.1 5.9 %collective-permute-done.10.refs_0_.refs_7_ = bf16[1,96,512]{2,1,0:T(8,128)(2,1)S(1)} collective-permute-done((bf16[1,96,512]{2,1,0:T(8,128)(2,1)S(1)}, bf16[1,96,512]{2,1,0:T(8,128)(2,1)S(1)}, u32[]{:S(2)}, u32[]{:S(2)}) %collective-permute-start.10) | collective-permute-done | bytes 98336 | tf_op jit(solution)/shard_map/ppermute | solution.py:128
  96.7 6.0 %solve.3 = bf16[8,96,256]{2,1,0:T(8,128)(2,1)} custom-call(s32[8]{0:T(128)S(1)} %stack.32.meta, s32[8,8]{1,0:T(8,128)S(1)} %copy-done.5, bf16[4,10,32,512]{3,2,1,0:T(8,128)(2,1)S(1)} %join.6.refs_0_, bf16[4,10,32,512]{3,2,1,0:T(8,128)(2,1)} %copy-done.1, bf16[4,10,32,512]{3,2,1,0:T(8,128)(2,1)} %copy-done.8, bf16[4,10,32,512]{3,2,1,0:T(8,128)(2,1)} %copy-done.9, ...), custom_call_target="tpu_custom_call" | custom-call | tf_op jit(solution)/shard_map/solve/pallas_call | solution.py:408
  102.6 4.7 %all-to-all-start = ((bf16[8,96,256]{2,1,0:T(8,128)(2,1)}), bf16[8,96,256]{2,1,0:T(8,128)(2,1)S(1)}, u32[]{:S(2)}, u32[]{:S(2)}) async-start(bf16[8,96,256]{2,1,0:T(8,128)(2,1)} %solve.3), calls=%async_computation | async-start | bytes 786432 | tf_op jit(solution)/shard_map/all_to_all | solution.py:519
  109.1 3.5 %collective-permute-done.11.right.source = bf16[2,10,32,512]{3,2,1,0:T(8,128)(2,1)S(1)} collective-permute-done((bf16[2,10,32,512]{3,2,1,0:T(8,128)(2,1)S(1)}, bf16[2,10,32,512]{3,2,1,0:T(8,128)(2,1)S(1)}, u32[]{:S(2)}, u32[]{:S(2)}) %collective-permute-start.11) | collective-permute-done | bytes 655392 | tf_op jit(solution)/shard_map/ppermute | solution.py:128
  113.5 5.0 %all-to-all-done.refs_0_ = bf16[8,96,256]{2,1,0:T(8,128)(2,1)S(1)} async-done(((bf16[8,96,256]{2,1,0:T(8,128)(2,1)}), bf16[8,96,256]{2,1,0:T(8,128)(2,1)S(1)}, u32[]{:S(2)}, u32[]{:S(2)}) %all-to-all-start) | async-done | bytes 393248 | tf_op jit(solution)/shard_map/all_to_all | solution.py:519
  118.5 3.8 %cross_terms.3 = (bf16[2,384,512]{2,1,0:T(8,128)(2,1)S(1)}, f32[2,384,512]{2,1,0:T(8,128)S(1)}) custom-call(s32[8]{0:T(128)S(1)} %stack.32.meta, s32[8,8]{1,0:T(8,128)S(1)} %copy-done.5, f32[4,768,512]{2,1,0:T(8,128)} %outer_terms.5.refs_0_.base, bf16[8,8,64,512]{3,2,1,0:T(8,128)(2,1)} %window.5, bf16[8,96,256]{2,1,0:T(8,128)(2,1)S(1)} %all-to-all-done.refs_0_, ...), custom_call_target="tpu_custom_call" | custom-call | tf_op jit(solution)/shard_map/cross_terms/pallas_call | solution.py:256
  125.0 6.8 %collective-permute-done.13.refs_1_.right = bf16[2,10,32,512]{3,2,1,0:T(8,128)(2,1)S(1)} collective-permute-done((bf16[2,10,32,512]{3,2,1,0:T(8,128)(2,1)}, bf16[2,10,32,512]{3,2,1,0:T(8,128)(2,1)S(1)}, u32[]{:S(2)}, u32[]{:S(2)}) %collective-permute-start.13) | collective-permute-done | bytes 655392 | tf_op jit(solution)/shard_map/ppermute | solution.py:132
  131.9 2.8 %cross_terms.4 = (bf16[1,384,512]{2,1,0:T(8,128)(2,1)S(1)}, f32[1,384,512]{2,1,0:T(8,128)S(1)}) custom-call(s32[8]{0:T(128)S(1)} %stack.32.meta, s32[8,8]{1,0:T(8,128)S(1)} %copy-done.5, f32[4,768,512]{2,1,0:T(8,128)} %outer_terms.5.refs_0_.base, bf16[8,8,64,512]{3,2,1,0:T(8,128)(2,1)} %window.5, bf16[8,96,256]{2,1,0:T(8,128)(2,1)S(1)} %all-to-all-done.refs_0_, ...), custom_call_target="tpu_custom_call" | custom-call | tf_op jit(solution)/shard_map/cross_terms/pallas_call | solution.py:256
  136.2 2.8 %cross_terms.5 = (bf16[1,384,512]{2,1,0:T(8,128)(2,1)S(1)}, f32[1,384,512]{2,1,0:T(8,128)S(1)}) custom-call(s32[8]{0:T(128)S(1)} %stack.32.meta, s32[8,8]{1,0:T(8,128)S(1)} %copy-done.5, f32[4,768,512]{2,1,0:T(8,128)} %outer_terms.5.refs_0_.base, bf16[8,8,64,512]{3,2,1,0:T(8,128)(2,1)} %window.5, bf16[8,96,256]{2,1,0:T(8,128)(2,1)S(1)} %all-to-all-done.refs_0_, ...), custom_call_target="tpu_custom_call" | custom-call | tf_op jit(solution)/shard_map/cross_terms/pallas_call | solution.py:256
  139.2 9.5 %collective-permute-done.20.got = bf16[2,384,512]{2,1,0:T(8,128)(2,1)S(1)} collective-permute-done((bf16[2,384,512]{2,1,0:T(8,128)(2,1)S(1)}, bf16[2,384,512]{2,1,0:T(8,128)(2,1)S(1)}, u32[]{:S(2)}, u32[]{:S(2)}) %collective-permute-start.20) | collective-permute-done | bytes 786464 | tf_op jit(solution)/shard_map/ppermute | solution.py:132
  150.2 7.0 %collective-permute-done.16.got = bf16[1,384,512]{2,1,0:T(8,128)(2,1)S(1)} collective-permute-done((bf16[1,384,512]{2,1,0:T(8,128)(2,1)S(1)}, bf16[1,384,512]{2,1,0:T(8,128)(2,1)S(1)}, u32[]{:S(2)}, u32[]{:S(2)}) %collective-permute-start.16) | collective-permute-done | bytes 393248 | tf_op jit(solution)/shard_map/ppermute | solution.py:132
  158.0 3.1 %collective-permute-done.21.got = bf16[2,2,96,512]{3,2,1,0:T(8,128)(2,1)S(1)} collective-permute-done((bf16[2,2,96,512]{3,2,1,0:T(8,128)(2,1)S(1)}, bf16[2,2,96,512]{3,2,1,0:T(8,128)(2,1)S(1)}, u32[]{:S(2)}, u32[]{:S(2)}) %collective-permute-start.21) | collective-permute-done | bytes 393248 | tf_op jit(solution)/shard_map/ppermute | solution.py:128
  164.7 3.2 %collective-permute-start.18 = (bf16[1,96,512]{2,1,0:T(8,128)(2,1)S(1)}, bf16[1,96,512]{2,1,0:T(8,128)(2,1)S(1)}, u32[]{:S(2)}, u32[]{:S(2)}) collective-permute-start(bf16[1,96,512]{2,1,0:T(8,128)(2,1)S(1)} %get-tuple-element.54), channel_id=1, source_target_pairs={{0,8},{2,10},{4,12},{6,14},{8,0},{10,2},{12,4},{14,6},{1,9},{3,11}... | collective-permute-start | bytes 294920 | tf_op jit(solution)/shard_map/ppermute | solution.py:128
  168.0 3.1 %collective-permute-done.23.refs_0_.refs_5_ = bf16[2,96,512]{2,1,0:T(8,128)(2,1)S(1)} collective-permute-done((bf16[2,96,512]{2,1,0:T(8,128)(2,1)S(1)}, bf16[2,96,512]{2,1,0:T(8,128)(2,1)S(1)}, u32[]{:S(2)}, u32[]{:S(2)}) %collective-permute-start.23) | collective-permute-done | bytes 196640 | tf_op jit(solution)/shard_map/ppermute | solution.py:128
  173.2 3.6 %solve.4.refs_8_ = bf16[2,96,512]{2,1,0:T(8,128)(2,1)S(1)} custom-call(s32[8]{0:T(128)S(1)} %stack.32.meta, s32[8,8]{1,0:T(8,128)S(1)} %copy-done.5, bf16[4,10,32,512]{3,2,1,0:T(8,128)(2,1)S(1)} %join.8.refs_0_, bf16[4,10,32,512]{3,2,1,0:T(8,128)(2,1)S(1)} %join.9.refs_1_, bf16[4,10,32,512]{3,2,1,0:T(8,128)(2,1)} %collective-permute-done.14.refs_2_, ...), custom_call_target="tpu_custom_call" | custom-call | tf_op jit(solution)/shard_map/solve/pallas_call | solution.py:408
  176.8 1.9 collective-permute-done.24.refs_7_
  178.7 4.5 %solve.5 = bf16[8,96,256]{2,1,0:T(8,128)(2,1)S(1)} custom-call(s32[8]{0:T(128)S(1)} %stack.32.meta, s32[8,8]{1,0:T(8,128)S(1)} %copy-done.5, bf16[4,10,32,512]{3,2,1,0:T(8,128)(2,1)S(1)} %join.8.refs_0_, bf16[4,10,32,512]{3,2,1,0:T(8,128)(2,1)S(1)} %join.9.refs_1_, bf16[4,10,32,512]{3,2,1,0:T(8,128)(2,1)} %collective-permute-done.14.refs_2_, ...), custom_call_target="tpu_custom_call" | custom-call | tf_op jit(solution)/shard_map/solve/pallas_call | solution.py:408
  183.2 13.5 %all_to_all.10.refs_1_ = bf16[8,96,256]{2,1,0:T(8,128)(2,1)S(1)} all-to-all(bf16[8,96,256]{2,1,0:T(8,128)(2,1)S(1)} %solve.5), channel_id=1, replica_groups=mesh['grp'=2,'own'=8,'tile'=2] {'own'}, dimensions={0} | all-to-all | bytes 786432 | tf_op jit(solution)/shard_map/all_to_all | solution.py:541
  (71 shorter events, 31.5 us)
Async XLA Ops:
  1.6 6.5 %copy-start.2 = (bf16[8,64,768]{2,1,0:T(8,128)(2,1)S(1)}, bf16[8,64,768]{2,1,0:T(8,128)(2,1)}, u32[]{:S(2)}) copy-start(bf16[8,64,768]{2,1,0:T(8,128)(2,1)} %draws.5) | copy-start | bytes 2359300
  1.6 6.5 %copy-start.6 = (s32[16]{0:T(128)S(1)}, s32[16]{0:T(128)}, u32[]{:S(2)}) copy-start(s32[16]{0:T(128)} %row_ref.5) | copy-start | bytes 196
  1.6 6.5 %copy-start.7 = (s32[16]{0:T(128)S(1)}, s32[16]{0:T(128)}, u32[]{:S(2)}) copy-start(s32[16]{0:T(128)} %col_ref.5) | copy-start | bytes 196
  4.0 32.9 %collective-permute-start = (bf16[1,20,32,512]{3,2,1,0:T(8,128)(2,1)S(1)}, bf16[1,20,32,512]{3,2,1,0:T(8,128)(2,1)S(1)}, u32[]{:S(2)}, u32[]{:S(2)}) collective-permute-start(bf16[1,20,32,512]{3,2,1,0:T(8,128)(2,1)S(1)} %own_weights.1.refs_0_.left), channel_id=1, source_target_pairs={{0,8},{2,10},{4,12},{6,14},{8,0},{10,2},{12,4},{14,6},{1,9},{3,11}... | collective-permute-start | bytes 1966088 | tf_op jit(solution)/shard_map/ppermute | solution.py:128
  16.9 28.9 %collective-permute-start.3 = (bf16[3,384,512]{2,1,0:T(8,128)(2,1)S(1)}, bf16[3,384,512]{2,1,0:T(8,128)(2,1)S(1)}, u32[]{:S(2)}, u32[]{:S(2)}) collective-permute-start(bf16[3,384,512]{2,1,0:T(8,128)(2,1)S(1)} %get-tuple-element.35.refs_0_), channel_id=1, source_target_pairs={{0,2},{2,0},{4,6},{6,4},{8,10},{10,8},{12,14},{14,12},{1,3},{3,1},... | collective-permute-start | bytes 3538952 | tf_op jit(solution)/shard_map/ppermute | solution.py:132
  37.1 16.4 %collective-permute-start.1 = (bf16[2,10,32,512]{3,2,1,0:T(8,128)(2,1)S(1)}, bf16[2,10,32,512]{3,2,1,0:T(8,128)(2,1)S(1)}, u32[]{:S(2)}, u32[]{:S(2)}) collective-permute-start(bf16[2,10,32,512]{3,2,1,0:T(8,128)(2,1)S(1)} %join.5.refs_0_.left), channel_id=1, source_target_pairs={{0,4},{2,6},{4,0},{6,2},{8,12},{10,14},{12,8},{14,10},{1,5},{3,7},... | collective-permute-start | bytes 1966088 | tf_op jit(solution)/shard_map/ppermute | solution.py:128
  37.9 15.0 %collective-permute-start.2 = (bf16[1,384,512]{2,1,0:T(8,128)(2,1)S(1)}, bf16[1,384,512]{2,1,0:T(8,128)(2,1)S(1)}, u32[]{:S(2)}, u32[]{:S(2)}) collective-permute-start(bf16[1,384,512]{2,1,0:T(8,128)(2,1)S(1)} %get-tuple-element.36.refs_0_), channel_id=1, source_target_pairs={{0,2},{2,0},{4,6},{6,4},{8,10},{10,8},{12,14},{14,12},{1,3},{3,1},... | collective-permute-start | bytes 1179656 | tf_op jit(solution)/shard_map/ppermute | solution.py:132
  54.0 30.6 %collective-permute-start.4 = (bf16[4,10,32,512]{3,2,1,0:T(8,128)(2,1)S(1)}, bf16[4,10,32,512]{3,2,1,0:T(8,128)(2,1)S(1)}, u32[]{:S(2)}, u32[]{:S(2)}) collective-permute-start(bf16[4,10,32,512]{3,2,1,0:T(8,128)(2,1)S(1)} %join.6.refs_0_), channel_id=1, source_target_pairs={{0,2},{2,0},{4,6},{6,4},{8,10},{10,8},{12,14},{14,12},{1,3},{3,1},... | collective-permute-start | bytes 3932168 | tf_op jit(solution)/shard_map/ppermute | solution.py:132
  55.8 14.2 %collective-permute-start.7 = (bf16[2,3,96,512]{3,2,1,0:T(8,128)(2,1)S(1)}, bf16[2,3,96,512]{3,2,1,0:T(8,128)(2,1)S(1)}, u32[]{:S(2)}, u32[]{:S(2)}) collective-permute-start(bf16[2,3,96,512]{3,2,1,0:T(8,128)(2,1)S(1)} %get-tuple-element.39.refs_0_), channel_id=1, source_target_pairs={{0,4},{2,6},{4,0},{6,2},{8,12},{10,14},{12,8},{14,10},{1,5},{3,7},... | collective-permute-start | bytes 1769480 | tf_op jit(solution)/shard_map/ppermute | solution.py:128
  70.1 14.5 %collective-permute-start.8 = (bf16[3,96,512]{2,1,0:T(8,128)(2,1)S(1)}, bf16[3,96,512]{2,1,0:T(8,128)(2,1)S(1)}, u32[]{:S(2)}, u32[]{:S(2)}) collective-permute-start(bf16[3,96,512]{2,1,0:T(8,128)(2,1)S(1)} %get-tuple-element.43.refs_0_), channel_id=1, source_target_pairs={{0,8},{2,10},{4,12},{6,14},{8,0},{10,2},{12,4},{14,6},{1,9},{3,11}... | collective-permute-start | bytes 884744 | tf_op jit(solution)/shard_map/ppermute | solution.py:128
  72.8 9.0 %collective-permute-start.6 = (bf16[2,1,96,512]{3,2,1,0:T(8,128)(2,1)S(1)}, bf16[2,1,96,512]{3,2,1,0:T(8,128)(2,1)S(1)}, u32[]{:S(2)}, u32[]{:S(2)}) collective-permute-start(bf16[2,1,96,512]{3,2,1,0:T(8,128)(2,1)S(1)} %get-tuple-element.40.refs_0_), channel_id=1, source_target_pairs={{0,4},{2,6},{4,0},{6,2},{8,12},{10,14},{12,8},{14,10},{1,5},{3,7},... | collective-permute-start | bytes 589832 | tf_op jit(solution)/shard_map/ppermute | solution.py:128
  74.2 20.9 %collective-permute-start.5 = (bf16[4,10,32,512]{3,2,1,0:T(8,128)(2,1)S(1)}, bf16[4,10,32,512]{3,2,1,0:T(8,128)(2,1)S(1)}, u32[]{:S(2)}, u32[]{:S(2)}) collective-permute-start(bf16[4,10,32,512]{3,2,1,0:T(8,128)(2,1)S(1)} %join.6.refs_0_), channel_id=1, source_target_pairs={{0,1},{1,0},{2,3},{3,2},{4,5},{5,4},{6,7},{7,6},{8,9},{9,8},{10,11... | collective-permute-start | bytes 3932168 | tf_op jit(solution)/shard_map/ppermute | solution.py:136
  84.6 8.4 %copy-start.1 = (bf16[4,10,32,512]{3,2,1,0:T(8,128)(2,1)}, bf16[4,10,32,512]{3,2,1,0:T(8,128)(2,1)S(1)}, u32[]{:S(2)}) copy-start(bf16[4,10,32,512]{3,2,1,0:T(8,128)(2,1)S(1)} %collective-permute-done.4.source.refs_1_) | copy-start | bytes 3932164
  84.7 12.0 %copy-start.5 = (s32[8,8]{1,0:T(8,128)S(1)}, s32[8,8]{1,0:T(8,128)}, u32[]{:S(2)}) copy-start(s32[8,8]{1,0:T(8,128)} %pattern.11) | copy-start | bytes 772
  84.7 10.4 %collective-permute-start.9 = (bf16[4,10,32,512]{3,2,1,0:T(8,128)(2,1)S(1)}, bf16[4,10,32,512]{3,2,1,0:T(8,128)(2,1)S(1)}, u32[]{:S(2)}, u32[]{:S(2)}) collective-permute-start(bf16[4,10,32,512]{3,2,1,0:T(8,128)(2,1)S(1)} %hold.2), channel_id=1, source_target_pairs={{0,1},{1,0},{2,3},{3,2},{4,5},{5,4},{6,7},{7,6},{8,9},{9,8},{10,11... | collective-permute-start | bytes 3932168 | tf_op jit(solution)/shard_map/ppermute | solution.py:136
  84.8 8.2 %collective-permute-start.10 = (bf16[1,96,512]{2,1,0:T(8,128)(2,1)S(1)}, bf16[1,96,512]{2,1,0:T(8,128)(2,1)S(1)}, u32[]{:S(2)}, u32[]{:S(2)}) collective-permute-start(bf16[1,96,512]{2,1,0:T(8,128)(2,1)S(1)} %get-tuple-element.44.refs_0_), channel_id=1, source_target_pairs={{0,8},{2,10},{4,12},{6,14},{8,0},{10,2},{12,4},{14,6},{1,9},{3,11}... | collective-permute-start | bytes 294920 | tf_op jit(solution)/shard_map/ppermute | solution.py:128
  93.2 15.8 %collective-permute-start.12 = (bf16[2,10,32,512]{3,2,1,0:T(8,128)(2,1)S(1)}, bf16[2,10,32,512]{3,2,1,0:T(8,128)(2,1)S(1)}, u32[]{:S(2)}, u32[]{:S(2)}) collective-permute-start(bf16[2,10,32,512]{3,2,1,0:T(8,128)(2,1)S(1)} %join.7.refs_8_.left), channel_id=1, source_target_pairs={{0,2},{2,0},{4,6},{6,4},{8,10},{10,8},{12,14},{14,12},{1,3},{3,1},... | collective-permute-start | bytes 1966088 | tf_op jit(solution)/shard_map/ppermute | solution.py:132
  94.4 18.1 %collective-permute-start.11 = (bf16[2,10,32,512]{3,2,1,0:T(8,128)(2,1)S(1)}, bf16[2,10,32,512]{3,2,1,0:T(8,128)(2,1)S(1)}, u32[]{:S(2)}, u32[]{:S(2)}) collective-permute-start(bf16[2,10,32,512]{3,2,1,0:T(8,128)(2,1)S(1)} %join.7.refs_8_.left), channel_id=1, source_target_pairs={{0,4},{2,6},{4,0},{6,2},{8,12},{10,14},{12,8},{14,10},{1,5},{3,7},... | collective-permute-start | bytes 1966088 | tf_op jit(solution)/shard_map/ppermute | solution.py:128
  102.6 15.9 %all-to-all-start = ((bf16[8,96,256]{2,1,0:T(8,128)(2,1)}), bf16[8,96,256]{2,1,0:T(8,128)(2,1)S(1)}, u32[]{:S(2)}, u32[]{:S(2)}) async-start(bf16[8,96,256]{2,1,0:T(8,128)(2,1)} %solve.3), calls=%async_computation | async-start | bytes 786432 | tf_op jit(solution)/shard_map/all_to_all | solution.py:519
  113.4 18.5 %collective-permute-start.13 = (bf16[2,10,32,512]{3,2,1,0:T(8,128)(2,1)}, bf16[2,10,32,512]{3,2,1,0:T(8,128)(2,1)S(1)}, u32[]{:S(2)}, u32[]{:S(2)}) collective-permute-start(bf16[2,10,32,512]{3,2,1,0:T(8,128)(2,1)} %hold.3), channel_id=1, source_target_pairs={{0,2},{2,0},{4,6},{6,4},{8,10},{10,8},{12,14},{14,12},{1,3},{3,1},... | collective-permute-start | bytes 1966088 | tf_op jit(solution)/shard_map/ppermute | solution.py:132
  123.5 25.3 %collective-permute-start.20 = (bf16[2,384,512]{2,1,0:T(8,128)(2,1)S(1)}, bf16[2,384,512]{2,1,0:T(8,128)(2,1)S(1)}, u32[]{:S(2)}, u32[]{:S(2)}) collective-permute-start(bf16[2,384,512]{2,1,0:T(8,128)(2,1)S(1)} %get-tuple-element.56), channel_id=1, source_target_pairs={{0,2},{2,0},{4,6},{6,4},{8,10},{10,8},{12,14},{14,12},{1,3},{3,1},... | collective-permute-start | bytes 2359304 | tf_op jit(solution)/shard_map/ppermute | solution.py:132
  135.2 38.0 %collective-permute-start.15 = (bf16[4,10,32,512]{3,2,1,0:T(8,128)(2,1)S(1)}, bf16[4,10,32,512]{3,2,1,0:T(8,128)(2,1)}, u32[]{:S(2)}, u32[]{:S(2)}) collective-permute-start(bf16[4,10,32,512]{3,2,1,0:T(8,128)(2,1)S(1)} %join.9.refs_1_), channel_id=1, source_target_pairs={{0,1},{1,0},{2,3},{3,2},{4,5},{5,4},{6,7},{7,6},{8,9},{9,8},{10,11... | collective-permute-start | bytes 3932168 | tf_op jit(solution)/shard_map/ppermute | solution.py:136
  135.7 13.0 %copy-start.4 = (f32[2,384,512]{2,1,0:T(8,128)S(1)}, f32[2,384,512]{2,1,0:T(8,128)}, u32[]{:S(2)}) copy-start(f32[2,384,512]{2,1,0:T(8,128)} %copy-done.3) | copy-start | bytes 4718596
  135.7 37.5 %collective-permute-start.14 = (bf16[4,10,32,512]{3,2,1,0:T(8,128)(2,1)S(1)}, bf16[4,10,32,512]{3,2,1,0:T(8,128)(2,1)}, u32[]{:S(2)}, u32[]{:S(2)}) collective-permute-start(bf16[4,10,32,512]{3,2,1,0:T(8,128)(2,1)S(1)} %join.8.refs_0_), channel_id=1, source_target_pairs={{0,1},{1,0},{2,3},{3,2},{4,5},{5,4},{6,7},{7,6},{8,9},{9,8},{10,11... | collective-permute-start | bytes 3932168 | tf_op jit(solution)/shard_map/ppermute | solution.py:136
  139.1 18.0 %collective-permute-start.16 = (bf16[1,384,512]{2,1,0:T(8,128)(2,1)S(1)}, bf16[1,384,512]{2,1,0:T(8,128)(2,1)S(1)}, u32[]{:S(2)}, u32[]{:S(2)}) collective-permute-start(bf16[1,384,512]{2,1,0:T(8,128)(2,1)S(1)} %get-tuple-element.50), channel_id=1, source_target_pairs={{0,2},{2,0},{4,6},{6,4},{8,10},{10,8},{12,14},{14,12},{1,3},{3,1},... | collective-permute-start | bytes 1179656 | tf_op jit(solution)/shard_map/ppermute | solution.py:132
  149.4 11.7 %collective-permute-start.21 = (bf16[2,2,96,512]{3,2,1,0:T(8,128)(2,1)S(1)}, bf16[2,2,96,512]{3,2,1,0:T(8,128)(2,1)S(1)}, u32[]{:S(2)}, u32[]{:S(2)}) collective-permute-start(bf16[2,2,96,512]{3,2,1,0:T(8,128)(2,1)S(1)} %get-tuple-element.58), channel_id=1, source_target_pairs={{0,4},{2,6},{4,0},{6,2},{8,12},{10,14},{12,8},{14,10},{1,5},{3,7},... | collective-permute-start | bytes 1179656 | tf_op jit(solution)/shard_map/ppermute | solution.py:128
  149.7 12.7 %collective-permute-start.19 = (bf16[1,384,512]{2,1,0:T(8,128)(2,1)S(1)}, bf16[1,384,512]{2,1,0:T(8,128)(2,1)S(1)}, u32[]{:S(2)}, u32[]{:S(2)}) collective-permute-start(bf16[1,384,512]{2,1,0:T(8,128)(2,1)S(1)} %get-tuple-element.55), channel_id=1, source_target_pairs={{0,2},{2,0},{4,6},{6,4},{8,10},{10,8},{12,14},{14,12},{1,3},{3,1},... | collective-permute-start | bytes 1179656 | tf_op jit(solution)/shard_map/ppermute | solution.py:132
  157.8 6.9 %collective-permute-start.17 = (bf16[2,1,96,512]{3,2,1,0:T(8,128)(2,1)S(1)}, bf16[2,1,96,512]{3,2,1,0:T(8,128)(2,1)S(1)}, u32[]{:S(2)}, u32[]{:S(2)}) collective-permute-start(bf16[2,1,96,512]{3,2,1,0:T(8,128)(2,1)S(1)} %get-tuple-element.52), channel_id=1, source_target_pairs={{0,4},{2,6},{4,0},{6,2},{8,12},{10,14},{12,8},{14,10},{1,5},{3,7},... | collective-permute-start | bytes 589832 | tf_op jit(solution)/shard_map/ppermute | solution.py:128
  161.2 9.9 %collective-permute-start.23 = (bf16[2,96,512]{2,1,0:T(8,128)(2,1)S(1)}, bf16[2,96,512]{2,1,0:T(8,128)(2,1)S(1)}, u32[]{:S(2)}, u32[]{:S(2)}) collective-permute-start(bf16[2,96,512]{2,1,0:T(8,128)(2,1)S(1)} %get-tuple-element.59.refs_0_), channel_id=1, source_target_pairs={{0,8},{2,10},{4,12},{6,14},{8,0},{10,2},{12,4},{14,6},{1,9},{3,11}... | collective-permute-start | bytes 589832 | tf_op jit(solution)/shard_map/ppermute | solution.py:128
  163.0 9.9 %collective-permute-start.22 = (bf16[2,1,96,512]{3,2,1,0:T(8,128)(2,1)S(1)}, bf16[2,1,96,512]{3,2,1,0:T(8,128)(2,1)S(1)}, u32[]{:S(2)}, u32[]{:S(2)}) collective-permute-start(bf16[2,1,96,512]{3,2,1,0:T(8,128)(2,1)S(1)} %get-tuple-element.61), channel_id=1, source_target_pairs={{0,4},{2,6},{4,0},{6,2},{8,12},{10,14},{12,8},{14,10},{1,5},{3,7},... | collective-permute-start | bytes 589832 | tf_op jit(solution)/shard_map/ppermute | solution.py:128
  164.7 12.1 %collective-permute-start.18 = (bf16[1,96,512]{2,1,0:T(8,128)(2,1)S(1)}, bf16[1,96,512]{2,1,0:T(8,128)(2,1)S(1)}, u32[]{:S(2)}, u32[]{:S(2)}) collective-permute-start(bf16[1,96,512]{2,1,0:T(8,128)(2,1)S(1)} %get-tuple-element.54), channel_id=1, source_target_pairs={{0,8},{2,10},{4,12},{6,14},{8,0},{10,2},{12,4},{14,6},{1,9},{3,11}... | collective-permute-start | bytes 294920 | tf_op jit(solution)/shard_map/ppermute | solution.py:128
  172.9 5.7 %collective-permute-start.24 = (bf16[1,96,512]{2,1,0:T(8,128)(2,1)S(1)}, bf16[1,96,512]{2,1,0:T(8,128)(2,1)S(1)}, u32[]{:S(2)}, u32[]{:S(2)}) collective-permute-start(bf16[1,96,512]{2,1,0:T(8,128)(2,1)S(1)} %get-tuple-element.63), channel_id=1, source_target_pairs={{0,8},{2,10},{4,12},{6,14},{8,0},{10,2},{12,4},{14,6},{1,9},{3,11}... | collective-permute-start | bytes 294920 | tf_op jit(solution)/shard_map/ppermute | solution.py:128
  (4 other events, 9.8 us)
